TPU v7x, 32 devices: a whole 2x2x4 slice. The times are simulated.
32 devices in a mesh: dp: 16 (over z, y, x), tensor: 2 (over core).
Axes of the slice: x: 2, y: 2, z: 4, core: 2. Of those that a mesh axis runs over, the one named last changes fastest.
Arguments:
- residual: bfloat16 [16384, 1024], P(('dp', 'tensor')), may hold values from -6 to 6
- norm1_gain: float32 [1024], replicated, may hold values from 0.5 to 1.5
- norm1_bias: float32 [1024], replicated, may hold values from -3 to 3
- norm2_gain: float32 [1024], replicated, may hold values from 0.5 to 1.5
- norm2_bias: float32 [1024], replicated, may hold values from -3 to 3
- qkv_weight: bfloat16 [1024, 3, 1024], P(None, None, 'tensor'), may hold values from -2 to 2, as said below
- qkv_bias: float32 [3, 1024], P(None, 'tensor'), may hold values from -3 to 3
- dense_weight: bfloat16 [1024, 1024], P('tensor'), may hold values from -0.75 to 0.75
- inner_weight: bfloat16 [1024, 4096], P(None, 'tensor'), may hold values from -0.1875 to 0.1875
- inner_bias: float32 [4096], P('tensor'), may hold values from -3 to 3
- outer_weight: bfloat16 [4096, 1024], P('tensor'), may hold values from -0.09375 to 0.09375
- out_bias: float32 [1024], replicated, may hold values from -3 to 3
- cotangent: bfloat16 [16384, 1024], P(('dp', 'tensor')), may hold values from -6 to 6
- seq_lengths: int32 [16, 4], P('dp'), may hold values from 0 to 512, as said below
Outputs:
- layer_out: bfloat16 [16384, 1024], P(('dp', 'tensor'))
- residual_grad: bfloat16 [16384, 1024], P(('dp', 'tensor'))
- gain1_grad: float32 [1024], replicated
- bias1_grad: float32 [1024], replicated
- gain2_grad: float32 [1024], replicated
- bias2_grad: float32 [1024], replicated
- qkv_grad: float32 [1024, 3, 1024], P(None, None, 'tensor')
- qkvbias_grad: float32 [3, 1024], P(None, 'tensor')
- dense_grad: float32 [1024, 1024], P('tensor')
- inner_grad: float32 [1024, 4096], P(None, 'tensor')
- innerbias_grad: float32 [4096], P('tensor')
- outer_grad: float32 [4096, 1024], P('tensor')
- outbias_grad: float32 [1024], replicated
Inputs may be any that keep to these rules, and one draw needn't show every extreme that they name: `seq_lengths`: row r lists the lengths of the sequences packed into index r of dp in order, zero for an unused slot; each row sums to at most 1024. In every draw some row holds two sequences of 512 rows and is full. `qkv_weight`: entries are independent.
All inputs are finite; a program needn't handle non-finite values.
Results may differ from a plain program's by a relative error of at most 0.0085.
Values may be sent and summed in bfloat16 or wider, within the bound.
No kernel may reach another device: no remote copies, remote signals or barrier semaphores. Data moves between devices by JAX's collectives and lax.ppermute only.
A program may use at most 256 MiB of HBM per device.

v0:
```python
import math

import jax
import jax.numpy as jnp
from jax import lax
from jax.sharding import PartitionSpec as P

HD = 64
ROT = 16


EPSILON = 1e-05
MASKED_SCORE = -1e30
SQRT_HALF = 0.7071067811865476
INV_ROOT_TWO_PI = 0.3989422804014327


def normalize(values):
    mean_val = jnp.mean(values, axis=-1, keepdims=True)
    centred = values - mean_val
    inv_std = lax.rsqrt(jnp.mean(centred * centred, axis=-1, keepdims=True) + EPSILON)
    return (centred * inv_std, inv_std)


def norm_back(upstream, normed, inv_std, gain):
    scaled = upstream * gain
    return inv_std * (
        scaled
        - jnp.mean(scaled, axis=-1, keepdims=True)
        - normed * jnp.mean(scaled * normed, axis=-1, keepdims=True)
    )


def gelu_slope(preact):
    return (
        0.5 * (1.0 + lax.erf(preact * SQRT_HALF))
        + preact * jnp.exp(-0.5 * preact * preact) * INV_ROOT_TWO_PI
    )


def layout(lengths, row_count):
    slot_count = lengths.shape[0]
    places = jnp.arange(row_count, dtype=jnp.int32)
    seq_ends = jnp.cumsum(lengths)
    seq_starts = seq_ends - lengths
    segment = jnp.sum((places[:, None] >= seq_ends[None, :]).astype(jnp.int32), axis=1)
    member = segment[:, None] == jnp.arange(slot_count, dtype=jnp.int32)[None, :]
    position = places - jnp.sum(jnp.where(member, seq_starts[None, :], 0), axis=1)
    return (segment, position)


def angles(position):
    half_rot = ROT // 2
    frequency = jnp.exp(-(2.0 * jnp.arange(half_rot, dtype=jnp.float32) / ROT) * math.log(10000.0))
    angle_table = position.astype(jnp.float32)[:, None] * frequency[None, :]
    return (jnp.cos(angle_table), jnp.sin(angle_table))


def rotate(values, cosine, sine_table):
    half_rot = ROT // 2
    lower = values[..., :half_rot]
    upper = values[..., half_rot:ROT]
    cos_grid = cosine[:, None, :]
    sin_grid = sine_table[:, None, :]
    return jnp.concatenate(
        [
            lower * cos_grid - upper * sin_grid,
            upper * cos_grid + lower * sin_grid,
            values[..., ROT:],
        ],
        axis=-1,
    )


def unrotate(values, cosine, sine_table):
    half_rot = ROT // 2
    lower = values[..., :half_rot]
    upper = values[..., half_rot:ROT]
    cos_grid = cosine[:, None, :]
    sin_grid = sine_table[:, None, :]
    return jnp.concatenate(
        [
            lower * cos_grid + upper * sin_grid,
            upper * cos_grid - lower * sin_grid,
            values[..., ROT:],
        ],
        axis=-1,
    )


def local(
    residual,
    norm1_gain,
    norm1_bias,
    norm2_gain,
    norm2_bias,
    qkv_weight,
    qkv_bias,
    dense_weight,
    inner_weight,
    inner_bias,
    outer_weight,
    out_bias,
    cotangent,
    seq_lengths,
):
    local_rows = residual.shape[0]
    feature_width = residual.shape[1]
    head_width = qkv_weight.shape[2]
    head_count = head_width // HD
    score_scale = HD ** (-0.5)
    gathered = lax.all_gather(residual, "tensor", axis=0, tiled=True)
    total_rows = gathered.shape[0]
    slot_count = seq_lengths.shape[1]
    segment, position = layout(seq_lengths[0], total_rows)
    cosine, sine_table = angles(position)
    normed, inv_std = normalize(gathered.astype(jnp.float32))
    first_in = (normed * norm1_gain + norm1_bias).astype(jnp.bfloat16)
    second_in = (normed * norm2_gain + norm2_bias).astype(jnp.bfloat16)
    qkv_flat = qkv_weight.reshape(feature_width, 3 * head_width)
    projected = (
        jnp.dot(first_in, qkv_flat, preferred_element_type=jnp.float32) + qkv_bias.reshape(-1)
    ).reshape(total_rows, 3, head_count, HD)
    queries = rotate(projected[:, 0], cosine, sine_table).astype(jnp.bfloat16)
    keys_bf = rotate(projected[:, 1], cosine, sine_table).astype(jnp.bfloat16)
    values_bf = projected[:, 2].astype(jnp.bfloat16)
    block_rows = min(512, total_rows)
    block_count = total_rows // block_rows
    columns = jnp.arange(total_rows, dtype=jnp.int32)

    def block_scores(block_start):
        rows_here = columns[block_start : block_start + block_rows]
        seg_here = segment[block_start : block_start + block_rows]
        allowed = (seg_here[:, None] == segment[None, :]) & (
            columns[None, :] <= rows_here[:, None]
        ) & (seg_here[:, None] < slot_count) | (columns[None, :] == rows_here[:, None])
        raw_scores = (
            jnp.einsum(
                "qhd,khd->hqk",
                queries[block_start : block_start + block_rows],
                keys_bf,
                preferred_element_type=jnp.float32,
            )
            * score_scale
        )
        return jnp.where(allowed[None], raw_scores, MASKED_SCORE)

    contexts = []
    logsums = []
    for block_index in range(block_count):
        block_start = block_index * block_rows
        scores = block_scores(block_start)
        highest = jnp.max(scores, axis=-1, keepdims=True)
        exponent = jnp.exp(scores - highest)
        row_total = jnp.sum(exponent, axis=-1, keepdims=True)
        probs_bf = (exponent / row_total).astype(jnp.bfloat16)
        logsums.append(highest + jnp.log(row_total))
        contexts.append(
            jnp.einsum(
                "hqk,khd->qhd", probs_bf, values_bf, preferred_element_type=jnp.float32
            ).astype(jnp.bfloat16)
        )
    context = jnp.concatenate(contexts, axis=0).reshape(total_rows, head_width)
    logsum = jnp.concatenate(logsums, axis=1)
    preact = jnp.dot(second_in, inner_weight, preferred_element_type=jnp.float32) + inner_bias
    active = jax.nn.gelu(preact, approximate=False).astype(jnp.bfloat16)
    summed = lax.psum_scatter(
        (
            jnp.dot(context, dense_weight, preferred_element_type=jnp.float32)
            + jnp.dot(active, outer_weight, preferred_element_type=jnp.float32)
        ).astype(jnp.bfloat16),
        "tensor",
        scatter_dimension=0,
        tiled=True,
    ).astype(jnp.float32)
    layer_out = (residual.astype(jnp.float32) + summed + out_bias).astype(jnp.bfloat16)
    cotangent_all = lax.all_gather(cotangent, "tensor", axis=0, tiled=True)
    outbias_local = jnp.sum(cotangent.astype(jnp.float32), axis=0)
    outer_grad = jnp.einsum("tf,td->fd", active, cotangent_all, preferred_element_type=jnp.float32)
    active_back = jnp.einsum(
        "td,fd->tf", cotangent_all, outer_weight, preferred_element_type=jnp.float32
    )
    pre_grad = active_back * gelu_slope(preact)
    innerbias_grad = jnp.sum(pre_grad, axis=0)
    pre_back = pre_grad.astype(jnp.bfloat16)
    inner_grad = jnp.einsum("td,tf->df", second_in, pre_back, preferred_element_type=jnp.float32)
    second_grad = jnp.einsum(
        "tf,df->td", pre_back, inner_weight, preferred_element_type=jnp.float32
    )
    dense_grad = jnp.einsum("tc,td->cd", context, cotangent_all, preferred_element_type=jnp.float32)
    context_back = (
        jnp.einsum("td,cd->tc", cotangent_all, dense_weight, preferred_element_type=jnp.float32)
        .astype(jnp.bfloat16)
        .reshape(total_rows, head_count, HD)
    )
    value_grad = jnp.zeros((total_rows, head_count, HD), jnp.float32)
    key_grad = jnp.zeros((total_rows, head_count, HD), jnp.float32)
    query_parts = []
    for block_index in range(block_count):
        block_start = block_index * block_rows
        scores = block_scores(block_start)
        weights_full = jnp.exp(scores - logsum[:, block_start : block_start + block_rows])
        weights_bf = weights_full.astype(jnp.bfloat16)
        back_block = context_back[block_start : block_start + block_rows]
        value_grad = value_grad + jnp.einsum(
            "hqk,qhd->khd", weights_bf, back_block, preferred_element_type=jnp.float32
        )
        prob_grad = jnp.einsum(
            "qhd,khd->hqk", back_block, values_bf, preferred_element_type=jnp.float32
        )
        row_delta = jnp.sum(weights_full * prob_grad, axis=-1, keepdims=True)
        score_back = (weights_full * (prob_grad - row_delta) * score_scale).astype(jnp.bfloat16)
        query_parts.append(
            jnp.einsum("hqk,khd->qhd", score_back, keys_bf, preferred_element_type=jnp.float32)
        )
        key_grad = key_grad + jnp.einsum(
            "hqk,qhd->khd",
            score_back,
            queries[block_start : block_start + block_rows],
            preferred_element_type=jnp.float32,
        )
    query_grad = jnp.concatenate(query_parts, axis=0)
    qkv_back = jnp.stack(
        [
            unrotate(query_grad, cosine, sine_table),
            unrotate(key_grad, cosine, sine_table),
            value_grad,
        ],
        axis=1,
    )
    qkvbias_grad = jnp.sum(qkv_back, axis=0).reshape(3, head_width)
    qkv_backb = qkv_back.reshape(total_rows, 3 * head_width).astype(jnp.bfloat16)
    qkv_grad = jnp.einsum(
        "td,tc->dc", first_in, qkv_backb, preferred_element_type=jnp.float32
    ).reshape(feature_width, 3, head_width)
    first_grad = jnp.einsum("tc,dc->td", qkv_backb, qkv_flat, preferred_element_type=jnp.float32)
    first_rows, second_rows = (
        lax.psum_scatter(first_grad, "tensor", scatter_dimension=0, tiled=True),
        lax.psum_scatter(second_grad, "tensor", scatter_dimension=0, tiled=True),
    )
    row_offset = lax.axis_index("tensor") * local_rows
    normed_rows = lax.dynamic_slice_in_dim(normed, row_offset, local_rows, 0)
    inv_rows = lax.dynamic_slice_in_dim(inv_std, row_offset, local_rows, 0)
    gain1_local = jnp.sum(first_rows * normed_rows, axis=0)
    bias1_local = jnp.sum(first_rows, axis=0)
    gain2_local = jnp.sum(second_rows * normed_rows, axis=0)
    bias2_local = jnp.sum(second_rows, axis=0)
    summed_back = norm_back(first_rows, normed_rows, inv_rows, norm1_gain) + norm_back(
        second_rows, normed_rows, inv_rows, norm2_gain
    )
    residual_grad = (cotangent.astype(jnp.float32) + summed_back).astype(jnp.bfloat16)
    gain1_grad, bias1_grad, gain2_grad, bias2_grad, outbias_grad = lax.psum(
        (gain1_local, bias1_local, gain2_local, bias2_local, outbias_local), ("dp", "tensor")
    )
    qkv_grad, qkvbias_grad, dense_grad, inner_grad, innerbias_grad, outer_grad = lax.psum(
        (qkv_grad, qkvbias_grad, dense_grad, inner_grad, innerbias_grad, outer_grad), "dp"
    )
    return (
        layer_out,
        residual_grad,
        gain1_grad,
        bias1_grad,
        gain2_grad,
        bias2_grad,
        qkv_grad,
        qkvbias_grad,
        dense_grad,
        inner_grad,
        innerbias_grad,
        outer_grad,
        outbias_grad,
    )


def solution(mesh):
    return jax.shard_map(
        local,
        mesh=mesh,
        in_specs=(
            P(("dp", "tensor"), None),
            P(),
            P(),
            P(),
            P(),
            P(None, None, "tensor"),
            P(None, "tensor"),
            P("tensor", None),
            P(None, "tensor"),
            P("tensor"),
            P("tensor", None),
            P(),
            P(("dp", "tensor"), None),
            P("dp", None),
        ),
        out_specs=(
            P(("dp", "tensor"), None),
            P(("dp", "tensor"), None),
            P(),
            P(),
            P(),
            P(),
            P(None, None, "tensor"),
            P(None, "tensor"),
            P("tensor", None),
            P(None, "tensor"),
            P("tensor"),
            P("tensor", None),
            P(),
        ),
        check_vma=False,
    )
```

profile of v0, /device:TPU:0, one launch (start us, length us, event | category | flops | bytes accessed | tf_op | source)
XLA Modules:
  0.0 1029.7 jit_solution(12968699456829167058)
XLA Ops:
  7.2 0.7 all-gather.3.cloned.1.call-update
  8.0 0.7 all-gather.5.cloned.1.call-update
  8.8 0.8 reduce-window.4
  9.6 0.7 fusion.99
  10.4 4.7 copy.34
  15.2 0.2 multiply_cosine_fusion
  15.4 1.7 fusion.75
  17.1 5.8 all-gather.3.cloned.1.call-done
  22.9 1.9 convert_reduce_fusion
  24.9 2.3 fusion.63
  27.2 8.8 convolution_add_fusion
  36.0 6.6 copy.35
  42.5 2.5 slice_bitcast_fusion
  45.6 3.1 fusion.115
  48.7 3.8 fusion.8
  52.5 1.9 copy-done.2
  54.4 5.9 fusion.91
  60.4 3.1 fusion.114
  63.5 3.8 fusion.9
  67.3 1.9 copy-done.3
  69.2 5.7 fusion.92
  74.9 2.9 convolution_convert_fusion
  77.9 10.1 fusion.119
  88.1 9.8 fusion.117
  98.1 25.1 %fusion.26 = (bf16[1024,2048]{1,0:T(8,128)(2,1)S(1)}, f32[1024,2048]{1,0:T(8,128)}) fusion(f32[2048]{0:T(1024)S(1)} %copy-done.40, bf16[1024,2048]{1,0:T(8,128)(2,1)S(1)} %copy-done.37, f32[1024]{0:T(1024)S(1)} %copy-done.43, f32[1024]{0:T(1024)S(1)} %copy-done.31, f32[1024]{0:T(1024)S(1)} %add_rsqrt_fusion, f32[1024]{0:T(1024)S(1)} %broadcast_multiply_fusion, ...), kind=kOutput, calls=%fused_computation.28 | convolution fusion | flops 4439670784 | bytes 18898944 | tf_op jit(solution)/shard_map/dot_general | solution.py:165
  123.2 4.5 fusion.123
  127.7 2.7 add_convert_fusion
  130.5 31.1 %fusion.13 = f32[8,64,1024]{2,1,0:T(8,128)} fusion(f32[8,512,1024]{2,1,0:T(8,128)} %fusion.119, f32[8,512,1024]{2,1,0:T(8,128)} %copy-done.2, f32[8,512]{1,0:T(8,128)S(1)} %log_add_fusion.1, bf16[1024,8,64]{0,2,1:T(8,128)(2,1)} %copy-done.21), kind=kOutput, calls=%fused_computation.22 | convolution fusion | flops 566236160 | bytes 69763072 | tf_op jit(solution)/shard_map/hqk,qhd->khd/dot_general | solution.py:216
  161.6 31.0 %add_bitcast_fusion.1 = f32[1024,8,64]{0,2,1:T(8,128)} fusion(f32[8,64,1024]{2,1,0:T(8,128)} %fusion.13, f32[8,512,1024]{2,1,0:T(8,128)} %fusion.117, f32[8,512,1024]{2,1,0:T(8,128)} %copy-done.3, f32[8,512]{1,0:T(8,128)S(1)} %log_add_fusion, bf16[1024,8,64]{0,2,1:T(8,128)(2,1)S(1)} %copy-done.22), kind=kOutput, calls=%fused_computation.97 | convolution fusion | flops 566760448 | bytes 71860224 | tf_op jit(solution)/shard_map/hqk,qhd->khd/dot_general | solution.py:216
  192.6 2.8 slice.130
  195.4 30.0 %fusion.86 = f32[512,8,64]{0,2,1:T(8,128)} fusion(f32[8,512,1024]{2,1,0:T(8,128)} %fusion.119, f32[8,512,1024]{2,1,0:T(8,128)} %copy-done.2, f32[8,512]{1,0:T(8,128)S(1)} %log_add_fusion.1, bf16[1024,8,48]{0,2,1:T(8,128)(2,1)} %copy-done.23, bf16[1024,8,8]{0,2,1:T(8,128)(2,1)S(1)} %get-tuple-element.42, bf16[1024,8,8]{0,2,1:T(8,128)(2,1)S(1)} %get-tuple-element.41), kind=kOutput, calls=%fused_computation.115 | convolution fusion | flops 569381888 | bytes 35667968 | tf_op jit(solution)/shard_map/hqk,khd->qhd/dot_general | solution.py:214
  225.4 37.2 %fusion.83 = f32[512,8,64]{0,2,1:T(8,128)} fusion(f32[8,512,1024]{2,1,0:T(8,128)} %fusion.117, f32[8,512,1024]{2,1,0:T(8,128)} %copy-done.3, f32[8,512]{1,0:T(8,128)S(1)} %log_add_fusion, bf16[1024,8,48]{0,2,1:T(8,128)(2,1)S(1)} %copy-done.24, bf16[1024,8,8]{0,2,1:T(8,128)(2,1)S(1)} %get-tuple-element.42, bf16[1024,8,8]{0,2,1:T(8,128)(2,1)S(1)} %get-tuple-element.41), kind=kOutput, calls=%fused_computation.114 | convolution fusion | flops 569381888 | bytes 35667968 | tf_op jit(solution)/shard_map/hqk,khd->qhd/dot_general | solution.py:214
  262.7 1.2 multiply_add_fusion.1
  263.9 1.1 multiply_add_fusion
  265.0 2.6 fusion.66
  267.6 8.9 fusion.32
  276.6 7.3 add_bitcast_fusion
  283.9 0.7 fusion.62
  284.6 0.6 copy-done.7
  285.2 1.7 copy-done.18
  286.8 0.6 copy-done.17
  287.5 5.1 fusion.124
  292.6 10.9 %fusion.116 = (f32[2048]{0:T(1024)S(1)}, bf16[1024,2048]{1,0:T(8,128)(2,1)S(1)}) fusion(f32[1024,2048]{1,0:T(8,128)} %get-tuple-element.61, f32[2048]{0:T(1024)S(1)} %copy-done.40, bf16[1024,1024]{1,0:T(8,128)(2,1)} %all-gather.5.cloned.1.call-done, bf16[2048,1024]{1,0:T(8,128)(2,1)} %param.24), kind=kOutput, calls=%fused_computation.171 | convolution fusion | flops 4320131072 | bytes 18890752 | tf_op jit(solution)/shard_map/td,fd->tf/dot_general | solution.py:180
  303.5 2.0 copy-done.44
  305.5 6.2 fusion.71
  311.8 4.3 fusion.125
  316.2 6.7 fusion.67
  322.9 6.9 fusion.126
  329.8 7.1 fusion.69
  337.0 3.2 fusion.61
  340.4 81.2 %all-reduce.1 = (f32[3,512]{1,0:T(4,128)}, f32[2048]{0:T(1024)}) all-reduce(f32[3,512]{1,0:T(4,128)S(1)} %reshape.352, f32[2048]{0:T(1024)S(1)} %get-tuple-element.66), channel_id=1, replica_groups=mesh['dp'=16,'tensor'=2] {'dp'}, use_global_device_ids=true, to_apply=%region_28.29 | all-reduce | flops 3584 | bytes 28672 | tf_op jit(solution)/shard_map/psum | solution.py:255
  421.6 2.5 fusion.59
  424.1 3.2 add_convert_fusion.3
  427.3 4.7 multiply_reduce_fusion.2
  432.1 0.3 copy-done.8
  432.4 3.2 convert_reduce_fusion.1
  435.6 41.8 %all-reduce = (f32[1024]{0:T(1024)}, f32[1024]{0:T(1024)}, f32[1024]{0:T(1024)}, f32[1024]{0:T(1024)}, f32[1024]{0:T(1024)}) all-reduce(f32[1024]{0:T(1024)S(1)} %get-tuple-element.18, f32[1024]{0:T(1024)S(1)} %get-tuple-element.21, f32[1024]{0:T(1024)S(1)} %get-tuple-element.13, ...), channel_id=1, replica_groups=mesh['dp'=16,'tensor'=2] {'dp','tensor'}, use_global_device_ids=true, to_apply=%region_19.20 | all-reduce | flops 5120 | bytes 40960 | tf_op jit(solution)/shard_map/psum | solution.py:252
  477.4 527.2 %all-reduce.5.cloned.1.call-done = (f32[1024,3,512]{2,0,1:T(8,128)}, f32[512,1024]{1,0:T(8,128)}, f32[1024,2048]{1,0:T(8,128)}, f32[2048,1024]{1,0:T(8,128)}) async-done(((f32[1024,3,512]{2,0,1:T(8,128)}, f32[512,1024]{1,0:T(8,128)}, f32[1024,2048]{1,0:T(8,128)}, f32[2048,1024]{1,0:T(8,128)}), (f32[1024,3,512]{2,0,1:T(8,128)}, f32[512,1024]{1,0:T(8,128)}, f32[1024,2048]{1,0:T(8,128)}, ...) | async-done | bytes 25165840 | tf_op jit(solution)/shard_map/psum | solution.py:255
  1004.6 6.9 copy.43
  1011.4 1.3 copy.44
  1012.8 0.6 slice-done.3
  1013.4 4.3 copy.45
  1017.6 1.4 slice-done.1
  1019.0 3.4 copy.46
  (138 shorter events, 1.6 us)
Async XLA Ops:
  7.2 67.8 %copy-start = (bf16[512,1024]{1,0:T(8,128)(2,1)S(1)}, bf16[512,1024]{1,0:T(8,128)(2,1)}, u32[]{:S(2)}) copy-start(bf16[512,1024]{1,0:T(8,128)(2,1)} %param.21) | copy-start | bytes 3145732
  7.2 7.9 copy-start.34
  7.2 15.7 %all-gather.3.cloned.1.call-start = ((), (), s32[]{:S(2)}) async-start(), calls=%async_computation.3 | async-start | bytes 3145728 | tf_op jit(solution)/shard_map/all_gather | solution.py:112
  7.9 19.2 %copy-start.32 = (f32[1024]{0:T(1024)S(1)}, f32[1024]{0:T(1024)}, u32[]{:S(2)}) copy-start(f32[1024]{0:T(1024)} %param.15) | copy-start | bytes 12292
  8.0 19.2 %copy-start.41 = (f32[1024]{0:T(1024)S(1)}, f32[1024]{0:T(1024)}, u32[]{:S(2)}) copy-start(f32[1024]{0:T(1024)} %param.16) | copy-start | bytes 12292
  8.0 67.0 %all-gather.5.cloned.1.call-start = ((), (), s32[]{:S(2)}) async-start(), calls=%async_computation.5 | async-start | bytes 3145728 | tf_op jit(solution)/shard_map/all_gather | solution.py:177
  8.7 415.4 %reduce-scatter.4.cloned.1.call-start = ((), (), s32[]{:S(2)}) async-start(), calls=%async_computation.4 | async-start | bytes 3145728 | tf_op jit(solution)/shard_map/reduce_scatter | solution.py:167
  15.4 29.9 %copy-start.25 = (f32[1024,8]{0,1:T(8,128)}, f32[1024,8]{0,1:T(8,128)S(1)}, u32[]{:S(2)}) copy-start(f32[1024,8]{0,1:T(8,128)S(1)} %get-tuple-element.52) | copy-start | bytes 98308
  15.4 29.9 %copy-start.27 = (f32[1024,8]{0,1:T(8,128)}, f32[1024,8]{0,1:T(8,128)S(1)}, u32[]{:S(2)}) copy-start(f32[1024,8]{0,1:T(8,128)S(1)} %get-tuple-element.53) | copy-start | bytes 98308
  45.3 15.1 %copy-start.23 = (bf16[1024,8,48]{0,2,1:T(8,128)(2,1)}, bf16[1024,8,48]{0,2,1:T(8,128)(2,1)S(1)}, u32[]{:S(2)}) copy-start(bf16[1024,8,48]{0,2,1:T(8,128)(2,1)S(1)} %slice.160) | copy-start | bytes 2359300
  45.6 14.8 %copy-start.21 = (bf16[1024,8,64]{0,2,1:T(8,128)(2,1)}, bf16[1024,8,64]{0,2,1:T(8,128)(2,1)S(1)}, u32[]{:S(2)}) copy-start(bf16[1024,8,64]{0,2,1:T(8,128)(2,1)S(1)} %pad_maximum_fusion.1) | copy-start | bytes 3145732
  48.7 5.7 copy-start.2
  63.5 5.7 copy-start.3
  77.9 10.1 copy-start.10
  77.9 10.1 copy-start.12
  88.0 9.9 copy-start.29
  88.0 9.9 copy-start.30
  88.0 10.0 copy-start.4
  88.0 10.0 copy-start.31
  88.0 10.0 copy-start.37
  88.0 10.0 copy-start.40
  88.0 10.0 copy-start.43
  98.1 29.6 %copy-start.15 = (bf16[1024,8,64]{0,2,1:T(8,128)(2,1)}, bf16[1024,8,64]{0,2,1:T(8,128)(2,1)S(1)}, u32[]{:S(2)}) copy-start(bf16[1024,8,64]{0,2,1:T(8,128)(2,1)S(1)} %pad_maximum_fusion.3) | copy-start | bytes 3145732
  98.1 25.1 %copy-start.36 = (bf16[2048,1024]{1,0:T(8,128)(2,1)S(1)}, bf16[2048,1024]{1,0:T(8,128)(2,1)}, u32[]{:S(2)}) copy-start(bf16[2048,1024]{1,0:T(8,128)(2,1)} %param.24) | copy-start | bytes 12582916
  123.2 4.5 copy-start.46
  130.4 31.2 %copy-start.22 = (bf16[1024,8,64]{0,2,1:T(8,128)(2,1)S(1)}, bf16[1024,8,64]{0,2,1:T(8,128)(2,1)}, u32[]{:S(2)}) copy-start(bf16[1024,8,64]{0,2,1:T(8,128)(2,1)} %copy-done.21) | copy-start | bytes 3145732
  130.5 296.9 %reduce-scatter.6.cloned.1.call-start = ((), (), s32[]{:S(2)}) async-start(), calls=%async_computation.6 | async-start | bytes 6291456 | tf_op jit(solution)/shard_map/reduce_scatter | solution.py:238
  195.4 30.0 %copy-start.24 = (bf16[1024,8,48]{0,2,1:T(8,128)(2,1)S(1)}, bf16[1024,8,48]{0,2,1:T(8,128)(2,1)}, u32[]{:S(2)}) copy-start(bf16[1024,8,48]{0,2,1:T(8,128)(2,1)} %copy-done.23) | copy-start | bytes 2359300
  225.4 37.2 %copy-start.26 = (f32[1024,8]{0,1:T(8,128)S(1)}, f32[1024,8]{0,1:T(8,128)}, u32[]{:S(2)}) copy-start(f32[1024,8]{0,1:T(8,128)} %copy-done.25) | copy-start | bytes 98308
  225.4 37.2 %copy-start.28 = (f32[1024,8]{0,1:T(8,128)S(1)}, f32[1024,8]{0,1:T(8,128)}, u32[]{:S(2)}) copy-start(f32[1024,8]{0,1:T(8,128)} %copy-done.27) | copy-start | bytes 98308
  262.6 5.0 copy-start.13
  267.6 16.3 %copy-start.5 = (f32[1024,1,8,64]{0,3,2,1:T(8,128)}, f32[1024,1,8,64]{0,3,2,1:T(8,128)S(1)}, u32[]{:S(2)}) copy-start(f32[1024,1,8,64]{0,3,2,1:T(8,128)S(1)} %get-tuple-element.68) | copy-start | bytes 6291460
  267.6 16.3 %copy-start.6 = (f32[1024,1,8,64]{0,3,2,1:T(8,128)}, f32[1024,1,8,64]{0,3,2,1:T(8,128)S(1)}, u32[]{:S(2)}) copy-start(f32[1024,1,8,64]{0,3,2,1:T(8,128)S(1)} %get-tuple-element.69) | copy-start | bytes 6291460
  267.6 8.9 copy-start.11
  283.9 1.3 copy-start.7
  283.9 3.6 copy-start.17
  285.2 1.7 copy-start.18
  292.6 134.8 %reduce-scatter.8.cloned.1.call-start = ((), (), s32[]{:S(2)}) async-start(), calls=%async_computation.7 | async-start | bytes 6291456 | tf_op jit(solution)/shard_map/reduce_scatter | solution.py:239
  292.6 12.9 %copy-start.38 = (bf16[1024,2048]{1,0:T(8,128)(2,1)S(1)}, bf16[1024,2048]{1,0:T(8,128)(2,1)}, u32[]{:S(2)}) copy-start(bf16[1024,2048]{1,0:T(8,128)(2,1)} %param.22) | copy-start | bytes 12582916
  303.5 2.0 copy-start.44
  305.5 6.3 copy-start.16
  311.7 4.4 copy-start.33
  311.7 4.4 copy-start.42
  311.7 692.8 %all-reduce.5.cloned.1.call-start = ((), (), s32[]{:S(2)}) async-start(), calls=%async_computation.8 | async-start | bytes 50331648 | tf_op jit(solution)/shard_map/psum | solution.py:255
  311.8 4.4 copy-start.19
  316.2 6.7 copy-start.39
  316.2 6.7 copy-start.47
  322.9 6.9 copy-start.45
  337.0 87.1 %copy-start.35 = (f32[1024]{0:T(1024)S(1)}, f32[1024]{0:T(1024)}, u32[]{:S(2)}) copy-start(f32[1024]{0:T(1024)} %param.25) | copy-start | bytes 12292
  424.1 8.0 copy-start.14
  427.3 4.8 copy-start.9
  427.3 5.1 copy-start.8
  1004.5 8.2 slice-start.2
  1004.5 6.9 copy-start.20
  1004.5 8.8 slice-start.3
  1011.4 6.2 slice-start
  1013.4 5.7 slice-start.1
  1013.4 9.1 copy-start.1
Sparse Core Ops, SparseCore 0:
  9.6 13.2 all-gather.2
  24.5 11.7 all-gather.4
  130.6 10.7 reduce-scatter.3
  292.7 13.1 reduce-scatter.5
  311.9 13.1 reduce-scatter.7
  337.1 667.3 all-reduce.4
where the time goes:
time: 1040 us; the launch traced here: 1030 us
  waiting for transfers between devices  534 us (51%)
  matrix products  274 us (26%)
  blocking collectives  123 us (12%)
  local copies, waits for them, and re-layouts  44.2 us (4%)
  other arithmetic  38.1 us (4%)
  between operations  15.3 us (1%)
    psum x1, waiting for transfers between devices, local(): lax.psum((qkv_grad, qkvbias_grad, dense_grad, inner_grad, innerbias_grad,...  527 us
    psum x1, blocking collectives, local(): lax.psum((qkv_grad, qkvbias_grad, dense_grad, inner_grad, innerbias_grad,...  81.2 us
    dot_general x2, matrix products, local(): jnp.einsum('hqk,khd->qhd', score_back, keys_bf, preferred_element_type=jn...  67.2 us
    dot_general x2, matrix products, local(): jnp.einsum('hqk,qhd->khd', score_back, queries[block_start:block_start +...  62.1 us
    psum x1, blocking collectives, local(): lax.psum((gain1_local, bias1_local, gain2_local, bias2_local, outbias_loc...  41.8 us
    unnamed x109, local copies, waits for them, and re-layouts  31.9 us
    dot_general x1, matrix products, local(): jnp.dot(second_in, inner_weight, preferred_element_type=jnp.float32)  25.1 us
  transfers between devices with their start and end apart: 6, of which 2 were waited for; matrix products, arithmetic and copies ran while one was open for 27% of the time, Pallas kernels for 0%

commit v1 on v0

v1 whole, which is shorter than its diff:
```python
import functools
import math

import jax
import jax.numpy as jnp
from jax import lax
from jax.experimental import pallas as pl
from jax.experimental.pallas import tpu as pltpu
from jax.sharding import PartitionSpec as P

HD = 64
ROT = 16
MAXLEN = 512
EPSILON = 1e-05
MASKED_SCORE = -1e30
SQRT_HALF = 0.7071067811865476
INV_ROOT_TWO_PI = 0.3989422804014327
F32 = jnp.float32
BF16 = jnp.bfloat16
PAIR = 2 * HD
QROWS = 256
HIDDEN = 256
VMEM = 56 * 1024 * 1024


def dot(lhs, rhs, contract):
    return lax.dot_general(lhs, rhs, (contract, ((), ())), preferred_element_type=F32)


NN = ((1,), (0,))
NT = ((1,), (1,))
TN = ((0,), (0,))


def ffn_kernel(second_ref, cot_ref, inner_ref, bias_ref, outer_ref, active_ref, back_ref, grads_ref, biasgrad_ref):
    second = second_ref[...]
    cot = cot_ref[...]
    preact = dot(second, inner_ref[...], NN) + bias_ref[...]
    cdf = 0.5 * (1.0 + lax.erf(preact * SQRT_HALF))
    slope = cdf + preact * jnp.exp(-0.5 * preact * preact) * INV_ROOT_TWO_PI
    active = (preact * cdf).astype(BF16)
    active_ref[...] = active
    pre_grad = dot(cot, outer_ref[...], NT) * slope
    biasgrad_ref[...] = jnp.sum(pre_grad, axis=0, keepdims=True)
    back = pre_grad.astype(BF16)
    back_ref[...] = back
    grads_ref[0] = dot(second, back, TN).astype(BF16)
    outer = dot(active, cot, TN).astype(BF16)
    for c in range(outer.shape[1] // HIDDEN):
        grads_ref[1, c * HIDDEN : (c + 1) * HIDDEN, :] = outer[:, c * HIDDEN : (c + 1) * HIDDEN]


def ffn_slice(second_in, cot, inner_weight, inner_bias, outer_weight, first, count):
    rows, width = second_in.shape
    cols = count * HIDDEN
    whole = pl.BlockSpec((rows, width), lambda j: (0, 0))
    return pl.pallas_call(
        ffn_kernel,
        grid=(count,),
        in_specs=[
            whole,
            whole,
            pl.BlockSpec((width, HIDDEN), lambda j: (0, first + j)),
            pl.BlockSpec((1, HIDDEN), lambda j: (0, first + j)),
            pl.BlockSpec((HIDDEN, width), lambda j: (first + j, 0)),
        ],
        out_specs=[
            pl.BlockSpec((rows, HIDDEN), lambda j: (0, j)),
            pl.BlockSpec((rows, HIDDEN), lambda j: (0, j)),
            pl.BlockSpec((2, width, HIDDEN), lambda j: (0, 0, j)),
            pl.BlockSpec((1, HIDDEN), lambda j: (0, j)),
        ],
        out_shape=[
            jax.ShapeDtypeStruct((rows, cols), BF16),
            jax.ShapeDtypeStruct((rows, cols), BF16),
            jax.ShapeDtypeStruct((2, width, cols), BF16),
            jax.ShapeDtypeStruct((1, cols), F32),
        ],
        compiler_params=pltpu.CompilerParams(vmem_limit_bytes=VMEM),
        cost_estimate=pl.CostEstimate(
            flops=8 * rows * width * cols, bytes_accessed=20 * width * cols, transcendentals=2 * rows * cols
        ),
    )(second_in, cot, inner_weight, inner_bias, outer_weight)


def partner(values):
    half = ROT // 2
    lane = lax.broadcasted_iota(jnp.int32, values.shape, 1) % HD
    lanes = values.shape[1]
    return jnp.where(lane < half, pltpu.roll(values, lanes - half, 1), pltpu.roll(values, half, 1))


def attention_kernel(
    slots, first_ref, cot_ref, w_ref, wbias_ref, dense_ref, cos_ref, sin_ref, segq_ref, segk_ref,
    context_ref, back_ref, grads_ref, biasgrad_ref, mask_ref, dk_ref, dv_ref,
):
    rows = first_ref.shape[0]
    blocks = rows // QROWS
    reach = -(-(MAXLEN - 1) // QROWS)

    @pl.when(pl.program_id(0) == 0)
    def _():
        for i in range(blocks):
            low = max(0, i - reach) * QROWS
            span = (i + 1) * QROWS - low
            seg_q = segq_ref[i * QROWS : (i + 1) * QROWS, :]
            seg_k = segk_ref[:, low : low + span]
            q_at = lax.broadcasted_iota(jnp.int32, (QROWS, span), 0) + i * QROWS
            k_at = lax.broadcasted_iota(jnp.int32, (QROWS, span), 1) + low
            allowed = ((seg_q == seg_k) & (k_at <= q_at) & (seg_q < slots)) | (k_at == q_at)
            mask_ref[i * QROWS : (i + 1) * QROWS, :span] = jnp.where(allowed, 0.0, MASKED_SCORE)

    first = first_ref[...]
    cot = cot_ref[...]
    weight = jnp.concatenate([w_ref[0], w_ref[1], w_ref[2]], axis=1)
    bias = jnp.concatenate([wbias_ref[0], wbias_ref[1], wbias_ref[2]], axis=1)
    projected = dot(first, weight, NN) + bias
    cosine = cos_ref[...]
    sine = sin_ref[...]
    q = projected[:, :PAIR]
    k = projected[:, PAIR : 2 * PAIR]
    queries = (q * cosine + partner(q) * sine).astype(BF16)
    keys = (k * cosine + partner(k) * sine).astype(BF16)
    values = projected[:, 2 * PAIR :].astype(BF16)
    context_back = dot(cot, dense_ref[...], NT).astype(BF16)

    lane_head = lax.broadcasted_iota(jnp.int32, (QROWS, PAIR), 1) // HD
    scale = HD**-0.5
    dk_ref[...] = jnp.zeros_like(dk_ref)
    dv_ref[...] = jnp.zeros_like(dv_ref)
    contexts = []
    dqs = []
    for i in range(blocks):
        low = max(0, i - reach) * QROWS
        high = (i + 1) * QROWS
        mask = mask_ref[i * QROWS : high, : high - low]
        q_block = queries[i * QROWS : high]
        b_block = context_back[i * QROWS : high]
        k_block = keys[low:high]
        v_block = values[low:high]
        ctx = None
        for h in range(2):
            mine = lane_head == h
            q_head = jnp.where(mine, q_block, jnp.zeros_like(q_block))
            b_head = jnp.where(mine, b_block, jnp.zeros_like(b_block))
            scores = dot(q_head, k_block, NT) * scale + mask
            highest = jnp.max(scores, axis=1, keepdims=True)
            exponent = jnp.exp(scores - highest)
            total = jnp.sum(exponent, axis=1, keepdims=True)
            weights = exponent * (1.0 / total)
            weights_bf = weights.astype(BF16)
            prob_grad = dot(b_head, v_block, NT)
            delta = jnp.sum(weights * prob_grad, axis=1, keepdims=True)
            score_back = (weights * (prob_grad - delta)).astype(BF16)
            ctx_head = dot(weights_bf, v_block, NN)
            dq_head = dot(score_back, k_block, NN)
            dk_ref[low:high, :] += dot(score_back, q_head, TN)
            dv_ref[low:high, :] += dot(weights_bf, b_head, TN)
            ctx = ctx_head if h == 0 else jnp.where(mine, ctx_head, ctx)
            dq = dq_head if h == 0 else jnp.where(mine, dq_head, dq)
        contexts.append(ctx.astype(BF16))
        dqs.append(dq)
    context = jnp.concatenate(contexts, axis=0)
    context_ref[...] = context
    dq = jnp.concatenate(dqs, axis=0) * scale
    dk = dk_ref[...] * scale
    dv = dv_ref[...]
    dq = dq * cosine - partner(dq) * sine
    dk = dk * cosine - partner(dk) * sine
    back = jnp.concatenate([dq, dk, dv], axis=1)
    biasgrad_ref[0] = jnp.sum(back, axis=0, keepdims=True)
    back = back.astype(BF16)
    back_ref[0] = back
    weight_grad = dot(first, back, TN).astype(BF16)
    grads_ref[0] = weight_grad[:, : 2 * PAIR]
    grads_ref[1, :, :PAIR] = weight_grad[:, 2 * PAIR :]
    dense_grad = dot(context, cot, TN).astype(BF16)
    for c in range(dense_grad.shape[1] // PAIR):
        grads_ref[1, c * PAIR : (c + 1) * PAIR, PAIR:] = dense_grad[:, c * PAIR : (c + 1) * PAIR]


def attention_slice(first_in, cot, qkv, qkv_bias, dense_weight, cosine, sine, segment, slots, first, count):
    rows, width = first_in.shape
    reach = -(-(MAXLEN - 1) // QROWS)
    span = min(rows, (reach + 1) * QROWS)
    whole = pl.BlockSpec((rows, width), lambda j: (0, 0))
    table = pl.BlockSpec((rows, PAIR), lambda j: (0, 0))
    return pl.pallas_call(
        functools.partial(attention_kernel, slots),
        grid=(count,),
        in_specs=[
            whole,
            whole,
            pl.BlockSpec((3, width, PAIR), lambda j: (0, 0, first + j)),
            pl.BlockSpec((3, 1, PAIR), lambda j: (0, 0, first + j)),
            pl.BlockSpec((PAIR, width), lambda j: (first + j, 0)),
            table,
            table,
            pl.BlockSpec((rows, 1), lambda j: (0, 0)),
            pl.BlockSpec((1, rows), lambda j: (0, 0)),
        ],
        out_specs=[
            pl.BlockSpec((rows, PAIR), lambda j: (0, j)),
            pl.BlockSpec((1, rows, 3 * PAIR), lambda j: (j, 0, 0)),
            pl.BlockSpec((2, width, 2 * PAIR), lambda j: (0, 0, j)),
            pl.BlockSpec((1, 1, 3 * PAIR), lambda j: (j, 0, 0)),
        ],
        out_shape=[
            jax.ShapeDtypeStruct((rows, count * PAIR), BF16),
            jax.ShapeDtypeStruct((count, rows, 3 * PAIR), BF16),
            jax.ShapeDtypeStruct((2, width, count * 2 * PAIR), BF16),
            jax.ShapeDtypeStruct((count, 1, 3 * PAIR), F32),
        ],
        scratch_shapes=[
            pltpu.VMEM((rows, span), F32),
            pltpu.VMEM((rows, PAIR), F32),
            pltpu.VMEM((rows, PAIR), F32),
        ],
        compiler_params=pltpu.CompilerParams(vmem_limit_bytes=VMEM),
        cost_estimate=pl.CostEstimate(
            flops=count * 30 * rows * width * PAIR,
            bytes_accessed=16 * width * count * PAIR,
            transcendentals=count * 2 * rows * span,
        ),
    )(first_in, cot, qkv, qkv_bias, dense_weight, cosine, sine, segment.reshape(rows, 1), segment.reshape(1, rows))


def rings(size):
    if size == 16:
        return [(4, 4), (2, 2), (1, 2)]
    lengths = []
    left = size
    while left > 1:
        length = next(f for f in (2, 4, 3, 5, 7, left) if left % f == 0 and (f != 2 or not lengths))
        lengths.insert(0, length)
        left //= length
    out = []
    stride = 1
    for length in reversed(lengths):
        out.insert(0, (stride, length))
        stride *= length
    while len(out) < 3:
        out.insert(0, (stride, 1))
    return [(out[0][0], math.prod(l for _, l in out[:-2]))] + out[-2:] if len(out) > 3 else out


def ring_pairs(size, stride, length):
    return [(i, i + ((i // stride + 1) % length - i // stride % length) * stride) for i in range(size)]


def piece(values, index, length):
    axis = values.ndim - 2
    rows = values.shape[axis] // length
    return lax.dynamic_slice_in_dim(values, index * rows, rows, axis)


def ring_reduce(values, size, ring):
    stride, length = ring
    if length == 1:
        return values
    at = lax.axis_index("dp") // stride % length
    pairs = ring_pairs(size, stride, length)
    held = piece(values, (at + length - 1) % length, length)
    for step in range(length - 1):
        came = lax.ppermute(held, "dp", pairs)
        own = piece(values, (at + 2 * length - 2 - step) % length, length)
        held = (came.astype(F32) + own.astype(F32)).astype(BF16)
    return held


def ring_gather(held, size, ring):
    stride, length = ring
    if length == 1:
        return held
    at = lax.axis_index("dp") // stride % length
    pairs = ring_pairs(size, stride, length)
    axis = held.ndim - 2
    parts = [held]
    for _ in range(length - 1):
        parts.append(lax.ppermute(parts[-1], "dp", pairs))
    ordered = []
    for slot in range(length):
        chosen = parts[0]
        for back in range(1, length):
            chosen = jnp.where((at + length - back) % length == slot, parts[back], chosen)
        ordered.append(chosen)
    return jnp.concatenate(ordered, axis=axis)


def reduce_over_dp(grads, size):
    slow, mid, fast = rings(size)
    left = ring_reduce(grads[0], size, fast)
    right = ring_reduce(grads[1], size, mid)
    left = ring_reduce(left, size, mid)
    right = ring_reduce(right, size, fast)
    both = jnp.stack([left, right])
    both = ring_gather(ring_reduce(both, size, slow), size, slow)
    left = ring_gather(both[0], size, mid)
    right = ring_gather(both[1], size, fast)
    left = ring_gather(left, size, fast)
    right = ring_gather(right, size, mid)
    return left, right


def butterfly(values, axis, size):
    if size & (size - 1):
        return lax.psum(values, axis)
    step = 1
    while step < size:
        values = values + lax.ppermute(values, axis, [(i, i ^ step) for i in range(size)])
        step *= 2
    return values


def normalize(values):
    mean_val = jnp.mean(values, axis=-1, keepdims=True)
    centred = values - mean_val
    inv_std = lax.rsqrt(jnp.mean(centred * centred, axis=-1, keepdims=True) + EPSILON)
    return (centred * inv_std, inv_std)


def layout(lengths, row_count):
    slot_count = lengths.shape[0]
    places = jnp.arange(row_count, dtype=jnp.int32)
    seq_ends = jnp.cumsum(lengths)
    seq_starts = seq_ends - lengths
    segment = jnp.sum((places[:, None] >= seq_ends[None, :]).astype(jnp.int32), axis=1)
    member = segment[:, None] == jnp.arange(slot_count, dtype=jnp.int32)[None, :]
    position = places - jnp.sum(jnp.where(member, seq_starts[None, :], 0), axis=1)
    return (segment, position)


def rotary_tables(position):
    half = ROT // 2
    lane = jnp.arange(PAIR, dtype=jnp.int32) % HD
    frequency = jnp.exp(-(2.0 * (lane % half).astype(F32) / ROT) * math.log(10000.0))
    angle = position.astype(F32)[:, None] * jnp.where(lane < ROT, frequency, 0.0)[None, :]
    sign = jnp.where(lane < half, -1.0, jnp.where(lane < ROT, 1.0, 0.0))
    return (jnp.cos(angle), jnp.sin(angle) * sign[None, :])


def gather_rows(values, size):
    if size != 2:
        return lax.all_gather(values, "tensor", axis=0, tiled=True)
    other = lax.ppermute(values, "tensor", [(0, 1), (1, 0)])
    here = lax.axis_index("tensor")
    return jnp.concatenate([jnp.where(here == 0, values, other), jnp.where(here == 0, other, values)], axis=0)


def scatter_sum(values, size):
    if size != 2:
        return lax.psum_scatter(values, "tensor", scatter_dimension=0, tiled=True).astype(F32)
    rows = values.shape[0] // 2
    here = lax.axis_index("tensor")
    away = lax.dynamic_slice_in_dim(values, (1 - here) * rows, rows, 0).astype(BF16)
    mine = lax.dynamic_slice_in_dim(values, here * rows, rows, 0)
    return lax.ppermute(away, "tensor", [(0, 1), (1, 0)]).astype(F32) + mine.astype(F32)


def local(
    dp_size,
    tensor_size,
    residual,
    norm1_gain,
    norm1_bias,
    norm2_gain,
    norm2_bias,
    qkv_weight,
    qkv_bias,
    dense_weight,
    inner_weight,
    inner_bias,
    outer_weight,
    out_bias,
    cotangent,
    seq_lengths,
):
    local_rows, width = residual.shape
    head_width = qkv_weight.shape[2]
    hidden = inner_weight.shape[1]
    slots = seq_lengths.shape[1]

    gathered = gather_rows(residual, tensor_size)
    cot = gather_rows(cotangent, tensor_size)
    rows = gathered.shape[0]
    segment, position = layout(seq_lengths[0], rows)
    cosine, sine = rotary_tables(position)
    qkv = jnp.transpose(qkv_weight, (1, 0, 2))
    normed, inv_std = normalize(gathered.astype(F32))
    first_in = (normed * norm1_gain + norm1_bias).astype(BF16)
    second_in = (normed * norm2_gain + norm2_bias).astype(BF16)

    steps = hidden // HIDDEN
    per = max(1, steps // 4)
    ffn = [
        ffn_slice(second_in, cot, inner_weight, inner_bias.reshape(1, -1), outer_weight, at, per)
        for at in range(0, steps, per)
    ]
    pairs = head_width // PAIR
    per_pair = max(1, pairs // 2)
    attn = [
        attention_slice(
            first_in, cot, qkv, qkv_bias.reshape(3, 1, -1), dense_weight, cosine, sine, segment, slots, at, per_pair
        )
        for at in range(0, pairs, per_pair)
    ]
    ffn_sums = [reduce_over_dp(f[2], dp_size) for f in ffn]
    attn_sums = [reduce_over_dp(a[2], dp_size) for a in attn]

    active = jnp.concatenate([f[0] for f in ffn], axis=1)
    pre_back = jnp.concatenate([f[1] for f in ffn], axis=1)
    context = jnp.concatenate([a[0] for a in attn], axis=1)
    qkv_back = jnp.concatenate([a[1] for a in attn], axis=0)
    branch = (dot(context, dense_weight, NN) + dot(active, outer_weight, NN)).astype(BF16)
    summed = scatter_sum(branch, tensor_size)
    layer_out = (residual.astype(F32) + summed + out_bias).astype(BF16)

    back3 = qkv_back.reshape(pairs, rows, 3, PAIR).transpose(1, 2, 0, 3).reshape(rows, 3 * head_width)
    weight3 = jnp.transpose(qkv, (0, 2, 1)).reshape(3 * head_width, width)
    first_grad = dot(back3, weight3, NN)
    second_grad = dot(pre_back, inner_weight, NT)
    combined = scatter_sum(first_grad * norm1_gain + second_grad * norm2_gain, tensor_size)
    own_normed, own_inv = normalize(residual.astype(F32))
    residual_grad = (
        cotangent.astype(F32)
        + own_inv
        * (
            combined
            - jnp.mean(combined, axis=-1, keepdims=True)
            - own_normed * jnp.mean(combined * own_normed, axis=-1, keepdims=True)
        )
    ).astype(BF16)

    over_all = jnp.stack(
        [
            jnp.sum(first_grad * normed, axis=0),
            jnp.sum(first_grad, axis=0),
            jnp.sum(second_grad * normed, axis=0),
            jnp.sum(second_grad, axis=0),
            jnp.sum(cotangent.astype(F32), axis=0),
        ]
    ).reshape(-1)
    over_all = butterfly(over_all, "tensor", tensor_size)
    qkvbias = jnp.concatenate([a[3] for a in attn], axis=0).reshape(pairs, 3, PAIR).transpose(1, 0, 2).reshape(-1)
    innerbias = jnp.concatenate([f[3] for f in ffn], axis=1).reshape(-1)
    vectors = butterfly(jnp.concatenate([over_all, qkvbias, innerbias]), "dp", dp_size)
    ends = [width * i for i in range(1, 6)] + [5 * width + 3 * head_width]
    gain1_grad, bias1_grad, gain2_grad, bias2_grad, outbias_grad, qkvbias_grad, innerbias_grad = jnp.split(vectors, ends)

    inner_grad = jnp.concatenate([s[0] for s in ffn_sums], axis=1).astype(F32)
    outer_grad = jnp.concatenate(
        [
            s[1].reshape(width // HIDDEN, HIDDEN, per, HIDDEN).transpose(2, 1, 0, 3).reshape(per * HIDDEN, width)
            for s in ffn_sums
        ],
        axis=0,
    ).astype(F32)
    qk_parts = [s[0].reshape(width, per_pair, 2, PAIR) for s in attn_sums]
    vd_parts = [s[1].reshape(width, per_pair, 2, PAIR) for s in attn_sums]
    qk_grad = jnp.concatenate(qk_parts, axis=1).transpose(0, 2, 1, 3).reshape(width, 2, head_width)
    v_grad = jnp.concatenate([p[:, :, 0] for p in vd_parts], axis=1).reshape(width, 1, head_width)
    qkv_grad = jnp.concatenate([qk_grad, v_grad], axis=1).astype(F32)
    dense_grad = jnp.concatenate(
        [
            p[:, :, 1].reshape(width // PAIR, PAIR, per_pair, PAIR).transpose(2, 1, 0, 3).reshape(per_pair * PAIR, width)
            for p in vd_parts
        ],
        axis=0,
    ).astype(F32)
    return (
        layer_out,
        residual_grad,
        gain1_grad,
        bias1_grad,
        gain2_grad,
        bias2_grad,
        qkv_grad,
        qkvbias_grad.reshape(3, head_width),
        dense_grad,
        inner_grad,
        innerbias_grad,
        outer_grad,
        outbias_grad,
    )


def solution(mesh):
    rows = P(("dp", "tensor"), None)
    return jax.shard_map(
        functools.partial(local, mesh.shape["dp"], mesh.shape["tensor"]),
        mesh=mesh,
        in_specs=(
            rows,
            P(),
            P(),
            P(),
            P(),
            P(None, None, "tensor"),
            P(None, "tensor"),
            P("tensor", None),
            P(None, "tensor"),
            P("tensor"),
            P("tensor", None),
            P(),
            rows,
            P("dp", None),
        ),
        out_specs=(
            rows,
            rows,
            P(),
            P(),
            P(),
            P(),
            P(None, None, "tensor"),
            P(None, "tensor"),
            P("tensor", None),
            P(None, "tensor"),
            P("tensor"),
            P("tensor", None),
            P(),
        ),
        check_vma=False,
    )
```

time: 1040 us -> 543 us (0.52)
  waiting for transfers between devices: 534 us -> 137 us
  matrix products: 274 us -> 22.6 us
  blocking collectives: 123 us -> 0 us
  starting transfers between devices: 0.24 us -> 94.2 us
  Pallas kernels: 0 us -> 86.2 us
  other arithmetic: 38.1 us -> 118 us
  local copies, waits for them, and re-layouts: 44.2 us -> 75.7 us
  between operations: 15.3 us -> 3.15 us
    psum x1 -> x0, waiting for transfers between devices: 527 us -> none  [local(): lax.psum((qkv_grad, qkvbias_grad, dense_grad, inner_grad, innerbias_grad,...]
    dot_general x24 -> x4, matrix products: 274 us -> 22.6 us  [dot(): lax.dot_general(lhs, rhs, (contract, ((), ())), preferred_element_type=F32)]
    ppermute x0 -> x93, waiting for transfers between devices: none -> 137 us  [the longest x42 75.2 us: ring_reduce(): came = lax.ppermute(held, 'dp', pairs)]
    psum x2 -> x0, blocking collectives: 123 us -> none  [the longest x1 81.2 us: local(): lax.psum((qkv_grad, qkvbias_grad, dense_grad, inner_grad, innerbias_grad,...]
    ppermute x0 -> x93, starting transfers between devices: none -> 94.2 us  [the longest x42 51.7 us: ring_reduce(): came = lax.ppermute(held, 'dp', pairs)]
    pallas_call x0 -> x6, Pallas kernels: none -> 86.2 us  [the longest x2 50.1 us: attention_slice(): pl.pallas_call(functools.partial(attention_kernel, slots), grid=(count,),...]
    convert_element_type x3 -> x36, other arithmetic: 3.89 us -> 54.7 us  [the longest x1 27.1 us: local(): inner_grad = jnp.concatenate([s[0] for s in ffn_sums], axis=1).astype(F32)]
    select_n x0 -> x26, other arithmetic: none -> 25.4 us  [the longest x24 23.2 us: ring_gather(): jnp.where((at + length - back) % length == slot, parts[back], chosen)]
  transfers between devices with their start and end apart: 6 -> 93, of which waited for: 2 -> 43; matrix products, arithmetic and copies ran while one was open for 27% -> 28% of each run, Pallas kernels for 0% -> 0%
where the time goes in v1:
time: 543 us; the launch traced here: 537 us
  waiting for transfers between devices  137 us (25%)
  other arithmetic  118 us (22%)
  starting transfers between devices  94.2 us (17%)
  Pallas kernels  86.2 us (16%)
  local copies, waits for them, and re-layouts  75.7 us (14%)
  matrix products  22.6 us (4%)
    ppermute x42, waiting for transfers between devices, ring_reduce(): came = lax.ppermute(held, 'dp', pairs)  75.2 us
    ppermute x42, starting transfers between devices, ring_reduce(): came = lax.ppermute(held, 'dp', pairs)  51.7 us
    pallas_call x2, Pallas kernels, attention_slice(): pl.pallas_call(functools.partial(attention_kernel, slots), grid=(count,),...  50.1 us
    pallas_call x4, Pallas kernels, ffn_slice(): pl.pallas_call(ffn_kernel, grid=(count,), in_specs=[whole, whole, pl.Bloc...  36 us
    ppermute x5, waiting for transfers between devices, butterfly(): lax.ppermute(values, axis, [(i, i ^ step) for i in range(size)])  36 us
    ppermute x42, starting transfers between devices, ring_gather(): parts.append(lax.ppermute(parts[-1], 'dp', pairs))  34.8 us
    convert_element_type x1, other arithmetic, local(): inner_grad = jnp.concatenate([s[0] for s in ffn_sums], axis=1).astype(F32)  27.1 us
    ppermute x42, waiting for transfers between devices, ring_gather(): parts.append(lax.ppermute(parts[-1], 'dp', pairs))  26.1 us
  transfers between devices with their start and end apart: 93, of which 43 were waited for; matrix products, arithmetic and copies ran while one was open for 28% of the time, Pallas kernels for 0%

profile of v1, /device:TPU:0, one launch (start us, length us, event | category | flops | bytes accessed | tf_op | source)
XLA Modules:
  0.0 537.5 jit_solution(15846711098725036728)
XLA Ops:
  6.8 4.6 copy.73
  12.6 3.0 fusion.56
  16.6 2.1 broadcast_select_fusion.1
  21.4 3.4 fusion.7
  24.7 25.3 %shard_map.238 = (bf16[1024,256]{1,0:T(8,128)(2,1)}, bf16[2,1024,384]{2,1,0:T(8,128)(2,1)}, bf16[2,1024,512]{2,1,0:T(8,128)(2,1)}, f32[2,1,384]{2,1,0:T(1,128)}) custom-call(bf16[1024,1024]{1,0:T(8,128)(2,1)} %get-tuple-element.70.first_ref, bf16[1024,1024]{1,0:T(8,128)(2,1)} %pad_maximum_fusion.2.cot_ref, bf16[3,1024,512]{2,1,0:T(8,128)(2,1)} %bitcast.250, ...), custom_call_target="tpu_custom_call" | custom-call | flops 8053063680 | bytes 4194304 | tf_op jit(solution)/shard_map/pallas_call | solution.py:188
  50.0 24.9 %shard_map.237 = (bf16[1024,256]{1,0:T(8,128)(2,1)}, bf16[2,1024,384]{2,1,0:T(8,128)(2,1)}, bf16[2,1024,512]{2,1,0:T(8,128)(2,1)}, f32[2,1,384]{2,1,0:T(1,128)}) custom-call(bf16[1024,1024]{1,0:T(8,128)(2,1)} %get-tuple-element.70.first_ref, bf16[1024,1024]{1,0:T(8,128)(2,1)} %pad_maximum_fusion.2.cot_ref, bf16[3,1024,512]{2,1,0:T(8,128)(2,1)} %bitcast.251, ...), custom_call_target="tpu_custom_call" | custom-call | flops 8053063680 | bytes 4194304 | tf_op jit(solution)/shard_map/pallas_call | solution.py:188
  74.9 8.8 %shard_map.242 = (bf16[1024,512]{1,0:T(8,128)(2,1)}, bf16[1024,512]{1,0:T(8,128)(2,1)}, bf16[2,1024,512]{2,1,0:T(8,128)(2,1)}, f32[1,512]{1,0:T(1,128)}) custom-call(bf16[1024,1024]{1,0:T(8,128)(2,1)} %get-tuple-element.71.second_ref, bf16[1024,1024]{1,0:T(8,128)(2,1)} %pad_maximum_fusion.2.cot_ref, bf16[1024,2048]{1,0:T(8,128)(2,1)} %inner_ref.7, ...), custom_call_target="tpu_custom_call" | custom-call | flops 4294967296 | bytes 10485760 | tf_op jit(solution)/shard_map/pallas_call | solution.py:57
  83.7 9.3 %shard_map.241 = (bf16[1024,512]{1,0:T(8,128)(2,1)}, bf16[1024,512]{1,0:T(8,128)(2,1)}, bf16[2,1024,512]{2,1,0:T(8,128)(2,1)}, f32[1,512]{1,0:T(1,128)}) custom-call(bf16[1024,1024]{1,0:T(8,128)(2,1)} %get-tuple-element.71.second_ref, bf16[1024,1024]{1,0:T(8,128)(2,1)} %pad_maximum_fusion.2.cot_ref, bf16[1024,2048]{1,0:T(8,128)(2,1)} %inner_ref.7, ...), custom_call_target="tpu_custom_call" | custom-call | flops 4294967296 | bytes 10485760 | tf_op jit(solution)/shard_map/pallas_call | solution.py:57
  93.0 8.9 %shard_map.240 = (bf16[1024,512]{1,0:T(8,128)(2,1)}, bf16[1024,512]{1,0:T(8,128)(2,1)}, bf16[2,1024,512]{2,1,0:T(8,128)(2,1)}, f32[1,512]{1,0:T(1,128)}) custom-call(bf16[1024,1024]{1,0:T(8,128)(2,1)} %get-tuple-element.71.second_ref, bf16[1024,1024]{1,0:T(8,128)(2,1)} %pad_maximum_fusion.2.cot_ref, bf16[1024,2048]{1,0:T(8,128)(2,1)} %inner_ref.7, ...), custom_call_target="tpu_custom_call" | custom-call | flops 4294967296 | bytes 10485760 | tf_op jit(solution)/shard_map/pallas_call | solution.py:57
  101.9 9.0 %shard_map.239 = (bf16[1024,512]{1,0:T(8,128)(2,1)}, bf16[1024,512]{1,0:T(8,128)(2,1)}, bf16[2,1024,512]{2,1,0:T(8,128)(2,1)}, f32[1,512]{1,0:T(1,128)}) custom-call(bf16[1024,1024]{1,0:T(8,128)(2,1)} %get-tuple-element.71.second_ref, bf16[1024,1024]{1,0:T(8,128)(2,1)} %pad_maximum_fusion.2.cot_ref, bf16[1024,2048]{1,0:T(8,128)(2,1)} %inner_ref.7, ...), custom_call_target="tpu_custom_call" | custom-call | flops 4294967296 | bytes 10485760 | tf_op jit(solution)/shard_map/pallas_call | solution.py:57
  113.0 4.6 copy.71
  117.6 2.3 copy.72
  120.4 5.0 fusion.115
  125.4 9.8 %fusion.104 = (f32[1024]{0:T(1024)}, f32[1024]{0:T(1024)}, f32[1024,1024]{1,0:T(8,128)S(1)}, f32[1024]{0:T(1024)}, f32[1024]{0:T(1024)}) fusion(f32[1024]{0:T(1024)S(1)} %add_rsqrt_fusion, f32[1024]{0:T(1024)S(1)} %broadcast_multiply_fusion, bf16[512,1024]{1,0:T(8,128)(2,1)S(1)} %get-tuple-element.200, bf16[512,1024]{1,0:T(8,128)(2,1)S(1)} %get-tuple-element.201, ...), kind=kOutput, calls=%fused_computation.382 | convolution fusion | flops 4327469056 | bytes 18907136 | tf_op jit(solution)/shard_map/dot_general | solution.py:27
  137.0 6.5 %fusion.13 = f32[1024,1024]{1,0:T(8,128)S(1)} fusion(bf16[2048,1024]{1,0:T(8,128)(2,1)S(1)} %copy-done.122, bf16[1024,512]{1,0:T(8,128)(2,1)S(1)} %copy-done.123, bf16[1024,512]{1,0:T(8,128)(2,1)} %get-tuple-element.41, bf16[1024,512]{1,0:T(8,128)(2,1)} %get-tuple-element.40, bf16[1024,512]{1,0:T(8,128)(2,1)} %get-tuple-element.39), kind=kOutput, calls=%fused_computation.15 | convolution fusion | flops 4311744512 | bytes 12582912 | tf_op jit(solution)/shard_map/dot_general | solution.py:27
  147.2 2.6 collective-permute-start.21
  166.3 7.6 %collective-permute-done.9 = bf16[512,512]{1,0:T(8,128)(2,1)} collective-permute-done((bf16[512,512]{1,0:T(8,128)(2,1)}, bf16[512,512]{1,0:T(8,128)(2,1)}, u32[]{:S(2)}, u32[]{:S(2)}) %collective-permute-start.9) | collective-permute-done | bytes 524320 | tf_op jit(solution)/shard_map/ppermute | solution.py:265
  180.7 8.2 %collective-permute-done.73 = bf16[512,512]{1,0:T(8,128)(2,1)S(1)} collective-permute-done((bf16[512,512]{1,0:T(8,128)(2,1)}, bf16[512,512]{1,0:T(8,128)(2,1)S(1)}, u32[]{:S(2)}, u32[]{:S(2)}) %collective-permute-start.73) | collective-permute-done | bytes 524320 | tf_op jit(solution)/shard_map/ppermute | solution.py:265
  192.7 7.4 %collective-permute-done.61 = bf16[512,512]{1,0:T(8,128)(2,1)S(1)} collective-permute-done((bf16[512,512]{1,0:T(8,128)(2,1)S(1)}, bf16[512,512]{1,0:T(8,128)(2,1)S(1)}, u32[]{:S(2)}, u32[]{:S(2)}) %collective-permute-start.61) | collective-permute-done | bytes 524320 | tf_op jit(solution)/shard_map/ppermute | solution.py:265
  203.8 7.6 %collective-permute-done.49 = bf16[512,512]{1,0:T(8,128)(2,1)S(1)} collective-permute-done((bf16[512,512]{1,0:T(8,128)(2,1)S(1)}, bf16[512,512]{1,0:T(8,128)(2,1)S(1)}, u32[]{:S(2)}, u32[]{:S(2)}) %collective-permute-start.49) | collective-permute-done | bytes 524320 | tf_op jit(solution)/shard_map/ppermute | solution.py:265
  215.8 5.6 %collective-permute-done.37 = bf16[512,512]{1,0:T(8,128)(2,1)S(1)} collective-permute-done((bf16[512,512]{1,0:T(8,128)(2,1)S(1)}, bf16[512,512]{1,0:T(8,128)(2,1)S(1)}, u32[]{:S(2)}, u32[]{:S(2)}) %collective-permute-start.37) | collective-permute-done | bytes 524320 | tf_op jit(solution)/shard_map/ppermute | solution.py:265
  223.0 3.2 collective-permute-done.39
  228.3 3.6 collective-permute-done.22
  233.1 2.2 collective-permute-done.10
  239.4 3.0 collective-permute-start.62
  263.4 3.0 collective-permute-done.25
  267.1 2.1 collective-permute-done.13
  269.9 2.1 collective-permute-done.77
  272.7 2.1 collective-permute-done.65
  275.5 2.1 collective-permute-done.53
  278.3 2.1 collective-permute-done.41
  285.5 4.2 convert_reduce_fusion.2
  290.7 2.2 collective-permute-start.42
  299.2 2.1 collective-permute-done.5
  307.0 2.1 collective-permute-start.67
  309.3 4.9 collective-permute-done.7
  315.5 3.3 collective-permute-start.8
  323.2 2.1 collective-permute-done.43
  326.1 27.7 %collective-permute-done.8 = f32[8704]{0:T(1024)S(1)} collective-permute-done((f32[8704]{0:T(1024)S(1)}, f32[8704]{0:T(1024)S(1)}, u32[]{:S(2)}, u32[]{:S(2)}) %collective-permute-start.8) | collective-permute-done | bytes 34848 | tf_op jit(solution)/shard_map/ppermute | solution.py:310
  354.4 4.4 collective-permute-start.17
  363.7 2.6 collective-permute-start.45
  390.8 3.2 collective-permute-done.33
  397.3 2.4 collective-permute-done.91
  401.2 4.1 collective-permute-done.89
  407.4 3.5 collective-permute-done.87
  424.5 5.8 %collective-permute-done.34 = bf16[512,512]{1,0:T(8,128)(2,1)} collective-permute-done((bf16[512,512]{1,0:T(8,128)(2,1)}, bf16[512,512]{1,0:T(8,128)(2,1)}, u32[]{:S(2)}, u32[]{:S(2)}) %collective-permute-start.34) | collective-permute-done | bytes 524320 | tf_op jit(solution)/shard_map/ppermute | solution.py:280
  433.2 2.1 collective-permute-start.92
  437.9 2.4 fusion.113
  442.8 4.3 maximum_bitcast_fusion
  447.1 2.3 fusion.112
  454.4 2.7 reshape.269
  464.7 2.2 broadcast_select_fusion.11
  467.9 2.1 reshape.281
  470.0 2.1 copy.87
  474.4 2.3 reshape.279
  476.7 2.1 copy.86
  482.0 2.2 broadcast_select_fusion.13
  485.3 2.1 reshape.277
  487.4 2.1 copy.85
  491.8 2.1 reshape.275
  493.9 2.1 copy.84
  498.8 3.1 maximum_convert_fusion.2
  505.0 3.9 maximum_convert_fusion.1
  510.1 27.1 %maximum_convert_fusion = f32[1024,2048]{1,0:T(8,128)} fusion(bf16[512,512]{1,0:T(8,128)(2,1)S(1)} %get-tuple-element.103, bf16[512,512]{1,0:T(8,128)(2,1)S(1)} %get-tuple-element.102, bf16[512,512]{1,0:T(8,128)(2,1)S(1)} %get-tuple-element.101, bf16[512,512]{1,0:T(8,128)(2,1)S(1)} %get-tuple-element.100, bf16[512,512]{1,0:T(8,128)(2,1)S(1)} %get-tuple-element.99, ...), kind=kLoop, calls=%fused_computation.31 | loop fusion | flops 33554432 | bytes 12582912 | tf_op jit(solution)/shard_map/convert_element_type | solution.py:450
  (596 shorter events, 198.3 us)
Async XLA Ops:
  0.7 15.0 %collective-permute-start.1 = (bf16[512,1024]{1,0:T(8,128)(2,1)}, bf16[512,1024]{1,0:T(8,128)(2,1)S(1)}, u32[]{:S(2)}, u32[]{:S(2)}) collective-permute-start(bf16[512,1024]{1,0:T(8,128)(2,1)} %param.26), channel_id=1, source_target_pairs={{0,1},{1,0},{2,3},{3,2},{4,5},{5,4},{6,7},{7,6},{8,9},{9,8},{10,11... | collective-permute-start | bytes 3145736 | tf_op jit(solution)/shard_map/ppermute | solution.py:345
  1.2 15.4 %collective-permute-start = (bf16[512,1024]{1,0:T(8,128)(2,1)}, bf16[512,1024]{1,0:T(8,128)(2,1)}, u32[]{:S(2)}, u32[]{:S(2)}) collective-permute-start(bf16[512,1024]{1,0:T(8,128)(2,1)} %param.14), channel_id=1, source_target_pairs={{0,1},{1,0},{2,3},{3,2},{4,5},{5,4},{6,7},{7,6},{8,9},{9,8},{10,11... | collective-permute-start | bytes 3145736 | tf_op jit(solution)/shard_map/ppermute | solution.py:345
  136.5 144.0 %collective-permute-start.3 = (bf16[512,1024]{1,0:T(8,128)(2,1)}, bf16[512,1024]{1,0:T(8,128)(2,1)}, u32[]{:S(2)}, u32[]{:S(2)}) collective-permute-start(bf16[512,1024]{1,0:T(8,128)(2,1)} %dynamic-slice_convert_fusion), channel_id=1, source_target_pairs={{0,1},{1,0},{2,3},{3,2},{4,5},{5,4},{6,7},{7,6},{8,9},{9,8},{10,11... | collective-permute-start | bytes 3145736 | tf_op jit(solution)/shard_map/ppermute | solution.py:357
  145.8 138.1 %collective-permute-start.2 = (bf16[512,1024]{1,0:T(8,128)(2,1)}, bf16[512,1024]{1,0:T(8,128)(2,1)}, u32[]{:S(2)}, u32[]{:S(2)}) collective-permute-start(bf16[512,1024]{1,0:T(8,128)(2,1)} %constant_dynamic-slice_fusion.12), channel_id=1, source_target_pairs={{0,1},{1,0},{2,3},{3,2},{4,5},{5,4},{6,7},{7,6},{8,9},{9,8},{10,11... | collective-permute-start | bytes 3145736 | tf_op jit(solution)/shard_map/ppermute | solution.py:357
  147.2 16.0 %collective-permute-start.21 = (bf16[512,512]{1,0:T(8,128)(2,1)}, bf16[512,512]{1,0:T(8,128)(2,1)}, u32[]{:S(2)}, u32[]{:S(2)}) collective-permute-start(bf16[512,512]{1,0:T(8,128)(2,1)} %dynamic-slice_bitcast_fusion.9), channel_id=1, source_target_pairs={{0,2},{2,0},{4,6},{6,4},{8,10},{10,8},{12,14},{14,12},{16,18},{18,... | collective-permute-start | bytes 1572872 | tf_op jit(solution)/shard_map/ppermute | solution.py:265
  150.7 26.2 %collective-permute-start.23 = (bf16[512,512]{1,0:T(8,128)(2,1)}, bf16[512,512]{1,0:T(8,128)(2,1)}, u32[]{:S(2)}, u32[]{:S(2)}) collective-permute-start(bf16[512,512]{1,0:T(8,128)(2,1)} %dynamic-slice_bitcast_fusion.8), channel_id=1, source_target_pairs={{0,4},{2,6},{4,0},{6,2},{8,12},{10,14},{12,8},{14,10},{16,20},{18,... | collective-permute-start | bytes 1572872 | tf_op jit(solution)/shard_map/ppermute | solution.py:265
  153.3 20.6 %collective-permute-start.9 = (bf16[512,512]{1,0:T(8,128)(2,1)}, bf16[512,512]{1,0:T(8,128)(2,1)}, u32[]{:S(2)}, u32[]{:S(2)}) collective-permute-start(bf16[512,512]{1,0:T(8,128)(2,1)} %dynamic-slice_bitcast_fusion.11), channel_id=1, source_target_pairs={{0,2},{2,0},{4,6},{6,4},{8,10},{10,8},{12,14},{14,12},{16,18},{18,... | collective-permute-start | bytes 1572872 | tf_op jit(solution)/shard_map/ppermute | solution.py:265
  163.3 16.6 %collective-permute-start.11 = (bf16[512,512]{1,0:T(8,128)(2,1)}, bf16[512,512]{1,0:T(8,128)(2,1)S(1)}, u32[]{:S(2)}, u32[]{:S(2)}) collective-permute-start(bf16[512,512]{1,0:T(8,128)(2,1)} %dynamic-slice_bitcast_fusion.10), channel_id=1, source_target_pairs={{0,4},{2,6},{4,0},{6,2},{8,12},{10,14},{12,8},{14,10},{16,20},{18,... | collective-permute-start | bytes 1572872 | tf_op jit(solution)/shard_map/ppermute | solution.py:265
  173.9 15.0 %collective-permute-start.73 = (bf16[512,512]{1,0:T(8,128)(2,1)}, bf16[512,512]{1,0:T(8,128)(2,1)S(1)}, u32[]{:S(2)}, u32[]{:S(2)}) collective-permute-start(bf16[512,512]{1,0:T(8,128)(2,1)} %dynamic-slice_bitcast_fusion.1), channel_id=1, source_target_pairs={{0,2},{2,0},{4,6},{6,4},{8,10},{10,8},{12,14},{14,12},{16,18},{18,... | collective-permute-start | bytes 1572872 | tf_op jit(solution)/shard_map/ppermute | solution.py:265
  177.0 14.5 %collective-permute-start.75 = (bf16[512,512]{1,0:T(8,128)(2,1)}, bf16[512,512]{1,0:T(8,128)(2,1)S(1)}, u32[]{:S(2)}, u32[]{:S(2)}) collective-permute-start(bf16[512,512]{1,0:T(8,128)(2,1)} %dynamic-slice_bitcast_fusion), channel_id=1, source_target_pairs={{0,4},{2,6},{4,0},{6,2},{8,12},{10,14},{12,8},{14,10},{16,20},{18,... | collective-permute-start | bytes 1572872 | tf_op jit(solution)/shard_map/ppermute | solution.py:265
  179.9 20.2 %collective-permute-start.61 = (bf16[512,512]{1,0:T(8,128)(2,1)S(1)}, bf16[512,512]{1,0:T(8,128)(2,1)S(1)}, u32[]{:S(2)}, u32[]{:S(2)}) collective-permute-start(bf16[512,512]{1,0:T(8,128)(2,1)S(1)} %copy-done.102), channel_id=1, source_target_pairs={{0,2},{2,0},{4,6},{6,4},{8,10},{10,8},{12,14},{14,12},{16,18},{18,... | collective-permute-start | bytes 1572872 | tf_op jit(solution)/shard_map/ppermute | solution.py:265
  188.9 13.8 %collective-permute-start.63 = (bf16[512,512]{1,0:T(8,128)(2,1)S(1)}, bf16[512,512]{1,0:T(8,128)(2,1)S(1)}, u32[]{:S(2)}, u32[]{:S(2)}) collective-permute-start(bf16[512,512]{1,0:T(8,128)(2,1)S(1)} %copy-done.100), channel_id=1, source_target_pairs={{0,4},{2,6},{4,0},{6,2},{8,12},{10,14},{12,8},{14,10},{16,20},{18,... | collective-permute-start | bytes 1572872 | tf_op jit(solution)/shard_map/ppermute | solution.py:265
  191.4 19.9 %collective-permute-start.49 = (bf16[512,512]{1,0:T(8,128)(2,1)S(1)}, bf16[512,512]{1,0:T(8,128)(2,1)S(1)}, u32[]{:S(2)}, u32[]{:S(2)}) collective-permute-start(bf16[512,512]{1,0:T(8,128)(2,1)S(1)} %copy-done.101), channel_id=1, source_target_pairs={{0,2},{2,0},{4,6},{6,4},{8,10},{10,8},{12,14},{14,12},{16,18},{18,... | collective-permute-start | bytes 1572872 | tf_op jit(solution)/shard_map/ppermute | solution.py:265
  200.1 13.8 %collective-permute-start.51 = (bf16[512,512]{1,0:T(8,128)(2,1)S(1)}, bf16[512,512]{1,0:T(8,128)(2,1)S(1)}, u32[]{:S(2)}, u32[]{:S(2)}) collective-permute-start(bf16[512,512]{1,0:T(8,128)(2,1)S(1)} %copy-done.99), channel_id=1, source_target_pairs={{0,4},{2,6},{4,0},{6,2},{8,12},{10,14},{12,8},{14,10},{16,20},{18,... | collective-permute-start | bytes 1572872 | tf_op jit(solution)/shard_map/ppermute | solution.py:265
  202.7 18.7 %collective-permute-start.37 = (bf16[512,512]{1,0:T(8,128)(2,1)S(1)}, bf16[512,512]{1,0:T(8,128)(2,1)S(1)}, u32[]{:S(2)}, u32[]{:S(2)}) collective-permute-start(bf16[512,512]{1,0:T(8,128)(2,1)S(1)} %copy-done.98), channel_id=1, source_target_pairs={{0,2},{2,0},{4,6},{6,4},{8,10},{10,8},{12,14},{14,12},{16,18},{18,... | collective-permute-start | bytes 1572872 | tf_op jit(solution)/shard_map/ppermute | solution.py:265
  211.4 14.9 %collective-permute-start.39 = (bf16[512,512]{1,0:T(8,128)(2,1)S(1)}, bf16[512,512]{1,0:T(8,128)(2,1)S(1)}, u32[]{:S(2)}, u32[]{:S(2)}) collective-permute-start(bf16[512,512]{1,0:T(8,128)(2,1)S(1)} %copy-done.97), channel_id=1, source_target_pairs={{0,4},{2,6},{4,0},{6,2},{8,12},{10,14},{12,8},{14,10},{16,20},{18,... | collective-permute-start | bytes 1572872 | tf_op jit(solution)/shard_map/ppermute | solution.py:265
  213.9 17.9 %collective-permute-start.22 = (bf16[256,512]{1,0:T(8,128)(2,1)S(1)}, bf16[256,512]{1,0:T(8,128)(2,1)S(1)}, u32[]{:S(2)}, u32[]{:S(2)}) collective-permute-start(bf16[256,512]{1,0:T(8,128)(2,1)S(1)} %constant_dynamic-slice_fusion.9), channel_id=1, source_target_pairs={{0,4},{2,6},{4,0},{6,2},{8,12},{10,14},{12,8},{14,10},{16,20},{18,... | collective-permute-start | bytes 786440 | tf_op jit(solution)/shard_map/ppermute | solution.py:265
  221.4 15.5 %collective-permute-start.24 = (bf16[256,512]{1,0:T(8,128)(2,1)S(1)}, bf16[256,512]{1,0:T(8,128)(2,1)S(1)}, u32[]{:S(2)}, u32[]{:S(2)}) collective-permute-start(bf16[256,512]{1,0:T(8,128)(2,1)S(1)} %constant_dynamic-slice_fusion.8), channel_id=1, source_target_pairs={{0,2},{2,0},{4,6},{6,4},{8,10},{10,8},{12,14},{14,12},{16,18},{18,... | collective-permute-start | bytes 786440 | tf_op jit(solution)/shard_map/ppermute | solution.py:265
  239.4 10.4 %collective-permute-start.62 = (bf16[256,512]{1,0:T(8,128)(2,1)S(1)}, bf16[256,512]{1,0:T(8,128)(2,1)S(1)}, u32[]{:S(2)}, u32[]{:S(2)}) collective-permute-start(bf16[256,512]{1,0:T(8,128)(2,1)S(1)} %constant_dynamic-slice_fusion.3), channel_id=1, source_target_pairs={{0,4},{2,6},{4,0},{6,2},{8,12},{10,14},{12,8},{14,10},{16,20},{18,... | collective-permute-start | bytes 786440 | tf_op jit(solution)/shard_map/ppermute | solution.py:265
  261.8 10.2 %collective-permute-start.77 = (bf16[2,64,512]{2,1,0:T(8,128)(2,1)S(1)}, bf16[2,64,512]{2,1,0:T(8,128)(2,1)S(1)}, u32[]{:S(2)}, u32[]{:S(2)}) collective-permute-start(bf16[2,64,512]{2,1,0:T(8,128)(2,1)S(1)} %fusion.70), channel_id=1, source_target_pairs={{0,8},{2,10},{4,12},{6,14},{8,16},{10,18},{12,20},{14,22},{16,24},... | collective-permute-start | bytes 393224 | tf_op jit(solution)/shard_map/ppermute | solution.py:265
  274.9 15.8 %collective-permute-start.26 = (bf16[2,64,512]{2,1,0:T(8,128)(2,1)}, bf16[2,64,512]{2,1,0:T(8,128)(2,1)}, u32[]{:S(2)}, u32[]{:S(2)}) collective-permute-start(bf16[2,64,512]{2,1,0:T(8,128)(2,1)} %add_convert_fusion.27), channel_id=1, source_target_pairs={{0,8},{2,10},{4,12},{6,14},{8,16},{10,18},{12,20},{14,22},{16,24},... | collective-permute-start | bytes 393224 | tf_op jit(solution)/shard_map/ppermute | solution.py:265
  277.7 16.1 %collective-permute-start.14 = (bf16[2,64,512]{2,1,0:T(8,128)(2,1)}, bf16[2,64,512]{2,1,0:T(8,128)(2,1)}, u32[]{:S(2)}, u32[]{:S(2)}) collective-permute-start(bf16[2,64,512]{2,1,0:T(8,128)(2,1)} %add_convert_fusion.30), channel_id=1, source_target_pairs={{0,8},{2,10},{4,12},{6,14},{8,16},{10,18},{12,20},{14,22},{16,24},... | collective-permute-start | bytes 393224 | tf_op jit(solution)/shard_map/ppermute | solution.py:265
  280.5 14.4 %collective-permute-start.78 = (bf16[2,64,512]{2,1,0:T(8,128)(2,1)}, bf16[2,64,512]{2,1,0:T(8,128)(2,1)}, u32[]{:S(2)}, u32[]{:S(2)}) collective-permute-start(bf16[2,64,512]{2,1,0:T(8,128)(2,1)} %add_convert_fusion.15), channel_id=1, source_target_pairs={{0,8},{2,10},{4,12},{6,14},{8,16},{10,18},{12,20},{14,22},{16,24},... | collective-permute-start | bytes 393224 | tf_op jit(solution)/shard_map/ppermute | solution.py:265
  280.5 16.7 %collective-permute-start.66 = (bf16[2,64,512]{2,1,0:T(8,128)(2,1)}, bf16[2,64,512]{2,1,0:T(8,128)(2,1)}, u32[]{:S(2)}, u32[]{:S(2)}) collective-permute-start(bf16[2,64,512]{2,1,0:T(8,128)(2,1)} %add_convert_fusion.18), channel_id=1, source_target_pairs={{0,8},{2,10},{4,12},{6,14},{8,16},{10,18},{12,20},{14,22},{16,24},... | collective-permute-start | bytes 393224 | tf_op jit(solution)/shard_map/ppermute | solution.py:265
  283.9 19.1 %collective-permute-start.54 = (bf16[2,64,512]{2,1,0:T(8,128)(2,1)}, bf16[2,64,512]{2,1,0:T(8,128)(2,1)}, u32[]{:S(2)}, u32[]{:S(2)}) collective-permute-start(bf16[2,64,512]{2,1,0:T(8,128)(2,1)} %add_convert_fusion.21), channel_id=1, source_target_pairs={{0,8},{2,10},{4,12},{6,14},{8,16},{10,18},{12,20},{14,22},{16,24},... | collective-permute-start | bytes 393224 | tf_op jit(solution)/shard_map/ppermute | solution.py:265
  290.7 18.5 %collective-permute-start.42 = (bf16[2,64,512]{2,1,0:T(8,128)(2,1)S(1)}, bf16[2,64,512]{2,1,0:T(8,128)(2,1)S(1)}, u32[]{:S(2)}, u32[]{:S(2)}) collective-permute-start(bf16[2,64,512]{2,1,0:T(8,128)(2,1)S(1)} %add_convert_fusion.24), channel_id=1, source_target_pairs={{0,8},{2,10},{4,12},{6,14},{8,16},{10,18},{12,20},{14,22},{16,24},... | collective-permute-start | bytes 393224 | tf_op jit(solution)/shard_map/ppermute | solution.py:265
  294.9 20.3 %collective-permute-start.27 = (bf16[2,64,512]{2,1,0:T(8,128)(2,1)S(1)}, bf16[2,64,512]{2,1,0:T(8,128)(2,1)S(1)}, u32[]{:S(2)}, u32[]{:S(2)}) collective-permute-start(bf16[2,64,512]{2,1,0:T(8,128)(2,1)S(1)} %add_convert_fusion.26), channel_id=1, source_target_pairs={{0,8},{2,10},{4,12},{6,14},{8,16},{10,18},{12,20},{14,22},{16,24},... | collective-permute-start | bytes 393224 | tf_op jit(solution)/shard_map/ppermute | solution.py:265
  295.9 19.6 %collective-permute-start.15 = (bf16[2,64,512]{2,1,0:T(8,128)(2,1)S(1)}, bf16[2,64,512]{2,1,0:T(8,128)(2,1)S(1)}, u32[]{:S(2)}, u32[]{:S(2)}) collective-permute-start(bf16[2,64,512]{2,1,0:T(8,128)(2,1)S(1)} %add_convert_fusion.29), channel_id=1, source_target_pairs={{0,8},{2,10},{4,12},{6,14},{8,16},{10,18},{12,20},{14,22},{16,24},... | collective-permute-start | bytes 393224 | tf_op jit(solution)/shard_map/ppermute | solution.py:265
  301.2 17.6 %collective-permute-start.79 = (bf16[2,64,512]{2,1,0:T(8,128)(2,1)S(1)}, bf16[2,64,512]{2,1,0:T(8,128)(2,1)S(1)}, u32[]{:S(2)}, u32[]{:S(2)}) collective-permute-start(bf16[2,64,512]{2,1,0:T(8,128)(2,1)S(1)} %add_convert_fusion.14), channel_id=1, source_target_pairs={{0,8},{2,10},{4,12},{6,14},{8,16},{10,18},{12,20},{14,22},{16,24},... | collective-permute-start | bytes 393224 | tf_op jit(solution)/shard_map/ppermute | solution.py:265
  307.0 12.9 %collective-permute-start.67 = (bf16[2,64,512]{2,1,0:T(8,128)(2,1)S(1)}, bf16[2,64,512]{2,1,0:T(8,128)(2,1)S(1)}, u32[]{:S(2)}, u32[]{:S(2)}) collective-permute-start(bf16[2,64,512]{2,1,0:T(8,128)(2,1)S(1)} %add_convert_fusion.17), channel_id=1, source_target_pairs={{0,8},{2,10},{4,12},{6,14},{8,16},{10,18},{12,20},{14,22},{16,24},... | collective-permute-start | bytes 393224 | tf_op jit(solution)/shard_map/ppermute | solution.py:265
  315.2 10.1 %collective-permute-start.43 = (bf16[2,64,512]{2,1,0:T(8,128)(2,1)S(1)}, bf16[2,64,512]{2,1,0:T(8,128)(2,1)S(1)}, u32[]{:S(2)}, u32[]{:S(2)}) collective-permute-start(bf16[2,64,512]{2,1,0:T(8,128)(2,1)S(1)} %add_convert_fusion.23), channel_id=1, source_target_pairs={{0,8},{2,10},{4,12},{6,14},{8,16},{10,18},{12,20},{14,22},{16,24},... | collective-permute-start | bytes 393224 | tf_op jit(solution)/shard_map/ppermute | solution.py:265
  315.5 38.3 %collective-permute-start.8 = (f32[8704]{0:T(1024)S(1)}, f32[8704]{0:T(1024)S(1)}, u32[]{:S(2)}, u32[]{:S(2)}) collective-permute-start(f32[8704]{0:T(1024)S(1)} %add.859), channel_id=1, source_target_pairs={{0,16},{2,18},{4,20},{6,22},{8,24},{10,26},{12,28},{14,30},{16,0},... | collective-permute-start | bytes 104456 | tf_op jit(solution)/shard_map/ppermute | solution.py:310
  318.9 34.9 %collective-permute-start.28 = (bf16[2,64,512]{2,1,0:T(8,128)(2,1)S(1)}, bf16[2,64,512]{2,1,0:T(8,128)(2,1)}, u32[]{:S(2)}, u32[]{:S(2)}) collective-permute-start(bf16[2,64,512]{2,1,0:T(8,128)(2,1)S(1)} %add_convert_fusion.25), channel_id=1, source_target_pairs={{0,8},{2,10},{4,12},{6,14},{8,16},{10,18},{12,20},{14,22},{16,24},... | collective-permute-start | bytes 393224 | tf_op jit(solution)/shard_map/ppermute | solution.py:280
  319.9 34.0 %collective-permute-start.16 = (bf16[2,64,512]{2,1,0:T(8,128)(2,1)S(1)}, bf16[2,64,512]{2,1,0:T(8,128)(2,1)}, u32[]{:S(2)}, u32[]{:S(2)}) collective-permute-start(bf16[2,64,512]{2,1,0:T(8,128)(2,1)S(1)} %add_convert_fusion.28), channel_id=1, source_target_pairs={{0,8},{2,10},{4,12},{6,14},{8,16},{10,18},{12,20},{14,22},{16,24},... | collective-permute-start | bytes 393224 | tf_op jit(solution)/shard_map/ppermute | solution.py:280
  322.5 31.5 %collective-permute-start.80 = (bf16[2,64,512]{2,1,0:T(8,128)(2,1)S(1)}, bf16[2,64,512]{2,1,0:T(8,128)(2,1)}, u32[]{:S(2)}, u32[]{:S(2)}) collective-permute-start(bf16[2,64,512]{2,1,0:T(8,128)(2,1)S(1)} %add_convert_fusion.13), channel_id=1, source_target_pairs={{0,8},{2,10},{4,12},{6,14},{8,16},{10,18},{12,20},{14,22},{16,24},... | collective-permute-start | bytes 393224 | tf_op jit(solution)/shard_map/ppermute | solution.py:280
  325.3 36.1 %collective-permute-start.68 = (bf16[2,64,512]{2,1,0:T(8,128)(2,1)}, bf16[2,64,512]{2,1,0:T(8,128)(2,1)}, u32[]{:S(2)}, u32[]{:S(2)}) collective-permute-start(bf16[2,64,512]{2,1,0:T(8,128)(2,1)} %add_convert_fusion.16), channel_id=1, source_target_pairs={{0,8},{2,10},{4,12},{6,14},{8,16},{10,18},{12,20},{14,22},{16,24},... | collective-permute-start | bytes 393224 | tf_op jit(solution)/shard_map/ppermute | solution.py:280
  353.9 9.7 %collective-permute-start.29 = (bf16[2,64,512]{2,1,0:T(8,128)(2,1)}, bf16[2,64,512]{2,1,0:T(8,128)(2,1)}, u32[]{:S(2)}, u32[]{:S(2)}) collective-permute-start(bf16[2,64,512]{2,1,0:T(8,128)(2,1)} %collective-permute-done.28), channel_id=1, source_target_pairs={{0,8},{2,10},{4,12},{6,14},{8,16},{10,18},{12,20},{14,22},{16,24},... | collective-permute-start | bytes 393224 | tf_op jit(solution)/shard_map/ppermute | solution.py:280
  354.4 11.9 %collective-permute-start.17 = (bf16[2,64,512]{2,1,0:T(8,128)(2,1)}, bf16[2,64,512]{2,1,0:T(8,128)(2,1)}, u32[]{:S(2)}, u32[]{:S(2)}) collective-permute-start(bf16[2,64,512]{2,1,0:T(8,128)(2,1)} %collective-permute-done.16), channel_id=1, source_target_pairs={{0,8},{2,10},{4,12},{6,14},{8,16},{10,18},{12,20},{14,22},{16,24},... | collective-permute-start | bytes 393224 | tf_op jit(solution)/shard_map/ppermute | solution.py:280
  371.1 9.8 %collective-permute-start.70 = (bf16[2,64,512]{2,1,0:T(8,128)(2,1)S(1)}, bf16[2,64,512]{2,1,0:T(8,128)(2,1)S(1)}, u32[]{:S(2)}, u32[]{:S(2)}) collective-permute-start(bf16[2,64,512]{2,1,0:T(8,128)(2,1)S(1)} %collective-permute-done.69), channel_id=1, source_target_pairs={{0,8},{2,10},{4,12},{6,14},{8,16},{10,18},{12,20},{14,22},{16,24},... | collective-permute-start | bytes 393224 | tf_op jit(solution)/shard_map/ppermute | solution.py:280
  372.6 10.3 %collective-permute-start.58 = (bf16[2,64,512]{2,1,0:T(8,128)(2,1)S(1)}, bf16[2,64,512]{2,1,0:T(8,128)(2,1)S(1)}, u32[]{:S(2)}, u32[]{:S(2)}) collective-permute-start(bf16[2,64,512]{2,1,0:T(8,128)(2,1)S(1)} %collective-permute-done.57), channel_id=1, source_target_pairs={{0,8},{2,10},{4,12},{6,14},{8,16},{10,18},{12,20},{14,22},{16,24},... | collective-permute-start | bytes 393224 | tf_op jit(solution)/shard_map/ppermute | solution.py:280
  373.9 11.3 %collective-permute-start.46 = (bf16[2,64,512]{2,1,0:T(8,128)(2,1)S(1)}, bf16[2,64,512]{2,1,0:T(8,128)(2,1)S(1)}, u32[]{:S(2)}, u32[]{:S(2)}) collective-permute-start(bf16[2,64,512]{2,1,0:T(8,128)(2,1)S(1)} %collective-permute-done.45), channel_id=1, source_target_pairs={{0,8},{2,10},{4,12},{6,14},{8,16},{10,18},{12,20},{14,22},{16,24},... | collective-permute-start | bytes 393224 | tf_op jit(solution)/shard_map/ppermute | solution.py:280
  376.0 11.5 %collective-permute-start.31 = (bf16[256,512]{1,0:T(8,128)(2,1)S(1)}, bf16[256,512]{1,0:T(8,128)(2,1)S(1)}, u32[]{:S(2)}, u32[]{:S(2)}) collective-permute-start(bf16[256,512]{1,0:T(8,128)(2,1)S(1)} %get-tuple-element.181), channel_id=1, source_target_pairs={{0,4},{2,6},{4,0},{6,2},{8,12},{10,14},{12,8},{14,10},{16,20},{18,... | collective-permute-start | bytes 786440 | tf_op jit(solution)/shard_map/ppermute | solution.py:280
  379.1 9.7 %collective-permute-start.35 = (bf16[256,512]{1,0:T(8,128)(2,1)S(1)}, bf16[256,512]{1,0:T(8,128)(2,1)S(1)}, u32[]{:S(2)}, u32[]{:S(2)}) collective-permute-start(bf16[256,512]{1,0:T(8,128)(2,1)S(1)} %get-tuple-element.182), channel_id=1, source_target_pairs={{0,2},{2,0},{4,6},{6,4},{8,10},{10,8},{12,14},{14,12},{16,18},{18,... | collective-permute-start | bytes 786440 | tf_op jit(solution)/shard_map/ppermute | solution.py:280
  383.0 11.1 %collective-permute-start.33 = (bf16[256,512]{1,0:T(8,128)(2,1)S(1)}, bf16[256,512]{1,0:T(8,128)(2,1)S(1)}, u32[]{:S(2)}, u32[]{:S(2)}) collective-permute-start(bf16[256,512]{1,0:T(8,128)(2,1)S(1)} %get-tuple-element.178), channel_id=1, source_target_pairs={{0,2},{2,0},{4,6},{6,4},{8,10},{10,8},{12,14},{14,12},{16,18},{18,... | collective-permute-start | bytes 786440 | tf_op jit(solution)/shard_map/ppermute | solution.py:280
  385.2 14.4 %collective-permute-start.91 = (bf16[256,512]{1,0:T(8,128)(2,1)S(1)}, bf16[256,512]{1,0:T(8,128)(2,1)S(1)}, u32[]{:S(2)}, u32[]{:S(2)}) collective-permute-start(bf16[256,512]{1,0:T(8,128)(2,1)S(1)} %get-tuple-element.157), channel_id=1, source_target_pairs={{0,2},{2,0},{4,6},{6,4},{8,10},{10,8},{12,14},{14,12},{16,18},{18,... | collective-permute-start | bytes 786440 | tf_op jit(solution)/shard_map/ppermute | solution.py:280
  387.5 12.5 %collective-permute-start.83 = (bf16[256,512]{1,0:T(8,128)(2,1)S(1)}, bf16[256,512]{1,0:T(8,128)(2,1)S(1)}, u32[]{:S(2)}, u32[]{:S(2)}) collective-permute-start(bf16[256,512]{1,0:T(8,128)(2,1)S(1)} %get-tuple-element.158), channel_id=1, source_target_pairs={{0,4},{2,6},{4,0},{6,2},{8,12},{10,14},{12,8},{14,10},{16,20},{18,... | collective-permute-start | bytes 786440 | tf_op jit(solution)/shard_map/ppermute | solution.py:280
  388.8 16.4 %collective-permute-start.89 = (bf16[256,512]{1,0:T(8,128)(2,1)S(1)}, bf16[256,512]{1,0:T(8,128)(2,1)S(1)}, u32[]{:S(2)}, u32[]{:S(2)}) collective-permute-start(bf16[256,512]{1,0:T(8,128)(2,1)S(1)} %get-tuple-element.153), channel_id=1, source_target_pairs={{0,2},{2,0},{4,6},{6,4},{8,10},{10,8},{12,14},{14,12},{16,18},{18,... | collective-permute-start | bytes 786440 | tf_op jit(solution)/shard_map/ppermute | solution.py:280
  390.4 15.2 %collective-permute-start.71 = (bf16[256,512]{1,0:T(8,128)(2,1)S(1)}, bf16[256,512]{1,0:T(8,128)(2,1)S(1)}, u32[]{:S(2)}, u32[]{:S(2)}) collective-permute-start(bf16[256,512]{1,0:T(8,128)(2,1)S(1)} %get-tuple-element.154), channel_id=1, source_target_pairs={{0,4},{2,6},{4,0},{6,2},{8,12},{10,14},{12,8},{14,10},{16,20},{18,... | collective-permute-start | bytes 786440 | tf_op jit(solution)/shard_map/ppermute | solution.py:280
  394.0 16.9 %collective-permute-start.87 = (bf16[256,512]{1,0:T(8,128)(2,1)S(1)}, bf16[256,512]{1,0:T(8,128)(2,1)S(1)}, u32[]{:S(2)}, u32[]{:S(2)}) collective-permute-start(bf16[256,512]{1,0:T(8,128)(2,1)S(1)} %get-tuple-element.149), channel_id=1, source_target_pairs={{0,2},{2,0},{4,6},{6,4},{8,10},{10,8},{12,14},{14,12},{16,18},{18,... | collective-permute-start | bytes 786440 | tf_op jit(solution)/shard_map/ppermute | solution.py:280
  399.6 11.6 %collective-permute-start.59 = (bf16[256,512]{1,0:T(8,128)(2,1)S(1)}, bf16[256,512]{1,0:T(8,128)(2,1)S(1)}, u32[]{:S(2)}, u32[]{:S(2)}) collective-permute-start(bf16[256,512]{1,0:T(8,128)(2,1)S(1)} %get-tuple-element.150), channel_id=1, source_target_pairs={{0,4},{2,6},{4,0},{6,2},{8,12},{10,14},{12,8},{14,10},{16,20},{18,... | collective-permute-start | bytes 786440 | tf_op jit(solution)/shard_map/ppermute | solution.py:280
  400.0 16.5 %collective-permute-start.85 = (bf16[256,512]{1,0:T(8,128)(2,1)S(1)}, bf16[256,512]{1,0:T(8,128)(2,1)S(1)}, u32[]{:S(2)}, u32[]{:S(2)}) collective-permute-start(bf16[256,512]{1,0:T(8,128)(2,1)S(1)} %get-tuple-element.145), channel_id=1, source_target_pairs={{0,2},{2,0},{4,6},{6,4},{8,10},{10,8},{12,14},{14,12},{16,18},{18,... | collective-permute-start | bytes 786440 | tf_op jit(solution)/shard_map/ppermute | solution.py:280
  405.3 11.8 %collective-permute-start.47 = (bf16[256,512]{1,0:T(8,128)(2,1)S(1)}, bf16[256,512]{1,0:T(8,128)(2,1)S(1)}, u32[]{:S(2)}, u32[]{:S(2)}) collective-permute-start(bf16[256,512]{1,0:T(8,128)(2,1)S(1)} %get-tuple-element.146), channel_id=1, source_target_pairs={{0,4},{2,6},{4,0},{6,2},{8,12},{10,14},{12,8},{14,10},{16,20},{18,... | collective-permute-start | bytes 786440 | tf_op jit(solution)/shard_map/ppermute | solution.py:280
  405.6 17.3 %collective-permute-start.36 = (bf16[512,512]{1,0:T(8,128)(2,1)S(1)}, bf16[512,512]{1,0:T(8,128)(2,1)S(1)}, u32[]{:S(2)}, u32[]{:S(2)}) collective-permute-start(bf16[512,512]{1,0:T(8,128)(2,1)S(1)} %pad_maximum_fusion.17), channel_id=1, source_target_pairs={{0,4},{2,6},{4,0},{6,2},{8,12},{10,14},{12,8},{14,10},{16,20},{18,... | collective-permute-start | bytes 1572872 | tf_op jit(solution)/shard_map/ppermute | solution.py:280
  410.9 19.4 %collective-permute-start.34 = (bf16[512,512]{1,0:T(8,128)(2,1)}, bf16[512,512]{1,0:T(8,128)(2,1)}, u32[]{:S(2)}, u32[]{:S(2)}) collective-permute-start(bf16[512,512]{1,0:T(8,128)(2,1)} %pad_maximum_fusion.16), channel_id=1, source_target_pairs={{0,4},{2,6},{4,0},{6,2},{8,12},{10,14},{12,8},{14,10},{16,20},{18,... | collective-permute-start | bytes 1572872 | tf_op jit(solution)/shard_map/ppermute | solution.py:280
  411.2 22.0 %collective-permute-start.32 = (bf16[512,512]{1,0:T(8,128)(2,1)}, bf16[512,512]{1,0:T(8,128)(2,1)}, u32[]{:S(2)}, u32[]{:S(2)}) collective-permute-start(bf16[512,512]{1,0:T(8,128)(2,1)} %pad_maximum_fusion.15), channel_id=1, source_target_pairs={{0,2},{2,0},{4,6},{6,4},{8,10},{10,8},{12,14},{14,12},{16,18},{18,... | collective-permute-start | bytes 1572872 | tf_op jit(solution)/shard_map/ppermute | solution.py:280
  416.5 23.8 %collective-permute-start.20 = (bf16[512,512]{1,0:T(8,128)(2,1)}, bf16[512,512]{1,0:T(8,128)(2,1)}, u32[]{:S(2)}, u32[]{:S(2)}) collective-permute-start(bf16[512,512]{1,0:T(8,128)(2,1)} %pad_maximum_fusion.13), channel_id=1, source_target_pairs={{0,2},{2,0},{4,6},{6,4},{8,10},{10,8},{12,14},{14,12},{16,18},{18,... | collective-permute-start | bytes 1572872 | tf_op jit(solution)/shard_map/ppermute | solution.py:280
  417.1 79.2 %collective-permute-start.84 = (bf16[512,512]{1,0:T(8,128)(2,1)}, bf16[512,512]{1,0:T(8,128)(2,1)}, u32[]{:S(2)}, u32[]{:S(2)}) collective-permute-start(bf16[512,512]{1,0:T(8,128)(2,1)} %pad_maximum_fusion.25), channel_id=1, source_target_pairs={{0,2},{2,0},{4,6},{6,4},{8,10},{10,8},{12,14},{14,12},{16,18},{18,... | collective-permute-start | bytes 1572872 | tf_op jit(solution)/shard_map/ppermute | solution.py:280
  422.9 74.6 %collective-permute-start.72 = (bf16[512,512]{1,0:T(8,128)(2,1)}, bf16[512,512]{1,0:T(8,128)(2,1)}, u32[]{:S(2)}, u32[]{:S(2)}) collective-permute-start(bf16[512,512]{1,0:T(8,128)(2,1)} %pad_maximum_fusion.23), channel_id=1, source_target_pairs={{0,2},{2,0},{4,6},{6,4},{8,10},{10,8},{12,14},{14,12},{16,18},{18,... | collective-permute-start | bytes 1572872 | tf_op jit(solution)/shard_map/ppermute | solution.py:280
  430.3 71.7 %collective-permute-start.60 = (bf16[512,512]{1,0:T(8,128)(2,1)}, bf16[512,512]{1,0:T(8,128)(2,1)}, u32[]{:S(2)}, u32[]{:S(2)}) collective-permute-start(bf16[512,512]{1,0:T(8,128)(2,1)} %pad_maximum_fusion.21), channel_id=1, source_target_pairs={{0,2},{2,0},{4,6},{6,4},{8,10},{10,8},{12,14},{14,12},{16,18},{18,... | collective-permute-start | bytes 1572872 | tf_op jit(solution)/shard_map/ppermute | solution.py:280
  433.2 28.0 %collective-permute-start.92 = (bf16[512,512]{1,0:T(8,128)(2,1)}, bf16[512,512]{1,0:T(8,128)(2,1)}, u32[]{:S(2)}, u32[]{:S(2)}) collective-permute-start(bf16[512,512]{1,0:T(8,128)(2,1)} %pad_maximum_fusion.29), channel_id=1, source_target_pairs={{0,4},{2,6},{4,0},{6,2},{8,12},{10,14},{12,8},{14,10},{16,20},{18,... | collective-permute-start | bytes 1572872 | tf_op jit(solution)/shard_map/ppermute | solution.py:280
  440.3 24.2 %collective-permute-start.90 = (bf16[512,512]{1,0:T(8,128)(2,1)}, bf16[512,512]{1,0:T(8,128)(2,1)}, u32[]{:S(2)}, u32[]{:S(2)}) collective-permute-start(bf16[512,512]{1,0:T(8,128)(2,1)} %pad_maximum_fusion.28), channel_id=1, source_target_pairs={{0,4},{2,6},{4,0},{6,2},{8,12},{10,14},{12,8},{14,10},{16,20},{18,... | collective-permute-start | bytes 1572872 | tf_op jit(solution)/shard_map/ppermute | solution.py:280
  461.3 18.7 %collective-permute-start.88 = (bf16[512,512]{1,0:T(8,128)(2,1)}, bf16[512,512]{1,0:T(8,128)(2,1)}, u32[]{:S(2)}, u32[]{:S(2)}) collective-permute-start(bf16[512,512]{1,0:T(8,128)(2,1)} %pad_maximum_fusion.27), channel_id=1, source_target_pairs={{0,4},{2,6},{4,0},{6,2},{8,12},{10,14},{12,8},{14,10},{16,20},{18,... | collective-permute-start | bytes 1572872 | tf_op jit(solution)/shard_map/ppermute | solution.py:280
  464.6 17.4 %collective-permute-start.86 = (bf16[512,512]{1,0:T(8,128)(2,1)}, bf16[512,512]{1,0:T(8,128)(2,1)}, u32[]{:S(2)}, u32[]{:S(2)}) collective-permute-start(bf16[512,512]{1,0:T(8,128)(2,1)} %pad_maximum_fusion.26), channel_id=1, source_target_pairs={{0,4},{2,6},{4,0},{6,2},{8,12},{10,14},{12,8},{14,10},{16,20},{18,... | collective-permute-start | bytes 1572872 | tf_op jit(solution)/shard_map/ppermute | solution.py:280
  480.0 28.9 %collective-permute-start.48 = (bf16[512,512]{1,0:T(8,128)(2,1)}, bf16[512,512]{1,0:T(8,128)(2,1)}, u32[]{:S(2)}, u32[]{:S(2)}) collective-permute-start(bf16[512,512]{1,0:T(8,128)(2,1)} %pad_maximum_fusion.19), channel_id=1, source_target_pairs={{0,2},{2,0},{4,6},{6,4},{8,10},{10,8},{12,14},{14,12},{16,18},{18,... | collective-permute-start | bytes 1572872 | tf_op jit(solution)/shard_map/ppermute | solution.py:280
  (153 other events, 1552.4 us)

commit v2 on v1

v2 whole, which is shorter than its diff:
```python
import functools
import math

import jax
import jax.numpy as jnp
from jax import lax
from jax.experimental import pallas as pl
from jax.experimental.pallas import tpu as pltpu
from jax.sharding import PartitionSpec as P

HD = 64
ROT = 16
MAXLEN = 512
EPSILON = 1e-05
MASKED_SCORE = -1e30
SQRT_HALF = 0.7071067811865476
INV_ROOT_TWO_PI = 0.3989422804014327
F32 = jnp.float32
BF16 = jnp.bfloat16
PAIR = 2 * HD
QROWS = 256
HIDDEN = 256
VMEM = 56 * 1024 * 1024


def dot(lhs, rhs, contract):
    return lax.dot_general(lhs, rhs, (contract, ((), ())), preferred_element_type=F32)


NN = ((1,), (0,))
NT = ((1,), (1,))
TN = ((0,), (0,))


ANY = pl.BlockSpec(memory_space=pl.ANY)
PARAMS = pltpu.CompilerParams(vmem_limit_bytes=VMEM)


def after(kernel, inputs, held):
    def body(*refs):
        kernel(*refs[:inputs], *refs[inputs + held :])

    return body


def prep_kernel(slot_ref, own_ref, other_ref, own_cot_ref, other_cot_ref, g1_ref, b1_ref, g2_ref, b2_ref,
                normed_ref, first_ref, second_ref, cot_ref):
    def emit(x_ref, c_ref):
        x = x_ref[...].astype(F32)
        centred = x - jnp.mean(x, axis=1, keepdims=True)
        normed = centred * lax.rsqrt(jnp.mean(centred * centred, axis=1, keepdims=True) + EPSILON)
        normed_ref[...] = normed
        first_ref[...] = (normed * g1_ref[...] + b1_ref[...]).astype(BF16)
        second_ref[...] = (normed * g2_ref[...] + b2_ref[...]).astype(BF16)
        cot_ref[...] = c_ref[...]

    pl.when(pl.program_id(0) == 0)(lambda: emit(own_ref, own_cot_ref))
    pl.when(pl.program_id(0) == 1)(lambda: emit(other_ref, other_cot_ref))


def prep(own, other, own_cot, other_cot, here, gains):
    rows, width = own.shape
    block = min(rows, 256)
    count = rows // block
    mine = pl.BlockSpec((block, width), lambda j, i, slot: (jnp.where(j == 0, i, count - 1), 0))
    theirs = pl.BlockSpec((block, width), lambda j, i, slot: (jnp.where(j == 0, 0, i), 0))
    vector = pl.BlockSpec((1, width), lambda j, i, slot: (0, 0))
    out = pl.BlockSpec((block, width), lambda j, i, slot: (slot[j] * count + i, 0))
    return pl.pallas_call(
        prep_kernel,
        grid_spec=pltpu.PrefetchScalarGridSpec(
            num_scalar_prefetch=1,
            grid=(2, count),
            in_specs=[mine, theirs, mine, theirs] + [vector] * 4,
            out_specs=[out] * 4,
        ),
        out_shape=[
            jax.ShapeDtypeStruct((2 * rows, width), F32),
            jax.ShapeDtypeStruct((2 * rows, width), BF16),
            jax.ShapeDtypeStruct((2 * rows, width), BF16),
            jax.ShapeDtypeStruct((2 * rows, width), BF16),
        ],
        compiler_params=PARAMS,
        cost_estimate=pl.CostEstimate(flops=rows * width * 40, bytes_accessed=rows * width * 28, transcendentals=0),
    )(jnp.stack([here, 1 - here]), own, other, own_cot, other_cot, *[g.reshape(1, -1) for g in gains])


def ffn_kernel(second_ref, cot_ref, inner_ref, bias_ref, outer_ref, active_ref, back_ref, left_ref, right_ref, biasgrad_ref):
    second = second_ref[...]
    cot = cot_ref[...]
    preact = dot(second, inner_ref[...], NN) + bias_ref[...]
    cdf = 0.5 * (1.0 + lax.erf(preact * SQRT_HALF))
    slope = cdf + preact * jnp.exp(-0.5 * preact * preact) * INV_ROOT_TWO_PI
    active = (preact * cdf).astype(BF16)
    active_ref[...] = active
    pre_grad = dot(cot, outer_ref[...], NT) * slope
    biasgrad_ref[...] = jnp.sum(pre_grad, axis=0, keepdims=True)
    back = pre_grad.astype(BF16)
    back_ref[...] = back
    left_ref[...] = dot(second, back, TN).astype(BF16)
    outer = dot(active, cot, TN).astype(BF16)
    cols = right_ref.shape[2]
    for c in range(right_ref.shape[0]):
        right_ref[c] = outer[:, c * cols : (c + 1) * cols]


def ffn_slice(second_in, cot, inner_weight, inner_bias, outer_weight, first, count, held=()):
    rows, width = second_in.shape
    cols = count * HIDDEN
    whole = pl.BlockSpec((rows, width), lambda j: (0, 0))
    return pl.pallas_call(
        after(ffn_kernel, 5, len(held)),
        grid=(count,),
        in_specs=[
            whole,
            whole,
            pl.BlockSpec((width, HIDDEN), lambda j: (0, first + j)),
            pl.BlockSpec((1, HIDDEN), lambda j: (0, first + j)),
            pl.BlockSpec((HIDDEN, width), lambda j: (first + j, 0)),
        ]
        + [ANY] * len(held),
        out_specs=[
            pl.BlockSpec((rows, HIDDEN), lambda j: (0, j)),
            pl.BlockSpec((rows, HIDDEN), lambda j: (0, j)),
            pl.BlockSpec((width, HIDDEN), lambda j: (0, j)),
            pl.BlockSpec((width // cols, HIDDEN, cols), lambda j: (0, j, 0)),
            pl.BlockSpec((1, HIDDEN), lambda j: (0, j)),
        ],
        out_shape=[
            jax.ShapeDtypeStruct((rows, cols), BF16),
            jax.ShapeDtypeStruct((rows, cols), BF16),
            jax.ShapeDtypeStruct((width, cols), BF16),
            jax.ShapeDtypeStruct((width // cols, cols, cols), BF16),
            jax.ShapeDtypeStruct((1, cols), F32),
        ],
        compiler_params=PARAMS,
        cost_estimate=pl.CostEstimate(
            flops=8 * rows * width * cols, bytes_accessed=20 * width * cols, transcendentals=2 * rows * cols
        ),
    )(second_in, cot, inner_weight, inner_bias, outer_weight, *held)


def partner(values):
    half = ROT // 2
    lane = lax.broadcasted_iota(jnp.int32, values.shape, 1) % HD
    lanes = values.shape[1]
    return jnp.where(lane < half, pltpu.roll(values, lanes - half, 1), pltpu.roll(values, half, 1))


def attention_kernel(
    slots, first_ref, cot_ref, w_ref, wbias_ref, dense_ref, cos_ref, sin_ref, segq_ref, segk_ref,
    context_ref, back_ref, grads_ref, dense_grads_ref, biasgrad_ref, mask_ref, dk_ref, dv_ref,
):
    rows = first_ref.shape[0]
    blocks = rows // QROWS
    reach = -(-(MAXLEN - 1) // QROWS)

    @pl.when(pl.program_id(0) == 0)
    def _():
        for i in range(blocks):
            low = max(0, i - reach) * QROWS
            span = (i + 1) * QROWS - low
            seg_q = segq_ref[i * QROWS : (i + 1) * QROWS, :]
            seg_k = segk_ref[:, low : low + span]
            q_at = lax.broadcasted_iota(jnp.int32, (QROWS, span), 0) + i * QROWS
            k_at = lax.broadcasted_iota(jnp.int32, (QROWS, span), 1) + low
            allowed = ((seg_q == seg_k) & (k_at <= q_at) & (seg_q < slots)) | (k_at == q_at)
            mask_ref[i * QROWS : (i + 1) * QROWS, :span] = jnp.where(allowed, 0.0, MASKED_SCORE)

    first = first_ref[...]
    cot = cot_ref[...]
    weight = jnp.concatenate([w_ref[0], w_ref[1], w_ref[2]], axis=1)
    bias = jnp.concatenate([wbias_ref[0], wbias_ref[1], wbias_ref[2]], axis=1)
    projected = dot(first, weight, NN) + bias
    cosine = cos_ref[...]
    sine = sin_ref[...]
    q = projected[:, :PAIR]
    k = projected[:, PAIR : 2 * PAIR]
    queries = (q * cosine + partner(q) * sine).astype(BF16)
    keys = (k * cosine + partner(k) * sine).astype(BF16)
    values = projected[:, 2 * PAIR :].astype(BF16)
    context_back = dot(cot, dense_ref[...], NT).astype(BF16)

    lane_head = lax.broadcasted_iota(jnp.int32, (QROWS, PAIR), 1) // HD
    scale = HD**-0.5
    dk_ref[...] = jnp.zeros_like(dk_ref)
    dv_ref[...] = jnp.zeros_like(dv_ref)
    contexts = []
    dqs = []
    for i in range(blocks):
        low = max(0, i - reach) * QROWS
        high = (i + 1) * QROWS
        mask = mask_ref[i * QROWS : high, : high - low]
        q_block = queries[i * QROWS : high]
        b_block = context_back[i * QROWS : high]
        k_block = keys[low:high]
        v_block = values[low:high]
        ctx = None
        for h in range(2):
            mine = lane_head == h
            q_head = jnp.where(mine, q_block, jnp.zeros_like(q_block))
            b_head = jnp.where(mine, b_block, jnp.zeros_like(b_block))
            scores = dot(q_head, k_block, NT) * scale + mask
            highest = jnp.max(scores, axis=1, keepdims=True)
            exponent = jnp.exp(scores - highest)
            total = jnp.sum(exponent, axis=1, keepdims=True)
            weights = exponent * (1.0 / total)
            weights_bf = weights.astype(BF16)
            prob_grad = dot(b_head, v_block, NT)
            delta = jnp.sum(weights * prob_grad, axis=1, keepdims=True)
            score_back = (weights * (prob_grad - delta)).astype(BF16)
            ctx_head = dot(weights_bf, v_block, NN)
            dq_head = dot(score_back, k_block, NN)
            dk_ref[low:high, :] += dot(score_back, q_head, TN)
            dv_ref[low:high, :] += dot(weights_bf, b_head, TN)
            ctx = ctx_head if h == 0 else jnp.where(mine, ctx_head, ctx)
            dq = dq_head if h == 0 else jnp.where(mine, dq_head, dq)
        contexts.append(ctx.astype(BF16))
        dqs.append(dq)
    context = jnp.concatenate(contexts, axis=0)
    context_ref[...] = context
    dq = jnp.concatenate(dqs, axis=0) * scale
    dk = dk_ref[...] * scale
    dv = dv_ref[...]
    dq = dq * cosine - partner(dq) * sine
    dk = dk * cosine - partner(dk) * sine
    back = jnp.concatenate([dq, dk, dv], axis=1)
    biasgrad_ref[...] = jnp.sum(back, axis=0, keepdims=True)
    back = back.astype(BF16)
    back_ref[...] = back
    weight_grad = dot(first, back, TN).astype(BF16)
    for c in range(3):
        grads_ref[c] = weight_grad[:, c * PAIR : (c + 1) * PAIR]
    dense_grads_ref[...] = dot(context, cot, TN).astype(BF16)


def attention_pair(first_in, cot, qkv, qkv_bias, dense_weight, cosine, sine, segment, slots, at, held=()):
    rows, width = first_in.shape
    reach = -(-(MAXLEN - 1) // QROWS)
    span = min(rows, (reach + 1) * QROWS)
    whole = pl.BlockSpec((rows, width), lambda j: (0, 0))
    table = pl.BlockSpec((rows, PAIR), lambda j: (0, 0))
    return pl.pallas_call(
        after(functools.partial(attention_kernel, slots), 9, len(held)),
        grid=(1,),
        in_specs=[
            whole,
            whole,
            pl.BlockSpec((3, width, PAIR), lambda j: (0, 0, at)),
            pl.BlockSpec((3, 1, PAIR), lambda j: (0, 0, at)),
            pl.BlockSpec((PAIR, width), lambda j: (at, 0)),
            table,
            table,
            pl.BlockSpec((rows, 1), lambda j: (0, 0)),
            pl.BlockSpec((1, rows), lambda j: (0, 0)),
        ]
        + [ANY] * len(held),
        out_specs=[
            pl.BlockSpec((rows, PAIR), lambda j: (0, 0)),
            pl.BlockSpec((rows, 3 * PAIR), lambda j: (0, 0)),
            pl.BlockSpec((3, width, PAIR), lambda j: (0, 0, 0)),
            pl.BlockSpec((PAIR, width), lambda j: (0, 0)),
            pl.BlockSpec((1, 3 * PAIR), lambda j: (0, 0)),
        ],
        out_shape=[
            jax.ShapeDtypeStruct((rows, PAIR), BF16),
            jax.ShapeDtypeStruct((rows, 3 * PAIR), BF16),
            jax.ShapeDtypeStruct((3, width, PAIR), BF16),
            jax.ShapeDtypeStruct((PAIR, width), BF16),
            jax.ShapeDtypeStruct((1, 3 * PAIR), F32),
        ],
        scratch_shapes=[
            pltpu.VMEM((rows, span), F32),
            pltpu.VMEM((rows, PAIR), F32),
            pltpu.VMEM((rows, PAIR), F32),
        ],
        compiler_params=PARAMS,
        cost_estimate=pl.CostEstimate(
            flops=30 * rows * width * PAIR,
            bytes_accessed=16 * width * PAIR,
            transcendentals=2 * rows * span,
        ),
    )(first_in, cot, qkv, qkv_bias, dense_weight, cosine, sine, segment.reshape(rows, 1), segment.reshape(1, rows), *held)


def branch_kernel(contexts, actives, slot_ref, *refs):
    context = jnp.concatenate([r[...] for r in refs[:contexts]], axis=1)
    active = jnp.concatenate([r[...] for r in refs[contexts : contexts + actives]], axis=1)
    dense_ref, outer_ref, away_ref, own_ref = refs[contexts + actives :]
    branch = (dot(context, dense_ref[...], NN) + dot(active, outer_ref[...], NN)).astype(BF16)

    @pl.when(pl.program_id(0) == 0)
    def _():
        away_ref[...] = branch

    @pl.when(pl.program_id(0) == 1)
    def _():
        own_ref[...] = branch


def back_kernel(qkv_backs, pre_backs, slot_ref, *refs):
    lanes = refs[:qkv_backs]
    pre_back = jnp.concatenate([r[...] for r in refs[qkv_backs : qkv_backs + pre_backs]], axis=1)
    qkv_ref, inner_ref, g1_ref, g2_ref, normed_ref, away_ref, own_ref, sums_ref = refs[qkv_backs + pre_backs :]
    first = None
    for c in range(3):
        part = jnp.concatenate([r[:, c * PAIR : (c + 1) * PAIR] for r in lanes], axis=1)
        term = dot(part, qkv_ref[c], NT)
        first = term if first is None else first + term
    second = dot(pre_back, inner_ref[...], NT)
    combined = first * g1_ref[...] + second * g2_ref[...]
    normed = normed_ref[...]
    sums = jnp.concatenate(
        [jnp.sum(v, axis=0, keepdims=True) for v in (first * normed, first, second * normed, second)], axis=0
    )

    @pl.when((pl.program_id(0) == 0) & (pl.program_id(1) == 0))
    def _():
        sums_ref[...] = jnp.zeros_like(sums_ref)

    sums_ref[...] += sums

    @pl.when(pl.program_id(0) == 0)
    def _():
        away_ref[...] = combined.astype(BF16)

    @pl.when(pl.program_id(0) == 1)
    def _():
        own_ref[...] = combined


def rows_call(kernel, here, sliced, whole, by_rows, own_type, sums, held, flops):
    rows = sliced[0].shape[0]
    width = whole[0].shape[-1] if whole[0].ndim == 2 else whole[0].shape[1]
    half = rows // 2
    block = min(half, 256)
    count = half // block
    at = lambda j, i, slot: (slot[j] * count + i, 0)
    in_specs = [pl.BlockSpec((block, v.shape[1]), at) for v in sliced]
    in_specs += [pl.BlockSpec(v.shape, lambda j, i, slot, n=v.ndim: (0,) * n) for v in whole]
    in_specs += [pl.BlockSpec((block, v.shape[1]), at) for v in by_rows]
    out_specs = [
        pl.BlockSpec((block, width), lambda j, i, slot: (jnp.where(j == 0, i, count - 1), 0)),
        pl.BlockSpec((block, width), lambda j, i, slot: (jnp.where(j == 0, 0, i), 0)),
    ]
    out_shape = [jax.ShapeDtypeStruct((half, width), BF16), jax.ShapeDtypeStruct((half, width), own_type)]
    if sums:
        out_specs.append(pl.BlockSpec((sums, width), lambda j, i, slot: (0, 0)))
        out_shape.append(jax.ShapeDtypeStruct((sums, width), F32))
    return pl.pallas_call(
        after(kernel, 1 + len(in_specs), len(held)),
        grid_spec=pltpu.PrefetchScalarGridSpec(
            num_scalar_prefetch=1, grid=(2, count), in_specs=in_specs + [ANY] * len(held), out_specs=out_specs
        ),
        out_shape=out_shape,
        compiler_params=PARAMS,
        cost_estimate=pl.CostEstimate(flops=flops, bytes_accessed=16 * rows * width, transcendentals=0),
    )(jnp.stack([1 - here, here]), *sliced, *whole, *by_rows, *held)


def rings(size):
    fast = 2 if size % 2 == 0 else 1
    mid = 4 if size % 32 == 0 else 2 if size % 4 == 0 else 1
    return [(fast * mid, size // (fast * mid)), (fast, mid), (1, fast)]


def position(ring):
    return lax.axis_index("dp") // ring[0] % ring[1]


def hop(values, size, ring):
    stride, length = ring
    pairs = [(i, i + ((i // stride + 1) % length - i // stride % length) * stride) for i in range(size)]
    return lax.ppermute(values, "dp", pairs)


def rows_of(values, index, length):
    rows = values.shape[0] // length
    return lax.dynamic_slice_in_dim(values, index * rows, rows, 0)


def add(came, own):
    return (came.astype(F32) + own.astype(F32)).astype(BF16)


def ring_reduce(values, size, ring):
    length = ring[1]
    if length == 1:
        return values
    at = position(ring)
    held = rows_of(values, (at + length - 1) % length, length)
    for step in range(length - 1):
        yield [held]
        came = hop(held, size, ring)
        held = add(came, rows_of(values, (at + 2 * length - 2 - step) % length, length))
    return held


def ring_pieces(held, size, ring):
    pieces = [held]
    for _ in range(ring[1] - 1):
        yield [pieces[-1]]
        pieces.append(hop(pieces[-1], size, ring))
    return pieces


def slots_of(ring):
    at = position(ring)
    return [(at + ring[1] - back) % ring[1] for back in range(ring[1])]


def join(pieces, ring):
    slots = slots_of(ring)
    ordered = []
    for slot in range(ring[1]):
        chosen = pieces[0]
        for back in range(1, ring[1]):
            chosen = jnp.where(slots[back] == slot, pieces[back], chosen)
        ordered.append(chosen)
    return jnp.concatenate(ordered, axis=0)


def together(one, two):
    results = [None, None]
    live = [one, two]
    while any(g is not None for g in live):
        held = []
        for k, g in enumerate(live):
            if g is None:
                continue
            try:
                held += next(g)
            except StopIteration as stop:
                results[k] = stop.value
                live[k] = None
        if held:
            yield held
    return results


def reduce_over_dp(left, right, size):
    slow, mid, fast = rings(size)
    left, right = yield from together(ring_reduce(left, size, fast), ring_reduce(right, size, mid))
    left, right = yield from together(ring_reduce(left, size, mid), ring_reduce(right, size, fast))
    both = jnp.stack([left, right])
    step = 1
    while step < slow[1]:
        yield [both]
        both = add(lax.ppermute(both, "dp", [(i, i ^ (step * slow[0])) for i in range(size)]), both)
        step *= 2
    left, right = yield from together(ring_pieces(both[0], size, mid), ring_pieces(both[1], size, fast))
    left, right = join(left, mid), join(right, fast)
    return (yield from together(ring_pieces(left, size, fast), ring_pieces(right, size, mid)))


def place_kernel(count, tile, slot_ref, *refs):
    out_ref = refs[-1]
    for k in range(count):

        @pl.when(pl.program_id(0) == k)
        def _():
            if tile:
                for t in range(refs[k].shape[0] // tile):
                    out_ref[:, t * tile : (t + 1) * tile] = refs[k][t * tile : (t + 1) * tile, :].astype(F32)
            else:
                out_ref[...] = refs[k][...].astype(F32)


def place(total, shape, pieces, ring, at, across):
    count = len(pieces)
    rows, cols = pieces[0].shape
    if across:
        out_spec = pl.BlockSpec((cols, rows), lambda j, slot: (at, slot[j]))
    else:
        out_spec = pl.BlockSpec((rows, cols), lambda j, slot: (slot[j], at))
    kernel = functools.partial(place_kernel, count, cols if across else 0)
    extra = [] if total is None else [total]
    return pl.pallas_call(
        after(kernel, 1 + count, len(extra)),
        grid_spec=pltpu.PrefetchScalarGridSpec(
            num_scalar_prefetch=1,
            grid=(count,),
            in_specs=[pl.BlockSpec((rows, cols), lambda j, slot: (0, 0))] * count + [ANY] * len(extra),
            out_specs=out_spec,
        ),
        out_shape=jax.ShapeDtypeStruct(shape, F32),
        input_output_aliases={1 + count: 0} if extra else {},
        compiler_params=PARAMS,
        cost_estimate=pl.CostEstimate(flops=0, bytes_accessed=6 * count * rows * cols, transcendentals=0),
    )(jnp.stack(slots_of(ring)), *pieces, *extra)


def butterfly(values, axis, size):
    if size & (size - 1):
        return lax.psum(values, axis)
    step = 1
    while step < size:
        values = values + lax.ppermute(values, axis, [(i, i ^ step) for i in range(size)])
        step *= 2
    return values


class Rounds:
    def __init__(self):
        self.live = []
        self.done = {}

    def add(self, name, steps):
        self.live.append((name, steps))

    def turn(self):
        held = []
        left = []
        for name, steps in self.live:
            try:
                held += next(steps)
                left.append((name, steps))
            except StopIteration as stop:
                self.done[name] = stop.value
        self.live = left
        return held


def normalize(values):
    mean_val = jnp.mean(values, axis=-1, keepdims=True)
    centred = values - mean_val
    inv_std = lax.rsqrt(jnp.mean(centred * centred, axis=-1, keepdims=True) + EPSILON)
    return (centred * inv_std, inv_std)


def layout(lengths, row_count):
    slot_count = lengths.shape[0]
    places = jnp.arange(row_count, dtype=jnp.int32)
    seq_ends = jnp.cumsum(lengths)
    seq_starts = seq_ends - lengths
    segment = jnp.sum((places[:, None] >= seq_ends[None, :]).astype(jnp.int32), axis=1)
    member = segment[:, None] == jnp.arange(slot_count, dtype=jnp.int32)[None, :]
    place = places - jnp.sum(jnp.where(member, seq_starts[None, :], 0), axis=1)
    return (segment, place)


def rotary_tables(places):
    half = ROT // 2
    lane = jnp.arange(PAIR, dtype=jnp.int32) % HD
    frequency = jnp.exp(-(2.0 * (lane % half).astype(F32) / ROT) * math.log(10000.0))
    angle = places.astype(F32)[:, None] * jnp.where(lane < ROT, frequency, 0.0)[None, :]
    sign = jnp.where(lane < half, -1.0, jnp.where(lane < ROT, 1.0, 0.0))
    return (jnp.cos(angle), jnp.sin(angle) * sign[None, :])


def local(
    dp_size,
    tensor_size,
    residual,
    norm1_gain,
    norm1_bias,
    norm2_gain,
    norm2_bias,
    qkv_weight,
    qkv_bias,
    dense_weight,
    inner_weight,
    inner_bias,
    outer_weight,
    out_bias,
    cotangent,
    seq_lengths,
):
    width = residual.shape[1]
    head_width = qkv_weight.shape[2]
    hidden = inner_weight.shape[1]
    slots = seq_lengths.shape[1]
    here = lax.axis_index("tensor")
    swap = [(0, 1), (1, 0)]

    if tensor_size == 2:
        other = lax.ppermute(residual, "tensor", swap)
        other_cot = lax.ppermute(cotangent, "tensor", swap)
        parts = (residual, other, cotangent, other_cot)
        order = here
    else:
        gathered = lax.all_gather(residual, "tensor", axis=0, tiled=True)
        gathered_cot = lax.all_gather(cotangent, "tensor", axis=0, tiled=True)
        middle = gathered.shape[0] // 2
        parts = (gathered[:middle], gathered[middle:], gathered_cot[:middle], gathered_cot[middle:])
        order = jnp.int32(0)
    normed, first_in, second_in, cot = prep(*parts, order, (norm1_gain, norm1_bias, norm2_gain, norm2_bias))
    rows = cot.shape[0]

    rounds = Rounds()
    ffn = []
    steps = hidden // HIDDEN
    per = max(1, steps // 4)

    def feed_forward():
        at = len(ffn) * per
        held = rounds.turn()
        out = ffn_slice(second_in, cot, inner_weight, inner_bias.reshape(1, -1), outer_weight, at, per, held)
        rounds.add(len(ffn), reduce_over_dp(out[2], out[3].reshape(width, per * HIDDEN), dp_size))
        ffn.append(out)

    early = (steps // per + 1) // 2
    for _ in range(early):
        feed_forward()

    lengths, late_qkv, _ = lax.optimization_barrier((seq_lengths, qkv_weight, ffn[0][4]))
    segment, places = layout(lengths[0], rows)
    cosine, sine = rotary_tables(places)
    qkv = jnp.transpose(late_qkv, (1, 0, 2))
    attn = []
    for pair in range(head_width // PAIR):
        held = rounds.turn()
        attn.append(
            attention_pair(
                first_in, cot, qkv, qkv_bias.reshape(3, 1, -1), dense_weight, cosine, sine, segment, slots, pair, held
            )
        )
    attn_sums = lax.psum(([a[2] for a in attn], [a[3] for a in attn]), "dp")
    while len(ffn) * per < steps:
        feed_forward()

    order = here if tensor_size == 2 else jnp.int32(1)
    held = rounds.turn()
    branch_away, branch_own = rows_call(
        functools.partial(branch_kernel, len(attn), len(ffn)), order, [a[0] for a in attn] + [f[0] for f in ffn],
        [dense_weight, outer_weight], [], BF16, 0, held, 2 * rows * width * (head_width + hidden),
    )
    held = rounds.turn()
    away, own, sums = rows_call(
        functools.partial(back_kernel, len(attn), len(ffn)), order, [a[1] for a in attn] + [f[1] for f in ffn],
        [qkv, inner_weight, norm1_gain.reshape(1, -1), norm2_gain.reshape(1, -1)], [normed], F32, 4, held,
        2 * rows * width * (3 * head_width + hidden),
    )
    if tensor_size == 2:
        summed = lax.ppermute(branch_away, "tensor", swap).astype(F32) + branch_own.astype(F32)
        combined = lax.ppermute(away, "tensor", swap).astype(F32) + own
    else:
        scatter = functools.partial(lax.psum_scatter, axis_name="tensor", scatter_dimension=0, tiled=True)
        summed = scatter(jnp.concatenate([branch_away, branch_own], axis=0)).astype(F32)
        combined = scatter(jnp.concatenate([away.astype(F32), own], axis=0))
    layer_out = (residual.astype(F32) + summed + out_bias).astype(BF16)
    own_normed, own_inv = normalize(residual.astype(F32))
    residual_grad = (
        cotangent.astype(F32)
        + own_inv
        * (
            combined
            - jnp.mean(combined, axis=-1, keepdims=True)
            - own_normed * jnp.mean(combined * own_normed, axis=-1, keepdims=True)
        )
    ).astype(BF16)

    over_all = jnp.concatenate([sums, jnp.sum(cotangent.astype(F32), axis=0, keepdims=True)], axis=0).reshape(-1)
    over_all = butterfly(over_all, "tensor", tensor_size)
    qkvbias = jnp.concatenate([a[4].reshape(3, PAIR) for a in attn], axis=1).reshape(-1)
    innerbias = jnp.concatenate([f[4] for f in ffn], axis=1).reshape(-1)
    vectors = butterfly(jnp.concatenate([over_all, qkvbias, innerbias]), "dp", dp_size)
    ends = [width * i for i in range(1, 6)] + [5 * width + 3 * head_width]
    gain1_grad, bias1_grad, gain2_grad, bias2_grad, outbias_grad, qkvbias_grad, innerbias_grad = jnp.split(vectors, ends)

    while rounds.live:
        rounds.turn()
    _, mid, fast = rings(dp_size)
    inner_grad = None
    outer_grad = None
    for k in range(len(ffn)):
        left, right = rounds.done[k]
        inner_grad = place(inner_grad, (width, hidden), left, fast, k, False)
        outer_grad = place(outer_grad, (hidden, width), right, mid, k, True)
    qkv_sums, dense_sums = attn_sums
    qkv_grad = jnp.concatenate([g.transpose(1, 0, 2) for g in qkv_sums], axis=2).astype(F32)
    dense_grad = jnp.concatenate(dense_sums, axis=0).astype(F32)
    return (
        layer_out,
        residual_grad,
        gain1_grad,
        bias1_grad,
        gain2_grad,
        bias2_grad,
        qkv_grad,
        qkvbias_grad.reshape(3, head_width),
        dense_grad,
        inner_grad,
        innerbias_grad,
        outer_grad,
        outbias_grad,
    )


def solution(mesh):
    rows = P(("dp", "tensor"), None)
    return jax.shard_map(
        functools.partial(local, mesh.shape["dp"], mesh.shape["tensor"]),
        mesh=mesh,
        in_specs=(
            rows,
            P(),
            P(),
            P(),
            P(),
            P(None, None, "tensor"),
            P(None, "tensor"),
            P("tensor", None),
            P(None, "tensor"),
            P("tensor"),
            P("tensor", None),
            P(),
            rows,
            P("dp", None),
        ),
        out_specs=(
            rows,
            rows,
            P(),
            P(),
            P(),
            P(),
            P(None, None, "tensor"),
            P(None, "tensor"),
            P("tensor", None),
            P(None, "tensor"),
            P("tensor"),
            P("tensor", None),
            P(),
        ),
        check_vma=False,
    )
```

time: 543 us -> 441 us (0.81)
  other arithmetic: 118 us -> 38.2 us
  Pallas kernels: 86.2 us -> 154 us
  local copies, waits for them, and re-layouts: 75.7 us -> 23.3 us
  starting transfers between devices: 94.2 us -> 53.7 us
  matrix products: 22.6 us -> 0 us
  between operations: 3.15 us -> 15.5 us
  waiting for transfers between devices: 137 us -> 149 us
    pallas_call x6 -> x19, Pallas kernels: 86.2 us -> 154 us  [the longest x4 56.2 us: attention_pair(): pl.pallas_call(after(functools.partial(attention_kernel, slots), 9, len(h...]
    ppermute x88 -> x44, waiting for transfers between devices: 101 us -> 143 us  [the longest x32 87.4 us: hop(): return lax.ppermute(values, 'dp', pairs)]
    convert_element_type x36 -> x19, other arithmetic: 54.7 us -> 14.7 us  [the longest x16 8.86 us: add(): return (came.astype(F32) + own.astype(F32)).astype(BF16)]
    ppermute x88 -> x44, starting transfers between devices: 87.9 us -> 50 us  [the longest x32 36.4 us: hop(): return lax.ppermute(values, 'dp', pairs)]
    ppermute x5, waiting for transfers between devices: 36 us -> 5.45 us  [butterfly(): lax.ppermute(values, axis, [(i, i ^ step) for i in range(size)])]
    select_n x25 -> x4, other arithmetic: 25.3 us -> 0.29 us  [join(): chosen = jnp.where(slots[back] == slot, pieces[back], chosen)]
    dot_general x4 -> x0, matrix products: 22.6 us -> none  [dot(): lax.dot_general(lhs, rhs, (contract, ((), ())), preferred_element_type=F32)]
    reshape x12 -> x2, local copies, waits for them, and re-layouts: 16.1 us -> 0.02 us  [the longest x1 0.01 us: local(): jnp.concatenate([a[4].reshape(3, PAIR) for a in attn], axis=1).reshape(-1)]
  transfers between devices with their start and end apart: 93 -> 50, of which waited for: 43 -> 16; matrix products, arithmetic and copies ran while one was open for 28% -> 10% of each run, Pallas kernels for 0% -> 30%
where the time goes in v2:
time: 441 us; the launch traced here: 433 us
  Pallas kernels  154 us (35%)
  waiting for transfers between devices  149 us (34%)
  starting transfers between devices  53.7 us (12%)
  other arithmetic  38.2 us (9%)
  local copies, waits for them, and re-layouts  23.3 us (5%)
  between operations  15.5 us (4%)
    ppermute x32, waiting for transfers between devices, hop(): return lax.ppermute(values, 'dp', pairs)  87.4 us
    pallas_call x4, Pallas kernels, attention_pair(): pl.pallas_call(after(functools.partial(attention_kernel, slots), 9, len(h...  56.2 us
    ppermute x8, waiting for transfers between devices, reduce_over_dp(): lax.ppermute(both, 'dp', [(i, i ^ step * slow[0]) for i in range(size)])  56.1 us
    ppermute x32, starting transfers between devices, hop(): return lax.ppermute(values, 'dp', pairs)  36.4 us
    pallas_call x4, Pallas kernels, ffn_slice(): pl.pallas_call(after(ffn_kernel, 5, len(held)), grid=(count,), in_specs=[...  35.7 us
    pallas_call x2, Pallas kernels, rows_call(): pl.pallas_call(after(kernel, 1 + len(in_specs), len(held)), grid_spec=plt...  27.8 us
    pallas_call x8, Pallas kernels, place(): pl.pallas_call(after(kernel, 1 + count, len(extra)), grid_spec=pltpu.Pref...  26.2 us
    dynamic_slice x16, local copies, waits for them, and re-layouts, rows_of(): return lax.dynamic_slice_in_dim(values, index * rows, rows, 0)  13.5 us
  transfers between devices with their start and end apart: 50, of which 16 were waited for; matrix products, arithmetic and copies ran while one was open for 10% of the time, Pallas kernels for 30%

profile of v2, /device:TPU:0, one launch (start us, length us, event | category | flops | bytes accessed | tf_op | source)
XLA Modules:
  0.0 433.2 jit_solution(14696889483089903765)
XLA Ops:
  10.3 1.4 convert_reduce_fusion
  11.7 1.6 fusion.7
  14.7 7.8 %shard_map.237 = (f32[1024,1024]{1,0:T(8,128)}, bf16[1024,1024]{1,0:T(8,128)(2,1)}, bf16[1024,1024]{1,0:T(8,128)(2,1)}, bf16[1024,1024]{1,0:T(8,128)(2,1)}) custom-call(s32[2]{0:T(128)} %pad_add_fusion.1.slot_ref, bf16[512,1024]{1,0:T(8,128)(2,1)} %own_ref.1, bf16[512,1024]{1,0:T(8,128)(2,1)} %copy-done.11, bf16[512,1024]{1,0:T(8,128)(2,1)} %own_cot_ref.1, ...), custom_call_target="tpu_custom_call" | custom-call | flops 20971520 | bytes 14680064 | tf_op jit(solution)/shard_map/pallas_call | solution.py:69
  22.5 8.9 %shard_map.238 = (bf16[1024,512]{1,0:T(8,128)(2,1)}, bf16[1024,512]{1,0:T(8,128)(2,1)}, bf16[1024,512]{1,0:T(8,128)(2,1)}, bf16[2,512,512]{2,1,0:T(8,128)(2,1)}, f32[1,512]{1,0:T(1,128)}) custom-call(bf16[1024,1024]{1,0:T(8,128)(2,1)} %get-tuple-element.66.refs_0_, bf16[1024,1024]{1,0:T(8,128)(2,1)} %get-tuple-element.65.refs_1_, ...), custom_call_target="tpu_custom_call" | custom-call | flops 4294967296 | bytes 10485760 | tf_op jit(solution)/shard_map/pallas_call | solution.py:111
  32.5 3.0 collective-permute-start.2
  35.5 1.9 constant_dynamic-slice_fusion.13.refs_6_
  37.4 1.5 collective-permute-start.3
  38.9 8.9 %shard_map.239 = (bf16[1024,512]{1,0:T(8,128)(2,1)}, bf16[1024,512]{1,0:T(8,128)(2,1)}, bf16[1024,512]{1,0:T(8,128)(2,1)}, bf16[2,512,512]{2,1,0:T(8,128)(2,1)}, f32[1,512]{1,0:T(1,128)}) custom-call(bf16[1024,1024]{1,0:T(8,128)(2,1)} %get-tuple-element.66.refs_0_, bf16[1024,1024]{1,0:T(8,128)(2,1)} %get-tuple-element.65.refs_1_, ...), custom_call_target="tpu_custom_call" | custom-call | flops 4294967296 | bytes 10485760 | tf_op jit(solution)/shard_map/pallas_call | solution.py:111
  48.1 1.9 constant_dynamic-slice_fusion.10.refs_12_
  50.0 1.9 constant_dynamic-slice_fusion.11.refs_11_
  53.6 3.3 fusion.12
  57.2 2.0 collective-permute-start.4
  60.4 1.6 collective-permute-start.5
  61.9 6.1 %collective-permute-done.6 = bf16[512,512]{1,0:T(8,128)(2,1)S(1)} collective-permute-done((bf16[512,512]{1,0:T(8,128)(2,1)}, bf16[512,512]{1,0:T(8,128)(2,1)S(1)}, u32[]{:S(2)}, u32[]{:S(2)}) %collective-permute-start.6) | collective-permute-done | bytes 524320 | tf_op jit(solution)/shard_map/ppermute | solution.py:374
  71.0 13.9 %shard_map.240 = (bf16[1024,128]{1,0:T(8,128)(2,1)}, bf16[1024,384]{1,0:T(8,128)(2,1)}, bf16[3,1024,128]{2,1,0:T(8,128)(2,1)}, bf16[128,1024]{1,0:T(8,128)(2,1)}, f32[1,384]{1,0:T(1,128)}) custom-call(bf16[1024,1024]{1,0:T(8,128)(2,1)} %get-tuple-element.64.refs_0_, bf16[1024,1024]{1,0:T(8,128)(2,1)} %get-tuple-element.65.refs_1_, ...), custom_call_target="tpu_custom_call" | custom-call | flops 4026531840 | bytes 2097152 | tf_op jit(solution)/shard_map/pallas_call | solution.py:243
  86.6 1.6 collective-permute-start.8
  90.8 14.3 %shard_map.241 = (bf16[1024,128]{1,0:T(8,128)(2,1)}, bf16[1024,384]{1,0:T(8,128)(2,1)}, bf16[3,1024,128]{2,1,0:T(8,128)(2,1)}, bf16[128,1024]{1,0:T(8,128)(2,1)}, f32[1,384]{1,0:T(1,128)}) custom-call(bf16[1024,1024]{1,0:T(8,128)(2,1)} %get-tuple-element.64.refs_0_, bf16[1024,1024]{1,0:T(8,128)(2,1)} %get-tuple-element.65.refs_1_, ...), custom_call_target="tpu_custom_call" | custom-call | flops 4026531840 | bytes 2097152 | tf_op jit(solution)/shard_map/pallas_call | solution.py:243
  106.0 2.7 collective-permute-start.11
  108.6 3.4 collective-permute-done.12
  112.2 2.6 collective-permute-start.15
  114.8 14.1 %shard_map.242 = (bf16[1024,128]{1,0:T(8,128)(2,1)}, bf16[1024,384]{1,0:T(8,128)(2,1)}, bf16[3,1024,128]{2,1,0:T(8,128)(2,1)}, bf16[128,1024]{1,0:T(8,128)(2,1)}, f32[1,384]{1,0:T(1,128)}) custom-call(bf16[1024,1024]{1,0:T(8,128)(2,1)} %get-tuple-element.64.refs_0_, bf16[1024,1024]{1,0:T(8,128)(2,1)} %get-tuple-element.65.refs_1_, ...), custom_call_target="tpu_custom_call" | custom-call | flops 4026531840 | bytes 2097152 | tf_op jit(solution)/shard_map/pallas_call | solution.py:243
  129.6 12.7 %collective-permute-done.11 = bf16[2,256,512]{2,1,0:T(8,128)(2,1)} collective-permute-done((bf16[2,256,512]{2,1,0:T(8,128)(2,1)S(1)}, bf16[2,256,512]{2,1,0:T(8,128)(2,1)}, u32[]{:S(2)}, u32[]{:S(2)}) %collective-permute-start.11) | collective-permute-done | bytes 524320 | tf_op jit(solution)/shard_map/ppermute | solution.py:449
  144.6 1.5 collective-permute-start.13
  146.1 4.2 collective-permute-done.15
  152.8 1.5 collective-permute-start.16
  156.1 8.8 %shard_map.244 = (bf16[1024,512]{1,0:T(8,128)(2,1)}, bf16[1024,512]{1,0:T(8,128)(2,1)}, bf16[1024,512]{1,0:T(8,128)(2,1)}, bf16[2,512,512]{2,1,0:T(8,128)(2,1)}, f32[1,512]{1,0:T(1,128)}) custom-call(bf16[1024,1024]{1,0:T(8,128)(2,1)} %get-tuple-element.66.refs_0_, bf16[1024,1024]{1,0:T(8,128)(2,1)} %get-tuple-element.65.refs_1_, ...), custom_call_target="tpu_custom_call" | custom-call | flops 4294967296 | bytes 10485760 | tf_op jit(solution)/shard_map/pallas_call | solution.py:111
  165.0 1.9 constant_dynamic-slice_fusion.6.refs_8_
  166.9 2.0 constant_dynamic-slice_fusion.7.refs_7_
  170.6 9.1 %shard_map.245 = (bf16[1024,512]{1,0:T(8,128)(2,1)}, bf16[1024,512]{1,0:T(8,128)(2,1)}, bf16[1024,512]{1,0:T(8,128)(2,1)}, bf16[2,512,512]{2,1,0:T(8,128)(2,1)}, f32[1,512]{1,0:T(1,128)}) custom-call(bf16[1024,1024]{1,0:T(8,128)(2,1)} %get-tuple-element.66.refs_0_, bf16[1024,1024]{1,0:T(8,128)(2,1)} %get-tuple-element.65.refs_1_, ...), custom_call_target="tpu_custom_call" | custom-call | flops 4294967296 | bytes 10485760 | tf_op jit(solution)/shard_map/pallas_call | solution.py:111
  179.7 1.9 constant_dynamic-slice_fusion.3.refs_13_
  182.1 13.9 %shard_map.243 = (bf16[1024,128]{1,0:T(8,128)(2,1)}, bf16[1024,384]{1,0:T(8,128)(2,1)}, bf16[3,1024,128]{2,1,0:T(8,128)(2,1)}, bf16[128,1024]{1,0:T(8,128)(2,1)}, f32[1,384]{1,0:T(1,128)}) custom-call(bf16[1024,1024]{1,0:T(8,128)(2,1)} %get-tuple-element.64.refs_0_, bf16[1024,1024]{1,0:T(8,128)(2,1)} %get-tuple-element.65.refs_1_, ...), custom_call_target="tpu_custom_call" | custom-call | flops 4026531840 | bytes 2097152 | tf_op jit(solution)/shard_map/pallas_call | solution.py:243
  197.8 1.5 collective-permute-start.42
  204.4 32.8 %collective-permute-done.24 = bf16[512,512]{1,0:T(8,128)(2,1)S(1)} collective-permute-done((bf16[512,512]{1,0:T(8,128)(2,1)S(1)}, bf16[512,512]{1,0:T(8,128)(2,1)S(1)}, u32[]{:S(2)}, u32[]{:S(2)}) %collective-permute-start.24) | collective-permute-done | bytes 524320 | tf_op jit(solution)/shard_map/ppermute | solution.py:374
  239.1 9.3 %collective-permute-done.19 = bf16[512,512]{1,0:T(8,128)(2,1)S(1)} collective-permute-done((bf16[512,512]{1,0:T(8,128)(2,1)}, bf16[512,512]{1,0:T(8,128)(2,1)S(1)}, u32[]{:S(2)}, u32[]{:S(2)}) %collective-permute-start.19) | collective-permute-done | bytes 524320 | tf_op jit(solution)/shard_map/ppermute | solution.py:374
  249.2 2.7 collective-permute-done.31
  253.8 3.5 collective-permute-done.21
  257.4 4.6 %collective-permute-done.22 = bf16[256,512]{1,0:T(8,128)(2,1)S(1)} collective-permute-done((bf16[256,512]{1,0:T(8,128)(2,1)S(1)}, bf16[256,512]{1,0:T(8,128)(2,1)S(1)}, u32[]{:S(2)}, u32[]{:S(2)}) %collective-permute-start.22) | collective-permute-done | bytes 262176 | tf_op jit(solution)/shard_map/ppermute | solution.py:374
  262.1 1.6 collective-permute-start.37
  263.7 16.1 %shard_map.247 = (bf16[512,1024]{1,0:T(8,128)(2,1)}, f32[512,1024]{1,0:T(8,128)}, f32[4,1024]{1,0:T(4,128)}) custom-call(s32[2]{0:T(128)} %pad_add_fusion.refs_0_, bf16[1024,384]{1,0:T(8,128)(2,1)} %get-tuple-element.88.refs_1_, bf16[1024,384]{1,0:T(8,128)(2,1)} %get-tuple-element.89.refs_2_, bf16[1024,384]{1,0:T(8,128)(2,1)} %get-tuple-element.90.refs_3_, ...), custom_call_target="tpu_custom_call" | custom-call | flops 7516192768 | bytes 16777216 | tf_op jit(solution)/shard_map/pallas_call | solution.py:350
  280.0 2.5 collective-permute-start.34
  282.5 11.6 %shard_map.246 = (bf16[512,1024]{1,0:T(8,128)(2,1)}, bf16[512,1024]{1,0:T(8,128)(2,1)}) custom-call(s32[2]{0:T(128)} %pad_add_fusion.refs_0_, bf16[1024,128]{1,0:T(8,128)(2,1)} %get-tuple-element.74.refs_1_, bf16[1024,128]{1,0:T(8,128)(2,1)} %get-tuple-element.75.refs_2_, bf16[1024,128]{1,0:T(8,128)(2,1)} %get-tuple-element.76.refs_3_, ...), custom_call_target="tpu_custom_call" | custom-call | flops 5368709120 | bytes 16777216 | tf_op jit(solution)/shard_map/pallas_call | solution.py:350
  294.7 14.6 %collective-permute-done.34 = bf16[2,256,512]{2,1,0:T(8,128)(2,1)} collective-permute-done((bf16[2,256,512]{2,1,0:T(8,128)(2,1)S(1)}, bf16[2,256,512]{2,1,0:T(8,128)(2,1)}, u32[]{:S(2)}, u32[]{:S(2)}) %collective-permute-start.34) | collective-permute-done | bytes 524320 | tf_op jit(solution)/shard_map/ppermute | solution.py:449
  312.1 2.4 convert_reduce_fusion.1
  315.8 1.4 collective-permute-start.35
  317.2 21.2 %collective-permute-done.38 = bf16[2,256,512]{2,1,0:T(8,128)(2,1)} collective-permute-done((bf16[2,256,512]{2,1,0:T(8,128)(2,1)S(1)}, bf16[2,256,512]{2,1,0:T(8,128)(2,1)}, u32[]{:S(2)}, u32[]{:S(2)}) %collective-permute-start.38) | collective-permute-done | bytes 524320 | tf_op jit(solution)/shard_map/ppermute | solution.py:449
  340.6 2.5 collective-permute-done.27
  343.2 1.5 collective-permute-start.28
  344.7 2.5 collective-permute-done.28
  349.3 1.4 collective-permute-start.39
  350.8 20.5 %collective-permute-done.45 = bf16[256,512]{1,0:T(8,128)(2,1)S(1)} collective-permute-done((bf16[256,512]{1,0:T(8,128)(2,1)S(1)}, bf16[256,512]{1,0:T(8,128)(2,1)S(1)}, u32[]{:S(2)}, u32[]{:S(2)}) %collective-permute-start.45) | collective-permute-done | bytes 262176 | tf_op jit(solution)/shard_map/ppermute | solution.py:374
  371.3 1.4 collective-permute-start.47
  376.0 2.0 collective-permute-start.40
  378.0 1.5 collective-permute-start.36
  380.1 7.7 %collective-permute-done.47.refs_2_ = bf16[512,512]{1,0:T(8,128)(2,1)S(1)} collective-permute-done((bf16[512,512]{1,0:T(8,128)(2,1)S(1)}, bf16[512,512]{1,0:T(8,128)(2,1)S(1)}, u32[]{:S(2)}, u32[]{:S(2)}) %collective-permute-start.47) | collective-permute-done | bytes 524320 | tf_op jit(solution)/shard_map/ppermute | solution.py:374
  389.6 3.3 shard_map.252.refs_3_
  392.9 3.3 shard_map.253.refs_3_
  396.1 3.3 shard_map.248.refs_3_
  399.4 3.3 shard_map.249.refs_3_
  405.3 3.3 shard_map.254.refs_3_
  408.6 3.3 shard_map.255
  412.7 3.3 shard_map.250.refs_3_
  416.8 3.3 shard_map.251
  420.1 2.9 maximum_convert_fusion.1
  423.0 2.9 maximum_convert_fusion
  (268 shorter events, 57.1 us)
Async XLA Ops:
  7.2 412.9 %all-reduce.3.cloned.1.call-start = ((), (), s32[]{:S(2)}) async-start(), calls=%async_computation | async-start | bytes 8388608 | tf_op jit(solution)/shard_map/psum | solution.py:618
  7.2 6.2 %collective-permute-start.1 = (bf16[512,1024]{1,0:T(8,128)(2,1)}, bf16[512,1024]{1,0:T(8,128)(2,1)S(1)}, u32[]{:S(2)}, u32[]{:S(2)}) collective-permute-start(bf16[512,1024]{1,0:T(8,128)(2,1)} %own_cot_ref.1), channel_id=1, source_target_pairs={{0,1},{1,0},{2,3},{3,2},{4,5},{5,4},{6,7},{7,6},{8,9},{9,8},{10,11... | collective-permute-start | bytes 3145736 | tf_op jit(solution)/shard_map/ppermute | solution.py:578
  7.7 5.7 %collective-permute-start = (bf16[512,1024]{1,0:T(8,128)(2,1)}, bf16[512,1024]{1,0:T(8,128)(2,1)S(1)}, u32[]{:S(2)}, u32[]{:S(2)}) collective-permute-start(bf16[512,1024]{1,0:T(8,128)(2,1)} %own_ref.1), channel_id=1, source_target_pairs={{0,1},{1,0},{2,3},{3,2},{4,5},{5,4},{6,7},{7,6},{8,9},{9,8},{10,11... | collective-permute-start | bytes 3145736 | tf_op jit(solution)/shard_map/ppermute | solution.py:577
  32.5 24.4 %collective-permute-start.2 = (bf16[512,512]{1,0:T(8,128)(2,1)S(1)}, bf16[512,512]{1,0:T(8,128)(2,1)S(1)}, u32[]{:S(2)}, u32[]{:S(2)}) collective-permute-start(bf16[512,512]{1,0:T(8,128)(2,1)S(1)} %constant_dynamic-slice_fusion.15.refs_5_), channel_id=1, source_target_pairs={{0,2},{2,0},{4,6},{6,4},{8,10},{10,8},{12,14},{14,12},{16,18},{18,... | collective-permute-start | bytes 1572872 | tf_op jit(solution)/shard_map/ppermute | solution.py:374
  37.4 21.8 %collective-permute-start.3 = (bf16[512,512]{1,0:T(8,128)(2,1)}, bf16[512,512]{1,0:T(8,128)(2,1)}, u32[]{:S(2)}, u32[]{:S(2)}) collective-permute-start(bf16[512,512]{1,0:T(8,128)(2,1)} %constant_dynamic-slice_fusion.13.refs_6_), channel_id=1, source_target_pairs={{0,4},{2,6},{4,0},{6,2},{8,12},{10,14},{12,8},{14,10},{16,20},{18,... | collective-permute-start | bytes 1572872 | tf_op jit(solution)/shard_map/ppermute | solution.py:374
  53.0 15.1 %collective-permute-start.6 = (bf16[512,512]{1,0:T(8,128)(2,1)}, bf16[512,512]{1,0:T(8,128)(2,1)S(1)}, u32[]{:S(2)}, u32[]{:S(2)}) collective-permute-start(bf16[512,512]{1,0:T(8,128)(2,1)} %constant_dynamic-slice_fusion.11.refs_11_), channel_id=1, source_target_pairs={{0,2},{2,0},{4,6},{6,4},{8,10},{10,8},{12,14},{14,12},{16,18},{18,... | collective-permute-start | bytes 1572872 | tf_op jit(solution)/shard_map/ppermute | solution.py:374
  53.5 15.3 %collective-permute-start.7 = (bf16[512,512]{1,0:T(8,128)(2,1)}, bf16[512,512]{1,0:T(8,128)(2,1)S(1)}, u32[]{:S(2)}, u32[]{:S(2)}) collective-permute-start(bf16[512,512]{1,0:T(8,128)(2,1)} %constant_dynamic-slice_fusion.10.refs_12_), channel_id=1, source_target_pairs={{0,4},{2,6},{4,0},{6,2},{8,12},{10,14},{12,8},{14,10},{16,20},{18,... | collective-permute-start | bytes 1572872 | tf_op jit(solution)/shard_map/ppermute | solution.py:374
  57.2 28.4 %collective-permute-start.4 = (bf16[256,512]{1,0:T(8,128)(2,1)S(1)}, bf16[256,512]{1,0:T(8,128)(2,1)S(1)}, u32[]{:S(2)}, u32[]{:S(2)}) collective-permute-start(bf16[256,512]{1,0:T(8,128)(2,1)S(1)} %constant_dynamic-slice_fusion.14.refs_9_), channel_id=1, source_target_pairs={{0,4},{2,6},{4,0},{6,2},{8,12},{10,14},{12,8},{14,10},{16,20},{18,... | collective-permute-start | bytes 786440 | tf_op jit(solution)/shard_map/ppermute | solution.py:374
  60.4 25.3 %collective-permute-start.5 = (bf16[256,512]{1,0:T(8,128)(2,1)S(1)}, bf16[256,512]{1,0:T(8,128)(2,1)S(1)}, u32[]{:S(2)}, u32[]{:S(2)}) collective-permute-start(bf16[256,512]{1,0:T(8,128)(2,1)S(1)} %constant_dynamic-slice_fusion.12.refs_10_), channel_id=1, source_target_pairs={{0,2},{2,0},{4,6},{6,4},{8,10},{10,8},{12,14},{14,12},{16,18},{18,... | collective-permute-start | bytes 786440 | tf_op jit(solution)/shard_map/ppermute | solution.py:374
  68.3 16.6 %copy-start.40 = (bf16[256,512]{1,0:T(8,128)(2,1)}, bf16[256,512]{1,0:T(8,128)(2,1)S(1)}, u32[]{:S(2)}) copy-start(bf16[256,512]{1,0:T(8,128)(2,1)S(1)} %constant_dynamic-slice_fusion.9.refs_10_) | copy-start | bytes 786436
  68.3 19.9 %collective-permute-start.9 = (bf16[256,512]{1,0:T(8,128)(2,1)S(1)}, bf16[256,512]{1,0:T(8,128)(2,1)}, u32[]{:S(2)}, u32[]{:S(2)}) collective-permute-start(bf16[256,512]{1,0:T(8,128)(2,1)S(1)} %constant_dynamic-slice_fusion.9.refs_10_), channel_id=1, source_target_pairs={{0,4},{2,6},{4,0},{6,2},{8,12},{10,14},{12,8},{14,10},{16,20},{18,... | collective-permute-start | bytes 786440 | tf_op jit(solution)/shard_map/ppermute | solution.py:374
  69.7 19.5 %collective-permute-start.10 = (bf16[256,512]{1,0:T(8,128)(2,1)}, bf16[256,512]{1,0:T(8,128)(2,1)}, u32[]{:S(2)}, u32[]{:S(2)}) collective-permute-start(bf16[256,512]{1,0:T(8,128)(2,1)} %constant_dynamic-slice_fusion.8.refs_11_), channel_id=1, source_target_pairs={{0,2},{2,0},{4,6},{6,4},{8,10},{10,8},{12,14},{14,12},{16,18},{18,... | collective-permute-start | bytes 786440 | tf_op jit(solution)/shard_map/ppermute | solution.py:374
  86.6 19.2 %collective-permute-start.8 = (bf16[2,256,512]{2,1,0:T(8,128)(2,1)}, bf16[2,256,512]{2,1,0:T(8,128)(2,1)S(1)}, u32[]{:S(2)}, u32[]{:S(2)}) collective-permute-start(bf16[2,256,512]{2,1,0:T(8,128)(2,1)} %pad_maximum_fusion.refs_9_), channel_id=1, source_target_pairs={{0,8},{2,10},{4,12},{6,14},{8,0},{10,2},{12,4},{14,6},{16,24},{18,... | collective-permute-start | bytes 1572872 | tf_op jit(solution)/shard_map/ppermute | solution.py:449
  90.3 21.7 %collective-permute-start.12 = (bf16[2,256,512]{2,1,0:T(8,128)(2,1)S(1)}, bf16[2,256,512]{2,1,0:T(8,128)(2,1)S(1)}, u32[]{:S(2)}, u32[]{:S(2)}) collective-permute-start(bf16[2,256,512]{2,1,0:T(8,128)(2,1)S(1)} %pad_maximum_fusion.1.refs_10_), channel_id=1, source_target_pairs={{0,8},{2,10},{4,12},{6,14},{8,0},{10,2},{12,4},{14,6},{16,24},{18,... | collective-permute-start | bytes 1572872 | tf_op jit(solution)/shard_map/ppermute | solution.py:449
  106.0 36.3 %collective-permute-start.11 = (bf16[2,256,512]{2,1,0:T(8,128)(2,1)S(1)}, bf16[2,256,512]{2,1,0:T(8,128)(2,1)}, u32[]{:S(2)}, u32[]{:S(2)}) collective-permute-start(bf16[2,256,512]{2,1,0:T(8,128)(2,1)S(1)} %add_convert_fusion.11.refs_9_), channel_id=1, source_target_pairs={{0,16},{2,18},{4,20},{6,22},{8,24},{10,26},{12,28},{14,30},{16,0},... | collective-permute-start | bytes 1572872 | tf_op jit(solution)/shard_map/ppermute | solution.py:449
  112.1 16.7 %copy-start.25 = (bf16[2,256,512]{2,1,0:T(8,128)(2,1)}, bf16[2,256,512]{2,1,0:T(8,128)(2,1)S(1)}, u32[]{:S(2)}) copy-start(bf16[2,256,512]{2,1,0:T(8,128)(2,1)S(1)} %add_convert_fusion.9.refs_11_) | copy-start | bytes 1572868
  112.2 38.2 %collective-permute-start.15 = (bf16[2,256,512]{2,1,0:T(8,128)(2,1)S(1)}, bf16[2,256,512]{2,1,0:T(8,128)(2,1)}, u32[]{:S(2)}, u32[]{:S(2)}) collective-permute-start(bf16[2,256,512]{2,1,0:T(8,128)(2,1)S(1)} %add_convert_fusion.9.refs_11_), channel_id=1, source_target_pairs={{0,16},{2,18},{4,20},{6,22},{8,24},{10,26},{12,28},{14,30},{16,0},... | collective-permute-start | bytes 1572872 | tf_op jit(solution)/shard_map/ppermute | solution.py:449
  143.6 10.7 %collective-permute-start.14 = (bf16[256,512]{1,0:T(8,128)(2,1)S(1)}, bf16[256,512]{1,0:T(8,128)(2,1)S(1)}, u32[]{:S(2)}, u32[]{:S(2)}) collective-permute-start(bf16[256,512]{1,0:T(8,128)(2,1)S(1)} %get-tuple-element.158.refs_10_), channel_id=1, source_target_pairs={{0,2},{2,0},{4,6},{6,4},{8,10},{10,8},{12,14},{14,12},{16,18},{18,... | collective-permute-start | bytes 786440 | tf_op jit(solution)/shard_map/ppermute | solution.py:374
  144.6 9.7 %collective-permute-start.13 = (bf16[256,512]{1,0:T(8,128)(2,1)S(1)}, bf16[256,512]{1,0:T(8,128)(2,1)S(1)}, u32[]{:S(2)}, u32[]{:S(2)}) collective-permute-start(bf16[256,512]{1,0:T(8,128)(2,1)S(1)} %get-tuple-element.159.refs_9_), channel_id=1, source_target_pairs={{0,4},{2,6},{4,0},{6,2},{8,12},{10,14},{12,8},{14,10},{16,20},{18,... | collective-permute-start | bytes 786440 | tf_op jit(solution)/shard_map/ppermute | solution.py:374
  151.6 17.2 %collective-permute-start.17 = (bf16[256,512]{1,0:T(8,128)(2,1)S(1)}, bf16[256,512]{1,0:T(8,128)(2,1)S(1)}, u32[]{:S(2)}, u32[]{:S(2)}) collective-permute-start(bf16[256,512]{1,0:T(8,128)(2,1)S(1)} %get-tuple-element.154.refs_8_), channel_id=1, source_target_pairs={{0,2},{2,0},{4,6},{6,4},{8,10},{10,8},{12,14},{14,12},{16,18},{18,... | collective-permute-start | bytes 786440 | tf_op jit(solution)/shard_map/ppermute | solution.py:374
  152.8 16.1 %collective-permute-start.16 = (bf16[256,512]{1,0:T(8,128)(2,1)S(1)}, bf16[256,512]{1,0:T(8,128)(2,1)S(1)}, u32[]{:S(2)}, u32[]{:S(2)}) collective-permute-start(bf16[256,512]{1,0:T(8,128)(2,1)S(1)} %get-tuple-element.155.refs_7_), channel_id=1, source_target_pairs={{0,4},{2,6},{4,0},{6,2},{8,12},{10,14},{12,8},{14,10},{16,20},{18,... | collective-permute-start | bytes 786440 | tf_op jit(solution)/shard_map/ppermute | solution.py:374
  181.6 20.4 %collective-permute-start.23 = (bf16[512,512]{1,0:T(8,128)(2,1)}, bf16[512,512]{1,0:T(8,128)(2,1)}, u32[]{:S(2)}, u32[]{:S(2)}) collective-permute-start(bf16[512,512]{1,0:T(8,128)(2,1)} %constant_dynamic-slice_fusion.3.refs_13_), channel_id=1, source_target_pairs={{0,2},{2,0},{4,6},{6,4},{8,10},{10,8},{12,14},{14,12},{16,18},{18,... | collective-permute-start | bytes 1572872 | tf_op jit(solution)/shard_map/ppermute | solution.py:374
  197.8 176.1 %collective-permute-start.42 = (bf16[512,512]{1,0:T(8,128)(2,1)S(1)}, bf16[512,512]{1,0:T(8,128)(2,1)}, u32[]{:S(2)}, u32[]{:S(2)}) collective-permute-start(bf16[512,512]{1,0:T(8,128)(2,1)S(1)} %copy-done.3), channel_id=1, source_target_pairs={{0,2},{2,0},{4,6},{6,4},{8,10},{10,8},{12,14},{14,12},{16,18},{18,... | collective-permute-start | bytes 1572872 | tf_op jit(solution)/shard_map/ppermute | solution.py:374
  199.3 175.3 %collective-permute-start.48 = (bf16[512,512]{1,0:T(8,128)(2,1)S(1)}, bf16[512,512]{1,0:T(8,128)(2,1)}, u32[]{:S(2)}, u32[]{:S(2)}) collective-permute-start(bf16[512,512]{1,0:T(8,128)(2,1)S(1)} %copy-done.4), channel_id=1, source_target_pairs={{0,4},{2,6},{4,0},{6,2},{8,12},{10,14},{12,8},{14,10},{16,20},{18,... | collective-permute-start | bytes 1572872 | tf_op jit(solution)/shard_map/ppermute | solution.py:374
  199.8 38.1 %collective-permute-start.18 = (bf16[512,512]{1,0:T(8,128)(2,1)}, bf16[512,512]{1,0:T(8,128)(2,1)S(1)}, u32[]{:S(2)}, u32[]{:S(2)}) collective-permute-start(bf16[512,512]{1,0:T(8,128)(2,1)} %constant_dynamic-slice_fusion.7.refs_7_), channel_id=1, source_target_pairs={{0,2},{2,0},{4,6},{6,4},{8,10},{10,8},{12,14},{14,12},{16,18},{18,... | collective-permute-start | bytes 1572872 | tf_op jit(solution)/shard_map/ppermute | solution.py:374
  200.8 36.5 %copy-start.34 = (bf16[512,512]{1,0:T(8,128)(2,1)}, bf16[512,512]{1,0:T(8,128)(2,1)S(1)}, u32[]{:S(2)}) copy-start(bf16[512,512]{1,0:T(8,128)(2,1)S(1)} %constant_dynamic-slice_fusion.2.refs_14_) | copy-start | bytes 1572868
  200.8 36.4 %collective-permute-start.24 = (bf16[512,512]{1,0:T(8,128)(2,1)S(1)}, bf16[512,512]{1,0:T(8,128)(2,1)S(1)}, u32[]{:S(2)}, u32[]{:S(2)}) collective-permute-start(bf16[512,512]{1,0:T(8,128)(2,1)S(1)} %constant_dynamic-slice_fusion.2.refs_14_), channel_id=1, source_target_pairs={{0,4},{2,6},{4,0},{6,2},{8,12},{10,14},{12,8},{14,10},{16,20},{18,... | collective-permute-start | bytes 1572872 | tf_op jit(solution)/shard_map/ppermute | solution.py:374
  202.0 37.0 %copy-start.14 = (bf16[1024,512]{1,0:T(8,128)(2,1)S(1)}, bf16[1024,512]{1,0:T(8,128)(2,1)}, u32[]{:S(2)}) copy-start(bf16[1024,512]{1,0:T(8,128)(2,1)} %get-tuple-element.81) | copy-start | bytes 3145732
  202.0 46.5 %collective-permute-start.19 = (bf16[512,512]{1,0:T(8,128)(2,1)}, bf16[512,512]{1,0:T(8,128)(2,1)S(1)}, u32[]{:S(2)}, u32[]{:S(2)}) collective-permute-start(bf16[512,512]{1,0:T(8,128)(2,1)} %constant_dynamic-slice_fusion.6.refs_8_), channel_id=1, source_target_pairs={{0,4},{2,6},{4,0},{6,2},{8,12},{10,14},{12,8},{14,10},{16,20},{18,... | collective-permute-start | bytes 1572872 | tf_op jit(solution)/shard_map/ppermute | solution.py:374
  204.4 34.8 %copy-start.37 = (bf16[256,512]{1,0:T(8,128)(2,1)}, bf16[256,512]{1,0:T(8,128)(2,1)S(1)}, u32[]{:S(2)}) copy-start(bf16[256,512]{1,0:T(8,128)(2,1)S(1)} %constant_dynamic-slice_fusion.1.refs_15_) | copy-start | bytes 786436
  204.4 44.6 %copy-start.13 = (bf16[2,512,512]{2,1,0:T(8,128)(2,1)S(1)}, bf16[2,512,512]{2,1,0:T(8,128)(2,1)}, u32[]{:S(2)}) copy-start(bf16[2,512,512]{2,1,0:T(8,128)(2,1)} %get-tuple-element.82) | copy-start | bytes 3145732
  237.2 14.6 %collective-permute-start.31 = (bf16[256,512]{1,0:T(8,128)(2,1)S(1)}, bf16[256,512]{1,0:T(8,128)(2,1)S(1)}, u32[]{:S(2)}, u32[]{:S(2)}) collective-permute-start(bf16[256,512]{1,0:T(8,128)(2,1)S(1)} %constant_dynamic-slice_fusion.1.refs_15_), channel_id=1, source_target_pairs={{0,4},{2,6},{4,0},{6,2},{8,12},{10,14},{12,8},{14,10},{16,20},{18,... | collective-permute-start | bytes 786440 | tf_op jit(solution)/shard_map/ppermute | solution.py:374
  237.9 14.5 %collective-permute-start.32 = (bf16[256,512]{1,0:T(8,128)(2,1)S(1)}, bf16[256,512]{1,0:T(8,128)(2,1)S(1)}, u32[]{:S(2)}, u32[]{:S(2)}) collective-permute-start(bf16[256,512]{1,0:T(8,128)(2,1)S(1)} %constant_dynamic-slice_fusion.refs_16_), channel_id=1, source_target_pairs={{0,2},{2,0},{4,6},{6,4},{8,10},{10,8},{12,14},{14,12},{16,18},{18,... | collective-permute-start | bytes 786440 | tf_op jit(solution)/shard_map/ppermute | solution.py:374
  248.5 8.8 %collective-permute-start.21 = (bf16[256,512]{1,0:T(8,128)(2,1)S(1)}, bf16[256,512]{1,0:T(8,128)(2,1)S(1)}, u32[]{:S(2)}, u32[]{:S(2)}) collective-permute-start(bf16[256,512]{1,0:T(8,128)(2,1)S(1)} %constant_dynamic-slice_fusion.5.refs_11_), channel_id=1, source_target_pairs={{0,4},{2,6},{4,0},{6,2},{8,12},{10,14},{12,8},{14,10},{16,20},{18,... | collective-permute-start | bytes 786440 | tf_op jit(solution)/shard_map/ppermute | solution.py:374
  251.8 10.2 %collective-permute-start.22 = (bf16[256,512]{1,0:T(8,128)(2,1)S(1)}, bf16[256,512]{1,0:T(8,128)(2,1)S(1)}, u32[]{:S(2)}, u32[]{:S(2)}) collective-permute-start(bf16[256,512]{1,0:T(8,128)(2,1)S(1)} %constant_dynamic-slice_fusion.4.refs_12_), channel_id=1, source_target_pairs={{0,2},{2,0},{4,6},{6,4},{8,10},{10,8},{12,14},{14,12},{16,18},{18,... | collective-permute-start | bytes 786440 | tf_op jit(solution)/shard_map/ppermute | solution.py:374
  252.6 27.3 %collective-permute-start.33 = (bf16[2,256,512]{2,1,0:T(8,128)(2,1)S(1)}, bf16[2,256,512]{2,1,0:T(8,128)(2,1)S(1)}, u32[]{:S(2)}, u32[]{:S(2)}) collective-permute-start(bf16[2,256,512]{2,1,0:T(8,128)(2,1)S(1)} %pad_maximum_fusion.7), channel_id=1, source_target_pairs={{0,8},{2,10},{4,12},{6,14},{8,0},{10,2},{12,4},{14,6},{16,24},{18,... | collective-permute-start | bytes 1572872 | tf_op jit(solution)/shard_map/ppermute | solution.py:449
  262.1 32.1 %collective-permute-start.37 = (bf16[2,256,512]{2,1,0:T(8,128)(2,1)S(1)}, bf16[2,256,512]{2,1,0:T(8,128)(2,1)S(1)}, u32[]{:S(2)}, u32[]{:S(2)}) collective-permute-start(bf16[2,256,512]{2,1,0:T(8,128)(2,1)S(1)} %pad_maximum_fusion.6.refs_14_), channel_id=1, source_target_pairs={{0,8},{2,10},{4,12},{6,14},{8,0},{10,2},{12,4},{14,6},{16,24},{18,... | collective-permute-start | bytes 1572872 | tf_op jit(solution)/shard_map/ppermute | solution.py:449
  279.8 30.7 %collective-permute-start.25 = (bf16[512,1024]{1,0:T(8,128)(2,1)}, bf16[512,1024]{1,0:T(8,128)(2,1)S(1)}, u32[]{:S(2)}, u32[]{:S(2)}) collective-permute-start(bf16[512,1024]{1,0:T(8,128)(2,1)} %get-tuple-element.97), channel_id=1, source_target_pairs={{0,1},{1,0},{2,3},{3,2},{4,5},{5,4},{6,7},{7,6},{8,9},{9,8},{10,11... | collective-permute-start | bytes 3145736 | tf_op jit(solution)/shard_map/ppermute | solution.py:636
  280.0 29.2 %collective-permute-start.34 = (bf16[2,256,512]{2,1,0:T(8,128)(2,1)S(1)}, bf16[2,256,512]{2,1,0:T(8,128)(2,1)}, u32[]{:S(2)}, u32[]{:S(2)}) collective-permute-start(bf16[2,256,512]{2,1,0:T(8,128)(2,1)S(1)} %add_convert_fusion.3), channel_id=1, source_target_pairs={{0,16},{2,18},{4,20},{6,22},{8,24},{10,26},{12,28},{14,30},{16,0},... | collective-permute-start | bytes 1572872 | tf_op jit(solution)/shard_map/ppermute | solution.py:449
  294.2 16.3 %copy-start = (bf16[512,1024]{1,0:T(8,128)(2,1)S(1)}, bf16[512,1024]{1,0:T(8,128)(2,1)}, u32[]{:S(2)}) copy-start(bf16[512,1024]{1,0:T(8,128)(2,1)} %own_ref.1) | copy-start | bytes 3145732
  294.2 16.3 %copy-start.1 = (f32[512,1024]{1,0:T(8,128)S(1)}, f32[512,1024]{1,0:T(8,128)}, u32[]{:S(2)}) copy-start(f32[512,1024]{1,0:T(8,128)} %get-tuple-element.98) | copy-start | bytes 6291460
  294.2 17.2 %collective-permute-start.20 = (bf16[512,1024]{1,0:T(8,128)(2,1)}, bf16[512,1024]{1,0:T(8,128)(2,1)S(1)}, u32[]{:S(2)}, u32[]{:S(2)}) collective-permute-start(bf16[512,1024]{1,0:T(8,128)(2,1)} %get-tuple-element.86), channel_id=1, source_target_pairs={{0,1},{1,0},{2,3},{3,2},{4,5},{5,4},{6,7},{7,6},{8,9},{9,8},{10,11... | collective-permute-start | bytes 3145736 | tf_op jit(solution)/shard_map/ppermute | solution.py:635
  309.2 29.1 %collective-permute-start.38 = (bf16[2,256,512]{2,1,0:T(8,128)(2,1)S(1)}, bf16[2,256,512]{2,1,0:T(8,128)(2,1)}, u32[]{:S(2)}, u32[]{:S(2)}) collective-permute-start(bf16[2,256,512]{2,1,0:T(8,128)(2,1)S(1)} %add_convert_fusion.1), channel_id=1, source_target_pairs={{0,16},{2,18},{4,20},{6,22},{8,24},{10,26},{12,28},{14,30},{16,0},... | collective-permute-start | bytes 1572872 | tf_op jit(solution)/shard_map/ppermute | solution.py:449
  314.5 32.7 %copy-start.5 = (bf16[512,512]{1,0:T(8,128)(2,1)S(1)}, bf16[512,512]{1,0:T(8,128)(2,1)}, u32[]{:S(2)}) copy-start(bf16[512,512]{1,0:T(8,128)(2,1)} %pad_maximum_fusion.4.refs_5_.refs_1_) | copy-start | bytes 1572868
  314.5 1.3 collective-permute-start.26
  314.7 33.6 %collective-permute-start.43 = (bf16[256,512]{1,0:T(8,128)(2,1)S(1)}, bf16[256,512]{1,0:T(8,128)(2,1)S(1)}, u32[]{:S(2)}, u32[]{:S(2)}) collective-permute-start(bf16[256,512]{1,0:T(8,128)(2,1)S(1)} %get-tuple-element.150), channel_id=1, source_target_pairs={{0,2},{2,0},{4,6},{6,4},{8,10},{10,8},{12,14},{14,12},{16,18},{18,... | collective-permute-start | bytes 786440 | tf_op jit(solution)/shard_map/ppermute | solution.py:374
  315.8 33.5 %collective-permute-start.35 = (bf16[256,512]{1,0:T(8,128)(2,1)S(1)}, bf16[256,512]{1,0:T(8,128)(2,1)S(1)}, u32[]{:S(2)}, u32[]{:S(2)}) collective-permute-start(bf16[256,512]{1,0:T(8,128)(2,1)S(1)} %get-tuple-element.151), channel_id=1, source_target_pairs={{0,4},{2,6},{4,0},{6,2},{8,12},{10,14},{12,8},{14,10},{16,20},{18,... | collective-permute-start | bytes 786440 | tf_op jit(solution)/shard_map/ppermute | solution.py:374
  338.3 4.8 %collective-permute-start.27 = (f32[8704]{0:T(1024)S(1)}, f32[8704]{0:T(1024)S(1)}, u32[]{:S(2)}, u32[]{:S(2)}) collective-permute-start(f32[8704]{0:T(1024)S(1)} %pad_maximum_fusion.12), channel_id=1, source_target_pairs={{0,2},{2,0},{4,6},{6,4},{8,10},{10,8},{12,14},{14,12},{16,18},{18,... | collective-permute-start | bytes 104456 | tf_op jit(solution)/shard_map/ppermute | solution.py:498
  340.6 30.7 %copy-start.6 = (bf16[512,512]{1,0:T(8,128)(2,1)S(1)}, bf16[512,512]{1,0:T(8,128)(2,1)}, u32[]{:S(2)}) copy-start(bf16[512,512]{1,0:T(8,128)(2,1)} %pad_maximum_fusion.5.refs_6_.refs_1_) | copy-start | bytes 1572868
  343.2 4.0 collective-permute-start.28
  347.2 28.8 %collective-permute-start.41 = (bf16[512,512]{1,0:T(8,128)(2,1)S(1)}, bf16[512,512]{1,0:T(8,128)(2,1)S(1)}, u32[]{:S(2)}, u32[]{:S(2)}) collective-permute-start(bf16[512,512]{1,0:T(8,128)(2,1)S(1)} %copy-done.5), channel_id=1, source_target_pairs={{0,2},{2,0},{4,6},{6,4},{8,10},{10,8},{12,14},{14,12},{16,18},{18,... | collective-permute-start | bytes 1572872 | tf_op jit(solution)/shard_map/ppermute | solution.py:374
  348.2 23.1 %collective-permute-start.45 = (bf16[256,512]{1,0:T(8,128)(2,1)S(1)}, bf16[256,512]{1,0:T(8,128)(2,1)S(1)}, u32[]{:S(2)}, u32[]{:S(2)}) collective-permute-start(bf16[256,512]{1,0:T(8,128)(2,1)S(1)} %get-tuple-element.146), channel_id=1, source_target_pairs={{0,2},{2,0},{4,6},{6,4},{8,10},{10,8},{12,14},{14,12},{16,18},{18,... | collective-permute-start | bytes 786440 | tf_op jit(solution)/shard_map/ppermute | solution.py:374
  349.3 23.3 %collective-permute-start.39 = (bf16[256,512]{1,0:T(8,128)(2,1)S(1)}, bf16[256,512]{1,0:T(8,128)(2,1)S(1)}, u32[]{:S(2)}, u32[]{:S(2)}) collective-permute-start(bf16[256,512]{1,0:T(8,128)(2,1)S(1)} %get-tuple-element.147), channel_id=1, source_target_pairs={{0,4},{2,6},{4,0},{6,2},{8,12},{10,14},{12,8},{14,10},{16,20},{18,... | collective-permute-start | bytes 786440 | tf_op jit(solution)/shard_map/ppermute | solution.py:374
  371.3 16.5 %collective-permute-start.47 = (bf16[512,512]{1,0:T(8,128)(2,1)S(1)}, bf16[512,512]{1,0:T(8,128)(2,1)S(1)}, u32[]{:S(2)}, u32[]{:S(2)}) collective-permute-start(bf16[512,512]{1,0:T(8,128)(2,1)S(1)} %copy-done.6), channel_id=1, source_target_pairs={{0,4},{2,6},{4,0},{6,2},{8,12},{10,14},{12,8},{14,10},{16,20},{18,... | collective-permute-start | bytes 1572872 | tf_op jit(solution)/shard_map/ppermute | solution.py:374
  372.7 5.3 %collective-permute-start.29 = (f32[8704]{0:T(1024)S(1)}, f32[8704]{0:T(1024)S(1)}, u32[]{:S(2)}, u32[]{:S(2)}) collective-permute-start(f32[8704]{0:T(1024)S(1)} %add.420), channel_id=1, source_target_pairs={{0,8},{2,10},{4,12},{6,14},{8,0},{10,2},{12,4},{14,6},{16,24},{18,... | collective-permute-start | bytes 104456 | tf_op jit(solution)/shard_map/ppermute | solution.py:498
  372.8 20.1 %copy-start.8 = (bf16[512,512]{1,0:T(8,128)(2,1)}, bf16[512,512]{1,0:T(8,128)(2,1)S(1)}, u32[]{:S(2)}) copy-start(bf16[512,512]{1,0:T(8,128)(2,1)S(1)} %pad_maximum_fusion.10.refs_1_) | copy-start | bytes 1572868
  372.8 20.0 %copy-start.7 = (bf16[512,512]{1,0:T(8,128)(2,1)}, bf16[512,512]{1,0:T(8,128)(2,1)S(1)}, u32[]{:S(2)}) copy-start(bf16[512,512]{1,0:T(8,128)(2,1)S(1)} %pad_maximum_fusion.8.refs_1_) | copy-start | bytes 1572868
  373.8 19.0 %copy-start.9 = (bf16[512,512]{1,0:T(8,128)(2,1)}, bf16[512,512]{1,0:T(8,128)(2,1)S(1)}, u32[]{:S(2)}) copy-start(bf16[512,512]{1,0:T(8,128)(2,1)S(1)} %pad_maximum_fusion.9.refs_1_) | copy-start | bytes 1572868
  373.9 30.7 %collective-permute-start.46 = (bf16[512,512]{1,0:T(8,128)(2,1)}, bf16[512,512]{1,0:T(8,128)(2,1)S(1)}, u32[]{:S(2)}, u32[]{:S(2)}) collective-permute-start(bf16[512,512]{1,0:T(8,128)(2,1)} %pad_maximum_fusion.11.refs_1_), channel_id=1, source_target_pairs={{0,4},{2,6},{4,0},{6,2},{8,12},{10,14},{12,8},{14,10},{16,20},{18,... | collective-permute-start | bytes 1572872 | tf_op jit(solution)/shard_map/ppermute | solution.py:374
  374.6 34.0 %collective-permute-start.44 = (bf16[512,512]{1,0:T(8,128)(2,1)S(1)}, bf16[512,512]{1,0:T(8,128)(2,1)}, u32[]{:S(2)}, u32[]{:S(2)}) collective-permute-start(bf16[512,512]{1,0:T(8,128)(2,1)S(1)} %pad_maximum_fusion.10.refs_1_), channel_id=1, source_target_pairs={{0,4},{2,6},{4,0},{6,2},{8,12},{10,14},{12,8},{14,10},{16,20},{18,... | collective-permute-start | bytes 1572872 | tf_op jit(solution)/shard_map/ppermute | solution.py:374
  376.0 16.9 %copy-start.26 = (bf16[512,512]{1,0:T(8,128)(2,1)}, bf16[512,512]{1,0:T(8,128)(2,1)S(1)}, u32[]{:S(2)}) copy-start(bf16[512,512]{1,0:T(8,128)(2,1)S(1)} %collective-permute-done.41.refs_2_) | copy-start | bytes 1572868
  376.0 35.9 %collective-permute-start.40 = (bf16[512,512]{1,0:T(8,128)(2,1)S(1)}, bf16[512,512]{1,0:T(8,128)(2,1)S(1)}, u32[]{:S(2)}, u32[]{:S(2)}) collective-permute-start(bf16[512,512]{1,0:T(8,128)(2,1)S(1)} %pad_maximum_fusion.9.refs_1_), channel_id=1, source_target_pairs={{0,2},{2,0},{4,6},{6,4},{8,10},{10,8},{12,14},{14,12},{16,18},{18,... | collective-permute-start | bytes 1572872 | tf_op jit(solution)/shard_map/ppermute | solution.py:374
  378.0 38.0 %collective-permute-start.36 = (bf16[512,512]{1,0:T(8,128)(2,1)S(1)}, bf16[512,512]{1,0:T(8,128)(2,1)S(1)}, u32[]{:S(2)}, u32[]{:S(2)}) collective-permute-start(bf16[512,512]{1,0:T(8,128)(2,1)S(1)} %pad_maximum_fusion.8.refs_1_), channel_id=1, source_target_pairs={{0,2},{2,0},{4,6},{6,4},{8,10},{10,8},{12,14},{14,12},{16,18},{18,... | collective-permute-start | bytes 1572872 | tf_op jit(solution)/shard_map/ppermute | solution.py:374
  387.8 14.9 %collective-permute-start.30 = (f32[8704]{0:T(1024)S(1)}, f32[8704]{0:T(1024)S(1)}, u32[]{:S(2)}, u32[]{:S(2)}) collective-permute-start(f32[8704]{0:T(1024)S(1)} %add.421), channel_id=1, source_target_pairs={{0,16},{2,18},{4,20},{6,22},{8,24},{10,26},{12,28},{14,30},{16,0},... | collective-permute-start | bytes 104456 | tf_op jit(solution)/shard_map/ppermute | solution.py:498
  (41 other events, 241.6 us)
Sparse Core Ops, SparseCore 0:
  197.0 206.0 all-reduce.2

commit v3 on v2

--- a/solution.py
+++ b/solution.py
@@ -18,7 +18,9 @@
 F32 = jnp.float32
 BF16 = jnp.bfloat16
 PAIR = 2 * HD
+FIRST = 1
 QROWS = 256
+ROWS = 512
 HIDDEN = 256
 VMEM = 56 * 1024 * 1024
 
@@ -44,12 +46,9 @@
 
 
 def prep_kernel(slot_ref, own_ref, other_ref, own_cot_ref, other_cot_ref, g1_ref, b1_ref, g2_ref, b2_ref,
-                normed_ref, first_ref, second_ref, cot_ref):
+                first_ref, second_ref, cot_ref):
     def emit(x_ref, c_ref):
-        x = x_ref[...].astype(F32)
-        centred = x - jnp.mean(x, axis=1, keepdims=True)
-        normed = centred * lax.rsqrt(jnp.mean(centred * centred, axis=1, keepdims=True) + EPSILON)
-        normed_ref[...] = normed
+        normed, _ = normalize(x_ref[...].astype(F32))
         first_ref[...] = (normed * g1_ref[...] + b1_ref[...]).astype(BF16)
         second_ref[...] = (normed * g2_ref[...] + b2_ref[...]).astype(BF16)
         cot_ref[...] = c_ref[...]
@@ -72,20 +71,19 @@
             num_scalar_prefetch=1,
             grid=(2, count),
             in_specs=[mine, theirs, mine, theirs] + [vector] * 4,
-            out_specs=[out] * 4,
+            out_specs=[out] * 3,
         ),
         out_shape=[
-            jax.ShapeDtypeStruct((2 * rows, width), F32),
             jax.ShapeDtypeStruct((2 * rows, width), BF16),
             jax.ShapeDtypeStruct((2 * rows, width), BF16),
             jax.ShapeDtypeStruct((2 * rows, width), BF16),
         ],
         compiler_params=PARAMS,
-        cost_estimate=pl.CostEstimate(flops=rows * width * 40, bytes_accessed=rows * width * 28, transcendentals=0),
+        cost_estimate=pl.CostEstimate(flops=rows * width * 40, bytes_accessed=rows * width * 20, transcendentals=0),
     )(jnp.stack([here, 1 - here]), own, other, own_cot, other_cot, *[g.reshape(1, -1) for g in gains])
 
 
-def ffn_kernel(second_ref, cot_ref, inner_ref, bias_ref, outer_ref, active_ref, back_ref, left_ref, right_ref, biasgrad_ref):
+def ffn_kernel(at_ref, second_ref, cot_ref, inner_ref, bias_ref, outer_ref, active_ref, back_ref, biasgrad_ref, *out_refs):
     second = second_ref[...]
     cot = cot_ref[...]
     preact = dot(second, inner_ref[...], NN) + bias_ref[...]
@@ -97,47 +95,79 @@
     biasgrad_ref[...] = jnp.sum(pre_grad, axis=0, keepdims=True)
     back = pre_grad.astype(BF16)
     back_ref[...] = back
-    left_ref[...] = dot(second, back, TN).astype(BF16)
-    outer = dot(active, cot, TN).astype(BF16)
-    cols = right_ref.shape[2]
-    for c in range(right_ref.shape[0]):
-        right_ref[c] = outer[:, c * cols : (c + 1) * cols]
-
-
-def ffn_slice(second_in, cot, inner_weight, inner_bias, outer_weight, first, count, held=()):
+    inner_grad = dot(second, back, TN)
+    outer_grad = dot(active, cot, TN)
+    if len(out_refs) == 4:
+        left_away, left_own, right_away, right_own = out_refs
+        half, cols = left_own.shape[0], right_own.shape[1]
+        low, high = inner_grad[:half].astype(BF16), inner_grad[half:].astype(BF16)
+        left_first = at_ref[0] == 0
+        left_away[...] = jnp.where(left_first, high, low)
+        left_own[...] = jnp.where(left_first, low, high)
+        low, high = outer_grad[:, :cols].astype(BF16), outer_grad[:, cols:].astype(BF16)
+        right_first = at_ref[1] == 0
+        right_away[...] = jnp.where(right_first, high, low)
+        right_own[...] = jnp.where(right_first, low, high)
+    else:
+        left_ref, right_ref = out_refs
+        left_ref[...] = inner_grad.astype(BF16)
+        cols = right_ref.shape[2]
+        for c in range(right_ref.shape[0]):
+            right_ref[c] = outer_grad[:, c * cols : (c + 1) * cols].astype(BF16)
+
+
+def ffn_slice(second_in, cot, inner_weight, inner_bias, outer_weight, first, count, fast, mid, held=()):
     rows, width = second_in.shape
     cols = count * HIDDEN
-    whole = pl.BlockSpec((rows, width), lambda j: (0, 0))
-    return pl.pallas_call(
-        after(ffn_kernel, 5, len(held)),
-        grid=(count,),
-        in_specs=[
-            whole,
-            whole,
-            pl.BlockSpec((width, HIDDEN), lambda j: (0, first + j)),
-            pl.BlockSpec((1, HIDDEN), lambda j: (0, first + j)),
-            pl.BlockSpec((HIDDEN, width), lambda j: (first + j, 0)),
+    whole = pl.BlockSpec((rows, width), lambda j, at: (0, 0))
+    split = fast[1] == 2 and mid[1] == 2 and width == 2 * cols
+    out_specs = [
+        pl.BlockSpec((rows, HIDDEN), lambda j, at: (0, j)),
+        pl.BlockSpec((rows, HIDDEN), lambda j, at: (0, j)),
+        pl.BlockSpec((1, HIDDEN), lambda j, at: (0, j)),
+    ]
+    out_shape = [
+        jax.ShapeDtypeStruct((rows, cols), BF16),
+        jax.ShapeDtypeStruct((rows, cols), BF16),
+        jax.ShapeDtypeStruct((1, cols), F32),
+    ]
+    if split:
+        out_specs += [pl.BlockSpec((cols, HIDDEN), lambda j, at: (0, j))] * 2
+        out_specs += [pl.BlockSpec((HIDDEN, cols), lambda j, at: (j, 0))] * 2
+        out_shape += [jax.ShapeDtypeStruct((cols, cols), BF16)] * 4
+    else:
+        out_specs += [
+            pl.BlockSpec((width, HIDDEN), lambda j, at: (0, j)),
+            pl.BlockSpec((width // cols, HIDDEN, cols), lambda j, at: (0, j, 0)),
         ]
-        + [ANY] * len(held),
-        out_specs=[
-            pl.BlockSpec((rows, HIDDEN), lambda j: (0, j)),
-            pl.BlockSpec((rows, HIDDEN), lambda j: (0, j)),
-            pl.BlockSpec((width, HIDDEN), lambda j: (0, j)),
-            pl.BlockSpec((width // cols, HIDDEN, cols), lambda j: (0, j, 0)),
-            pl.BlockSpec((1, HIDDEN), lambda j: (0, j)),
-        ],
-        out_shape=[
-            jax.ShapeDtypeStruct((rows, cols), BF16),
-            jax.ShapeDtypeStruct((rows, cols), BF16),
+        out_shape += [
             jax.ShapeDtypeStruct((width, cols), BF16),
             jax.ShapeDtypeStruct((width // cols, cols, cols), BF16),
-            jax.ShapeDtypeStruct((1, cols), F32),
-        ],
+        ]
+    active, back, bias_grad, *grads = pl.pallas_call(
+        after(ffn_kernel, 6, len(held)),
+        grid_spec=pltpu.PrefetchScalarGridSpec(
+            num_scalar_prefetch=1,
+            grid=(count,),
+            in_specs=[
+                whole,
+                whole,
+                pl.BlockSpec((width, HIDDEN), lambda j, at: (0, first + j)),
+                pl.BlockSpec((1, HIDDEN), lambda j, at: (0, first + j)),
+                pl.BlockSpec((HIDDEN, width), lambda j, at: (first + j, 0)),
+            ]
+            + [ANY] * len(held),
+            out_specs=out_specs,
+        ),
+        out_shape=out_shape,
         compiler_params=PARAMS,
         cost_estimate=pl.CostEstimate(
             flops=8 * rows * width * cols, bytes_accessed=20 * width * cols, transcendentals=2 * rows * cols
         ),
-    )(second_in, cot, inner_weight, inner_bias, outer_weight, *held)
+    )(jnp.stack([position(fast), position(mid)]), second_in, cot, inner_weight, inner_bias, outer_weight, *held)
+    if split:
+        return active, back, bias_grad, tuple(grads[:2]), tuple(grads[2:])
+    return active, back, bias_grad, grads[0], grads[1].reshape(width, cols)
 
 
 def partner(values):
@@ -301,7 +331,7 @@
 def back_kernel(qkv_backs, pre_backs, slot_ref, *refs):
     lanes = refs[:qkv_backs]
     pre_back = jnp.concatenate([r[...] for r in refs[qkv_backs : qkv_backs + pre_backs]], axis=1)
-    qkv_ref, inner_ref, g1_ref, g2_ref, normed_ref, away_ref, own_ref, sums_ref = refs[qkv_backs + pre_backs :]
+    qkv_ref, inner_ref, g1_ref, g2_ref, away_rows_ref, own_rows_ref, away_ref, own_ref, sums_ref = refs[qkv_backs + pre_backs :]
     first = None
     for c in range(3):
         part = jnp.concatenate([r[:, c * PAIR : (c + 1) * PAIR] for r in lanes], axis=1)
@@ -309,7 +339,7 @@
         first = term if first is None else first + term
     second = dot(pre_back, inner_ref[...], NT)
     combined = first * g1_ref[...] + second * g2_ref[...]
-    normed = normed_ref[...]
+    normed, _ = normalize(jnp.where(pl.program_id(0) == 0, away_rows_ref[...], own_rows_ref[...]).astype(F32))
     sums = jnp.concatenate(
         [jnp.sum(v, axis=0, keepdims=True) for v in (first * normed, first, second * normed, second)], axis=0
     )
@@ -329,20 +359,21 @@
         own_ref[...] = combined
 
 
-def rows_call(kernel, here, sliced, whole, by_rows, own_type, sums, held, flops):
+def rows_call(kernel, here, sliced, whole, halves, own_type, sums, held, flops):
     rows = sliced[0].shape[0]
     width = whole[0].shape[-1] if whole[0].ndim == 2 else whole[0].shape[1]
     half = rows // 2
-    block = min(half, 256)
+    block = min(half, ROWS)
     count = half // block
     at = lambda j, i, slot: (slot[j] * count + i, 0)
     in_specs = [pl.BlockSpec((block, v.shape[1]), at) for v in sliced]
     in_specs += [pl.BlockSpec(v.shape, lambda j, i, slot, n=v.ndim: (0,) * n) for v in whole]
-    in_specs += [pl.BlockSpec((block, v.shape[1]), at) for v in by_rows]
-    out_specs = [
+    by_half = [
         pl.BlockSpec((block, width), lambda j, i, slot: (jnp.where(j == 0, i, count - 1), 0)),
         pl.BlockSpec((block, width), lambda j, i, slot: (jnp.where(j == 0, 0, i), 0)),
     ]
+    in_specs += by_half[: len(halves)]
+    out_specs = list(by_half)
     out_shape = [jax.ShapeDtypeStruct((half, width), BF16), jax.ShapeDtypeStruct((half, width), own_type)]
     if sums:
         out_specs.append(pl.BlockSpec((sums, width), lambda j, i, slot: (0, 0)))
@@ -355,7 +386,7 @@
         out_shape=out_shape,
         compiler_params=PARAMS,
         cost_estimate=pl.CostEstimate(flops=flops, bytes_accessed=16 * rows * width, transcendentals=0),
-    )(jnp.stack([1 - here, here]), *sliced, *whole, *by_rows, *held)
+    )(jnp.stack([1 - here, here]), *sliced, *whole, *halves, *held)
 
 
 def rings(size):
@@ -385,6 +416,9 @@
 
 def ring_reduce(values, size, ring):
     length = ring[1]
+    if isinstance(values, tuple):
+        yield [values[0]]
+        return add(hop(values[0], size, ring), values[1])
     if length == 1:
         return values
     at = position(ring)
@@ -453,41 +487,64 @@
     return (yield from together(ring_pieces(left, size, fast), ring_pieces(right, size, mid)))
 
 
-def place_kernel(count, tile, slot_ref, *refs):
-    out_ref = refs[-1]
-    for k in range(count):
-
-        @pl.when(pl.program_id(0) == k)
+def place_kernel(lefts, rights, kept, left_ref, right_ref, *refs):
+    pieces, (inner_ref, outer_ref, token_ref) = refs[: lefts + rights], refs[lefts + rights + kept :]
+    step = pl.program_id(0)
+    for k in range(lefts):
+
+        @pl.when(step == k)
         def _():
-            if tile:
-                for t in range(refs[k].shape[0] // tile):
-                    out_ref[:, t * tile : (t + 1) * tile] = refs[k][t * tile : (t + 1) * tile, :].astype(F32)
-            else:
-                out_ref[...] = refs[k][...].astype(F32)
-
-
-def place(total, shape, pieces, ring, at, across):
-    count = len(pieces)
-    rows, cols = pieces[0].shape
-    if across:
-        out_spec = pl.BlockSpec((cols, rows), lambda j, slot: (at, slot[j]))
-    else:
-        out_spec = pl.BlockSpec((rows, cols), lambda j, slot: (slot[j], at))
-    kernel = functools.partial(place_kernel, count, cols if across else 0)
-    extra = [] if total is None else [total]
+            inner_ref[...] = pieces[k][...].astype(F32)
+
+    for k in range(rights):
+
+        @pl.when(step == k)
+        def _():
+            outer_ref[...] = pieces[lefts + k][...].astype(F32)
+
+    token_ref[...] = jnp.zeros_like(token_ref)
+
+
+def place(totals, shapes, left, right, fast, mid, at):
+    cuts = 2
+    steps = max(len(left), len(right))
+    rows, cols = left[0].shape
+    tall, wide = right[0].shape
+
+    def taken(k, count):
+        return lambda j, i, a, b: (jnp.where(j == k, i, jnp.where(j < k, 0, cuts - 1)), 0)
+
+    def last(j, i, count):
+        return jnp.minimum(j, count - 1), jnp.where(j < count, i, cuts - 1)
+
+    def left_at(j, i, a, b):
+        j, i = last(j, i, len(left))
+        return a[j] * cuts + i, at
+
+    def right_at(j, i, a, b):
+        j, i = last(j, i, len(right))
+        return at * cuts + i, b[j]
+
+    kept = list(totals) if totals else []
     return pl.pallas_call(
-        after(kernel, 1 + count, len(extra)),
+        functools.partial(place_kernel, len(left), len(right), len(kept)),
         grid_spec=pltpu.PrefetchScalarGridSpec(
-            num_scalar_prefetch=1,
-            grid=(count,),
-            in_specs=[pl.BlockSpec((rows, cols), lambda j, slot: (0, 0))] * count + [ANY] * len(extra),
-            out_specs=out_spec,
+            num_scalar_prefetch=2,
+            grid=(steps, cuts),
+            in_specs=[pl.BlockSpec((rows // cuts, cols), taken(k, len(left))) for k in range(len(left))]
+            + [pl.BlockSpec((tall // cuts, wide), taken(k, len(right))) for k in range(len(right))]
+            + [ANY] * len(kept),
+            out_specs=[
+                pl.BlockSpec((rows // cuts, cols), left_at),
+                pl.BlockSpec((tall // cuts, wide), right_at),
+                pl.BlockSpec((8, 128), lambda j, i, a, b: (0, 0)),
+            ],
         ),
-        out_shape=jax.ShapeDtypeStruct(shape, F32),
-        input_output_aliases={1 + count: 0} if extra else {},
+        out_shape=[jax.ShapeDtypeStruct(shape, F32) for shape in shapes] + [jax.ShapeDtypeStruct((8, 128), F32)],
+        input_output_aliases={2 + len(left) + len(right) + k: k for k in range(len(kept))},
         compiler_params=PARAMS,
-        cost_estimate=pl.CostEstimate(flops=0, bytes_accessed=6 * count * rows * cols, transcendentals=0),
-    )(jnp.stack(slots_of(ring)), *pieces, *extra)
+        cost_estimate=pl.CostEstimate(flops=0, bytes_accessed=12 * len(left) * rows * cols, transcendentals=0),
+    )(jnp.stack(slots_of(fast)), jnp.stack(slots_of(mid)), *left, *right, *kept)
 
 
 def butterfly(values, axis, size):
@@ -501,22 +558,23 @@
 
 
 class Rounds:
-    def __init__(self):
+    def __init__(self, finish):
         self.live = []
-        self.done = {}
-
-    def add(self, name, steps):
-        self.live.append((name, steps))
+        self.finish = finish
+        self.block = []
+
+    def add(self, at, steps):
+        self.live.append((at, steps))
 
     def turn(self):
-        held = []
+        held = self.block
         left = []
-        for name, steps in self.live:
+        for at, steps in self.live:
             try:
-                held += next(steps)
-                left.append((name, steps))
+                held = held + next(steps)
+                left.append((at, steps))
             except StopIteration as stop:
-                self.done[name] = stop.value
+                held = held + [self.finish(at, *stop.value)]
         self.live = left
         return held
 
@@ -578,43 +636,52 @@
         other_cot = lax.ppermute(cotangent, "tensor", swap)
         parts = (residual, other, cotangent, other_cot)
         order = here
+        row_halves = [other, residual]
     else:
         gathered = lax.all_gather(residual, "tensor", axis=0, tiled=True)
         gathered_cot = lax.all_gather(cotangent, "tensor", axis=0, tiled=True)
         middle = gathered.shape[0] // 2
         parts = (gathered[:middle], gathered[middle:], gathered_cot[:middle], gathered_cot[middle:])
+        row_halves = list(parts[:2])
         order = jnp.int32(0)
-    normed, first_in, second_in, cot = prep(*parts, order, (norm1_gain, norm1_bias, norm2_gain, norm2_bias))
+    first_in, second_in, cot = prep(*parts, order, (norm1_gain, norm1_bias, norm2_gain, norm2_bias))
     rows = cot.shape[0]
 
-    rounds = Rounds()
+    _, mid, fast = rings(dp_size)
+    totals = []
+
+    def finish(at, left, right):
+        inner, outer, token = place(totals, [(width, hidden), (hidden, width)], left, right, fast, mid, at)
+        totals[:] = [inner, outer]
+        return token
+
+    rounds = Rounds(finish)
     ffn = []
+    attn = []
     steps = hidden // HIDDEN
     per = max(1, steps // 4)
 
     def feed_forward():
-        at = len(ffn) * per
-        held = rounds.turn()
-        out = ffn_slice(second_in, cot, inner_weight, inner_bias.reshape(1, -1), outer_weight, at, per, held)
-        rounds.add(len(ffn), reduce_over_dp(out[2], out[3].reshape(width, per * HIDDEN), dp_size))
+        out = ffn_slice(
+            second_in, cot, inner_weight, inner_bias.reshape(1, -1), outer_weight, len(ffn) * per, per, fast, mid,
+            rounds.turn(),
+        )
+        rounds.block = [out[2]]
+        rounds.add(len(ffn), reduce_over_dp(out[3], out[4], dp_size))
         ffn.append(out)
 
-    early = (steps // per + 1) // 2
-    for _ in range(early):
+    for _ in range(FIRST):
         feed_forward()
-
-    lengths, late_qkv, _ = lax.optimization_barrier((seq_lengths, qkv_weight, ffn[0][4]))
-    segment, places = layout(lengths[0], rows)
+    segment, places = layout(seq_lengths[0], rows)
     cosine, sine = rotary_tables(places)
-    qkv = jnp.transpose(late_qkv, (1, 0, 2))
-    attn = []
+    qkv = jnp.transpose(qkv_weight, (1, 0, 2))
     for pair in range(head_width // PAIR):
-        held = rounds.turn()
-        attn.append(
-            attention_pair(
-                first_in, cot, qkv, qkv_bias.reshape(3, 1, -1), dense_weight, cosine, sine, segment, slots, pair, held
-            )
+        out = attention_pair(
+            first_in, cot, qkv, qkv_bias.reshape(3, 1, -1), dense_weight, cosine, sine, segment, slots, pair,
+            rounds.turn(),
         )
+        rounds.block = [out[4]]
+        attn.append(out)
     attn_sums = lax.psum(([a[2] for a in attn], [a[3] for a in attn]), "dp")
     while len(ffn) * per < steps:
         feed_forward()
@@ -625,10 +692,11 @@
         functools.partial(branch_kernel, len(attn), len(ffn)), order, [a[0] for a in attn] + [f[0] for f in ffn],
         [dense_weight, outer_weight], [], BF16, 0, held, 2 * rows * width * (head_width + hidden),
     )
-    held = rounds.turn()
+    rounds.block = []
+    held = rounds.turn() + [branch_away]
     away, own, sums = rows_call(
         functools.partial(back_kernel, len(attn), len(ffn)), order, [a[1] for a in attn] + [f[1] for f in ffn],
-        [qkv, inner_weight, norm1_gain.reshape(1, -1), norm2_gain.reshape(1, -1)], [normed], F32, 4, held,
+        [qkv, inner_weight, norm1_gain.reshape(1, -1), norm2_gain.reshape(1, -1)], row_halves, F32, 4, held,
         2 * rows * width * (3 * head_width + hidden),
     )
     if tensor_size == 2:
@@ -653,20 +721,14 @@
     over_all = jnp.concatenate([sums, jnp.sum(cotangent.astype(F32), axis=0, keepdims=True)], axis=0).reshape(-1)
     over_all = butterfly(over_all, "tensor", tensor_size)
     qkvbias = jnp.concatenate([a[4].reshape(3, PAIR) for a in attn], axis=1).reshape(-1)
-    innerbias = jnp.concatenate([f[4] for f in ffn], axis=1).reshape(-1)
+    innerbias = jnp.concatenate([f[2] for f in ffn], axis=1).reshape(-1)
     vectors = butterfly(jnp.concatenate([over_all, qkvbias, innerbias]), "dp", dp_size)
     ends = [width * i for i in range(1, 6)] + [5 * width + 3 * head_width]
     gain1_grad, bias1_grad, gain2_grad, bias2_grad, outbias_grad, qkvbias_grad, innerbias_grad = jnp.split(vectors, ends)
 
     while rounds.live:
         rounds.turn()
-    _, mid, fast = rings(dp_size)
-    inner_grad = None
-    outer_grad = None
-    for k in range(len(ffn)):
-        left, right = rounds.done[k]
-        inner_grad = place(inner_grad, (width, hidden), left, fast, k, False)
-        outer_grad = place(outer_grad, (hidden, width), right, mid, k, True)
+    inner_grad, outer_grad = totals
     qkv_sums, dense_sums = attn_sums
     qkv_grad = jnp.concatenate([g.transpose(1, 0, 2) for g in qkv_sums], axis=2).astype(F32)
     dense_grad = jnp.concatenate(dense_sums, axis=0).astype(F32)

time: 441 us -> 395 us (0.90)
  waiting for transfers between devices: 149 us -> 112 us
  starting transfers between devices: 53.7 us -> 69.4 us
  local copies, waits for them, and re-layouts: 23.3 us -> 10.2 us
  other arithmetic: 38.2 us -> 30.2 us
    ppermute x32, waiting for transfers between devices: 87.4 us -> 43.6 us  [hop(): return lax.ppermute(values, 'dp', pairs)]
    ppermute x32, starting transfers between devices: 36.4 us -> 58.1 us  [hop(): return lax.ppermute(values, 'dp', pairs)]
    dynamic_slice x16 -> x8, local copies, waits for them, and re-layouts: 13.5 us -> 0.21 us  [rows_of(): return lax.dynamic_slice_in_dim(values, index * rows, rows, 0)]
    ppermute x5, waiting for transfers between devices: 5.45 us -> 13.1 us  [butterfly(): lax.ppermute(values, axis, [(i, i ^ step) for i in range(size)])]
    pallas_call x12 -> x8, Pallas kernels: 61.9 us -> 59.8 us  [the longest x4 39 us: ffn_slice(): pl.pallas_call(after(ffn_kernel, 6, len(held)), grid_spec=pltpu.PrefetchS...]
  transfers between devices with their start and end apart: 50 -> 50, of which waited for: 16 -> 17; matrix products, arithmetic and copies ran while one was open for 10% -> 7% of each run, Pallas kernels for 30% -> 35%
where the time goes in v3:
time: 395 us; the launch traced here: 389 us
  Pallas kernels  152 us (38%)
  waiting for transfers between devices  112 us (28%)
  starting transfers between devices  69.4 us (18%)
  other arithmetic  30.2 us (8%)
  between operations  15.3 us (4%)
  local copies, waits for them, and re-layouts  10.2 us (3%)
    ppermute x32, starting transfers between devices, hop(): return lax.ppermute(values, 'dp', pairs)  58.1 us
    pallas_call x4, Pallas kernels, attention_pair(): pl.pallas_call(after(functools.partial(attention_kernel, slots), 9, len(h...  56.5 us
    ppermute x8, waiting for transfers between devices, reduce_over_dp(): lax.ppermute(both, 'dp', [(i, i ^ step * slow[0]) for i in range(size)])  55.5 us
    ppermute x32, waiting for transfers between devices, hop(): return lax.ppermute(values, 'dp', pairs)  43.6 us
    pallas_call x4, Pallas kernels, ffn_slice(): pl.pallas_call(after(ffn_kernel, 6, len(held)), grid_spec=pltpu.PrefetchS...  39 us
    pallas_call x2, Pallas kernels, rows_call(): pl.pallas_call(after(kernel, 1 + len(in_specs), len(held)), grid_spec=plt...  28.9 us
    pallas_call x4, Pallas kernels, place(): pl.pallas_call(functools.partial(place_kernel, len(left), len(right), len...  20.7 us
    ppermute x5, waiting for transfers between devices, butterfly(): lax.ppermute(values, axis, [(i, i ^ step) for i in range(size)])  13.1 us
  transfers between devices with their start and end apart: 50, of which 17 were waited for; matrix products, arithmetic and copies ran while one was open for 7% of the time, Pallas kernels for 35%

profile of v3, /device:TPU:0, one launch (start us, length us, event | category | flops | bytes accessed | tf_op | source)
XLA Modules:
  0.0 389.4 jit_solution(11260697201555927958)
XLA Ops:
  10.1 1.4 convert_reduce_fusion
  11.5 1.6 fusion.7
  14.5 6.7 %shard_map.237 = (bf16[1024,1024]{1,0:T(8,128)(2,1)}, bf16[1024,1024]{1,0:T(8,128)(2,1)}, bf16[1024,1024]{1,0:T(8,128)(2,1)}) custom-call(s32[2]{0:T(128)} %get-tuple-element.197.slot_ref, bf16[512,1024]{1,0:T(8,128)(2,1)} %refs_14_.1, bf16[512,1024]{1,0:T(8,128)(2,1)} %copy-done.11, bf16[512,1024]{1,0:T(8,128)(2,1)} %own_cot_ref.1, ...), custom_call_target="tpu_custom_call" | custom-call | flops 20971520 | bytes 10485760 | tf_op jit(solution)/shard_map/pallas_call | solution.py:68
  21.3 9.5 %shard_map.238 = (bf16[1024,512]{1,0:T(8,128)(2,1)}, bf16[1024,512]{1,0:T(8,128)(2,1)}, f32[1,512]{1,0:T(1,128)}, bf16[512,512]{1,0:T(8,128)(2,1)}, bf16[512,512...) custom-call(s32[2]{0:T(128)} %get-tuple-element.198.refs_0_, ...), custom_call_target="tpu_custom_call" | custom-call | flops 4294967296 | bytes 10485760 | tf_op jit(solution)/shard_map/pallas_call | solution.py:147
  30.8 3.0 collective-permute-start.3
  33.8 3.3 fusion.12
  37.2 1.6 collective-permute-start.2
  40.0 6.2 %collective-permute-done.3 = bf16[512,512]{1,0:T(8,128)(2,1)S(1)} collective-permute-done((bf16[512,512]{1,0:T(8,128)(2,1)}, bf16[512,512]{1,0:T(8,128)(2,1)S(1)}, u32[]{:S(2)}, u32[]{:S(2)}) %collective-permute-start.3) | collective-permute-done | bytes 524320 | tf_op jit(solution)/shard_map/ppermute | solution.py:405
  46.2 1.2 add_convert_fusion.14
  47.4 1.8 collective-permute-start.5
  49.2 3.0 collective-permute-done.2
  53.7 1.1 copy.37.refs_7_
  54.8 1.9 collective-permute-done.5
  56.8 2.1 collective-permute-done.4
  59.1 1.6 collective-permute-start.6
  60.7 13.9 %shard_map.239 = (bf16[1024,128]{1,0:T(8,128)(2,1)}, bf16[1024,384]{1,0:T(8,128)(2,1)}, bf16[3,1024,128]{2,1,0:T(8,128)(2,1)}, bf16[128,1024]{1,0:T(8,128)(2,1)}, f32[1,384]{1,0:T(1,128)}) custom-call(bf16[1024,1024]{1,0:T(8,128)(2,1)} %get-tuple-element.78.refs_0_, bf16[1024,1024]{1,0:T(8,128)(2,1)} %get-tuple-element.79.refs_2_.refs_1_, ...), custom_call_target="tpu_custom_call" | custom-call | flops 4026531840 | bytes 2097152 | tf_op jit(solution)/shard_map/pallas_call | solution.py:273
  75.3 14.4 %shard_map.240 = (bf16[1024,128]{1,0:T(8,128)(2,1)}, bf16[1024,384]{1,0:T(8,128)(2,1)}, bf16[3,1024,128]{2,1,0:T(8,128)(2,1)}, bf16[128,1024]{1,0:T(8,128)(2,1)}, f32[1,384]{1,0:T(1,128)}) custom-call(bf16[1024,1024]{1,0:T(8,128)(2,1)} %get-tuple-element.78.refs_0_, bf16[1024,1024]{1,0:T(8,128)(2,1)} %get-tuple-element.79.refs_2_.refs_1_, ...), custom_call_target="tpu_custom_call" | custom-call | flops 4026531840 | bytes 2097152 | tf_op jit(solution)/shard_map/pallas_call | solution.py:273
  90.6 2.6 collective-permute-start.7
  93.2 14.1 %shard_map.241 = (bf16[1024,128]{1,0:T(8,128)(2,1)}, bf16[1024,384]{1,0:T(8,128)(2,1)}, bf16[3,1024,128]{2,1,0:T(8,128)(2,1)}, bf16[128,1024]{1,0:T(8,128)(2,1)}, f32[1,384]{1,0:T(1,128)}) custom-call(bf16[1024,1024]{1,0:T(8,128)(2,1)} %get-tuple-element.78.refs_0_, bf16[1024,1024]{1,0:T(8,128)(2,1)} %get-tuple-element.79.refs_2_.refs_1_, ...), custom_call_target="tpu_custom_call" | custom-call | flops 4026531840 | bytes 2097152 | tf_op jit(solution)/shard_map/pallas_call | solution.py:273
  108.0 14.1 %shard_map.242 = (bf16[1024,128]{1,0:T(8,128)(2,1)}, bf16[1024,384]{1,0:T(8,128)(2,1)}, bf16[3,1024,128]{2,1,0:T(8,128)(2,1)}, bf16[128,1024]{1,0:T(8,128)(2,1)}, f32[1,384]{1,0:T(1,128)}) custom-call(bf16[1024,1024]{1,0:T(8,128)(2,1)} %get-tuple-element.78.refs_0_, bf16[1024,1024]{1,0:T(8,128)(2,1)} %get-tuple-element.79.refs_2_.refs_1_, ...), custom_call_target="tpu_custom_call" | custom-call | flops 4026531840 | bytes 2097152 | tf_op jit(solution)/shard_map/pallas_call | solution.py:273
  123.2 1.6 collective-permute-start.9
  124.8 10.2 %shard_map.243 = (bf16[1024,512]{1,0:T(8,128)(2,1)}, bf16[1024,512]{1,0:T(8,128)(2,1)}, f32[1,512]{1,0:T(1,128)}, bf16[512,512]{1,0:T(8,128)(2,1)}, bf16[512,512...) custom-call(s32[2]{0:T(128)} %get-tuple-element.198.refs_0_, ...), custom_call_target="tpu_custom_call" | custom-call | flops 4294967296 | bytes 10485760 | tf_op jit(solution)/shard_map/pallas_call | solution.py:147
  135.9 2.0 collective-permute-start.13
  138.1 1.1 collective-permute-start.10
  140.1 9.6 %shard_map.244 = (bf16[1024,512]{1,0:T(8,128)(2,1)}, bf16[1024,512]{1,0:T(8,128)(2,1)}, f32[1,512]{1,0:T(1,128)}, bf16[512,512]{1,0:T(8,128)(2,1)}, bf16[512,512...) custom-call(s32[2]{0:T(128)} %get-tuple-element.198.refs_0_, ...), custom_call_target="tpu_custom_call" | custom-call | flops 4294967296 | bytes 10485760 | tf_op jit(solution)/shard_map/pallas_call | solution.py:147
  149.7 1.4 collective-permute-start.17
  151.1 4.3 %collective-permute-done.13 = bf16[512,512]{1,0:T(8,128)(2,1)S(1)} collective-permute-done((bf16[512,512]{1,0:T(8,128)(2,1)}, bf16[512,512]{1,0:T(8,128)(2,1)S(1)}, u32[]{:S(2)}, u32[]{:S(2)}) %collective-permute-start.13) | collective-permute-done | bytes 524320 | tf_op jit(solution)/shard_map/ppermute | solution.py:405
  155.4 1.1 collective-permute-start.16
  157.8 24.2 %collective-permute-done.17 = bf16[512,512]{1,0:T(8,128)(2,1)S(1)} collective-permute-done((bf16[512,512]{1,0:T(8,128)(2,1)}, bf16[512,512]{1,0:T(8,128)(2,1)S(1)}, u32[]{:S(2)}, u32[]{:S(2)}) %collective-permute-start.17) | collective-permute-done | bytes 524320 | tf_op jit(solution)/shard_map/ppermute | solution.py:405
  183.4 2.1 collective-permute-start.20
  186.2 5.2 %shard_map.245 = (f32[1024,2048]{1,0:T(8,128)}, f32[2048,1024]{1,0:T(8,128)}, f32[8,128]{1,0:T(8,128)}) custom-call(s32[2]{0:T(128)} %pad_add_fusion.3.left_ref, s32[2]{0:T(128)} %pad_add_fusion.4.right_ref, bf16[512,512]{1,0:T(8,128)(2,1)} %copy-done.9, bf16[512,512]{1,0:T(8,128)(2,1)} %copy-done.27, bf16[512,512]{1,0:T(8,128)(2,1)} %copy-done.10, ...), custom_call_target="tpu_custom_call" | custom-call | bytes 6291456 | tf_op jit(solution)/shard_map/pallas_call | solution.py:529
  191.5 9.7 %shard_map.246 = (bf16[1024,512]{1,0:T(8,128)(2,1)}, bf16[1024,512]{1,0:T(8,128)(2,1)}, f32[1,512]{1,0:T(1,128)}, bf16[512,512]{1,0:T(8,128)(2,1)}, bf16[512,512...) custom-call(s32[2]{0:T(128)} %get-tuple-element.198.refs_0_, ...), custom_call_target="tpu_custom_call" | custom-call | flops 4294967296 | bytes 10485760 | tf_op jit(solution)/shard_map/pallas_call | solution.py:147
  201.1 1.2 collective-permute-start.22
  205.1 12.2 %shard_map.247 = (bf16[512,1024]{1,0:T(8,128)(2,1)}, bf16[512,1024]{1,0:T(8,128)(2,1)}) custom-call(s32[2]{0:T(128)} %pad_add_fusion.refs_0_, bf16[1024,128]{1,0:T(8,128)(2,1)} %get-tuple-element.84.refs_1_, bf16[1024,128]{1,0:T(8,128)(2,1)} %get-tuple-element.88.refs_2_, bf16[1024,128]{1,0:T(8,128)(2,1)} %get-tuple-element.90.refs_3_, ...), custom_call_target="tpu_custom_call" | custom-call | flops 5368709120 | bytes 16777216 | tf_op jit(solution)/shard_map/pallas_call | solution.py:381
  217.7 1.4 collective-permute-start.38
  220.3 1.2 collective-permute-start.30
  222.4 16.7 %shard_map.248 = (bf16[512,1024]{1,0:T(8,128)(2,1)}, f32[512,1024]{1,0:T(8,128)}, f32[4,1024]{1,0:T(4,128)}) custom-call(s32[2]{0:T(128)} %pad_add_fusion.refs_0_, bf16[1024,384]{1,0:T(8,128)(2,1)} %get-tuple-element.114.refs_1_, bf16[1024,384]{1,0:T(8,128)(2,1)} %get-tuple-element.115.refs_2_, bf16[1024,384]{1,0:T(8,128)(2,1)} %get-tuple-element.116.refs_3_, ...), custom_call_target="tpu_custom_call" | custom-call | flops 7516192768 | bytes 16777216 | tf_op jit(solution)/shard_map/pallas_call | solution.py:381
  240.3 3.2 collective-permute-done.38
  243.6 1.5 collective-permute-start.39
  245.1 8.0 %collective-permute-done.44 = bf16[2,256,512]{2,1,0:T(8,128)(2,1)S(1)} collective-permute-done((bf16[2,256,512]{2,1,0:T(8,128)(2,1)S(1)}, bf16[2,256,512]{2,1,0:T(8,128)(2,1)S(1)}, u32[]{:S(2)}, u32[]{:S(2)}) %collective-permute-start.44) | collective-permute-done | bytes 524320 | tf_op jit(solution)/shard_map/ppermute | solution.py:483
  253.3 1.7 collective-permute-start.47
  255.0 18.3 %collective-permute-done.32 = bf16[2,256,512]{2,1,0:T(8,128)(2,1)S(1)} collective-permute-done((bf16[2,256,512]{2,1,0:T(8,128)(2,1)S(1)}, bf16[2,256,512]{2,1,0:T(8,128)(2,1)S(1)}, u32[]{:S(2)}, u32[]{:S(2)}) %collective-permute-start.32) | collective-permute-done | bytes 524320 | tf_op jit(solution)/shard_map/ppermute | solution.py:483
  273.2 1.2 collective-permute-start.45
  274.5 7.0 %collective-permute-done.39 = bf16[2,256,512]{2,1,0:T(8,128)(2,1)S(1)} collective-permute-done((bf16[2,256,512]{2,1,0:T(8,128)(2,1)S(1)}, bf16[2,256,512]{2,1,0:T(8,128)(2,1)S(1)}, u32[]{:S(2)}, u32[]{:S(2)}) %collective-permute-start.39) | collective-permute-done | bytes 524320 | tf_op jit(solution)/shard_map/ppermute | solution.py:483
  282.6 1.3 collective-permute-start.42
  283.8 17.8 %collective-permute-start.40 = (bf16[256,512]{1,0:T(8,128)(2,1)}, bf16[256,512]{1,0:T(8,128)(2,1)}, u32[]{:S(2)}, u32[]{:S(2)}) collective-permute-start(bf16[256,512]{1,0:T(8,128)(2,1)} %get-tuple-element.179), channel_id=1, source_target_pairs={{0,4},{2,6},{4,0},{6,2},{8,12},{10,14},{12,8},{14,10},{16,20},{18,... | collective-permute-start | bytes 786440 | tf_op jit(solution)/shard_map/ppermute | solution.py:405
  301.8 2.0 collective-permute-start.46
  305.4 2.6 convert_reduce_fusion.1
  308.1 1.1 collective-permute-done.40
  309.2 1.1 broadcast_select_fusion.5
  310.3 2.0 collective-permute-start.26
  312.3 19.1 %collective-permute-done.33 = bf16[2,256,512]{2,1,0:T(8,128)(2,1)} collective-permute-done((bf16[2,256,512]{2,1,0:T(8,128)(2,1)S(1)}, bf16[2,256,512]{2,1,0:T(8,128)(2,1)}, u32[]{:S(2)}, u32[]{:S(2)}) %collective-permute-start.33) | collective-permute-done | bytes 524320 | tf_op jit(solution)/shard_map/ppermute | solution.py:483
  331.4 1.2 add_convert_fusion.3
  333.7 5.9 %collective-permute-start.34 = (bf16[256,512]{1,0:T(8,128)(2,1)S(1)}, bf16[256,512]{1,0:T(8,128)(2,1)S(1)}, u32[]{:S(2)}, u32[]{:S(2)}) collective-permute-start(bf16[256,512]{1,0:T(8,128)(2,1)S(1)} %get-tuple-element.183), channel_id=1, source_target_pairs={{0,4},{2,6},{4,0},{6,2},{8,12},{10,14},{12,8},{14,10},{16,20},{18,... | collective-permute-start | bytes 786440 | tf_op jit(solution)/shard_map/ppermute | solution.py:405
  339.7 4.6 %collective-permute-done.27 = f32[8704]{0:T(1024)S(1)} collective-permute-done((f32[8704]{0:T(1024)S(1)}, f32[8704]{0:T(1024)S(1)}, u32[]{:S(2)}, u32[]{:S(2)}) %collective-permute-start.27) | collective-permute-done | bytes 34848 | tf_op jit(solution)/shard_map/ppermute | solution.py:555
  344.4 3.9 %collective-permute-done.28 = f32[8704]{0:T(1024)S(1)} collective-permute-done((f32[8704]{0:T(1024)S(1)}, f32[8704]{0:T(1024)S(1)}, u32[]{:S(2)}, u32[]{:S(2)}) %collective-permute-start.28) | collective-permute-done | bytes 34848 | tf_op jit(solution)/shard_map/ppermute | solution.py:555
  348.3 1.9 collective-permute-start.41
  350.3 2.1 collective-permute-start.43
  352.6 4.6 %collective-permute-done.29 = f32[8704]{0:T(1024)S(1)} collective-permute-done((f32[8704]{0:T(1024)S(1)}, f32[8704]{0:T(1024)S(1)}, u32[]{:S(2)}, u32[]{:S(2)}) %collective-permute-start.29) | collective-permute-done | bytes 34848 | tf_op jit(solution)/shard_map/ppermute | solution.py:555
  359.3 5.2 %shard_map.249 = (f32[1024,2048]{1,0:T(8,128)}, f32[2048,1024]{1,0:T(8,128)}, f32[8,128]{1,0:T(8,128)}) custom-call(s32[2]{0:T(128)} %pad_add_fusion.3.left_ref, s32[2]{0:T(128)} %pad_add_fusion.4.right_ref, bf16[512,512]{1,0:T(8,128)(2,1)} %copy-done.3, ...), custom_call_target="tpu_custom_call", output_to_operand_aliasing={{0}: (6, {}), {1}: (7, {})} | custom-call | bytes 6291456 | tf_op jit(solution)/shard_map/pallas_call | solution.py:529
  364.9 5.2 %shard_map.250 = (f32[1024,2048]{1,0:T(8,128)}, f32[2048,1024]{1,0:T(8,128)}, f32[8,128]{1,0:T(8,128)}) custom-call(s32[2]{0:T(128)} %pad_add_fusion.3.left_ref, s32[2]{0:T(128)} %pad_add_fusion.4.right_ref, bf16[512,512]{1,0:T(8,128)(2,1)} %copy-done.5, ...), custom_call_target="tpu_custom_call", output_to_operand_aliasing={{0}: (6, {}), {1}: (7, {})} | custom-call | bytes 6291456 | tf_op jit(solution)/shard_map/pallas_call | solution.py:529
  371.2 5.2 %shard_map.251 = (f32[1024,2048]{1,0:T(8,128)}, f32[2048,1024]{1,0:T(8,128)}, f32[8,128]{1,0:T(8,128)}) custom-call(s32[2]{0:T(128)} %pad_add_fusion.3.left_ref, s32[2]{0:T(128)} %pad_add_fusion.4.right_ref, bf16[512,512]{1,0:T(8,128)(2,1)} %copy-done.7, ...), custom_call_target="tpu_custom_call", output_to_operand_aliasing={{0}: (6, {}), {1}: (7, {})} | custom-call | bytes 6291456 | tf_op jit(solution)/shard_map/pallas_call | solution.py:529
  376.4 4.3 %maximum_convert_fusion = f32[1024,3,512]{2,0,1:T(8,128)} fusion(bf16[1024,3,128]{2,0,1:T(8,128)(2,1)} %get-tuple-element.145, bf16[1024,3,128]{2,0,1:T(8,128)(2,1)} %get-tuple-element.146, bf16[1024,3,128]{2,0,1:T(8,128)(2,1)} %get-tuple-element.147, bf16[1024,3,128]{2,0,1:T(8,128)(2,1)} %get-tuple-element.148), kind=kLoop, calls=%fused_computation | loop fusion | flops 12582912 | bytes 9437184 | tf_op jit(solution)/shard_map/convert_element_type | solution.py:733
  380.8 1.6 maximum_convert_fusion.1
  (246 shorter events, 30.3 us)
Async XLA Ops:
  7.2 369.2 %all-reduce.3.cloned.1.call-start = ((), (), s32[]{:S(2)}) async-start(), calls=%async_computation | async-start | bytes 8388608 | tf_op jit(solution)/shard_map/psum | solution.py:685
  7.2 6.0 %collective-permute-start = (bf16[512,1024]{1,0:T(8,128)(2,1)}, bf16[512,1024]{1,0:T(8,128)(2,1)S(1)}, u32[]{:S(2)}, u32[]{:S(2)}) collective-permute-start(bf16[512,1024]{1,0:T(8,128)(2,1)} %refs_14_.1), channel_id=1, source_target_pairs={{0,1},{1,0},{2,3},{3,2},{4,5},{5,4},{6,7},{7,6},{8,9},{9,8},{10,11... | collective-permute-start | bytes 3145736 | tf_op jit(solution)/shard_map/ppermute | solution.py:635
  7.7 5.5 %collective-permute-start.1 = (bf16[512,1024]{1,0:T(8,128)(2,1)}, bf16[512,1024]{1,0:T(8,128)(2,1)S(1)}, u32[]{:S(2)}, u32[]{:S(2)}) collective-permute-start(bf16[512,1024]{1,0:T(8,128)(2,1)} %own_cot_ref.1), channel_id=1, source_target_pairs={{0,1},{1,0},{2,3},{3,2},{4,5},{5,4},{6,7},{7,6},{8,9},{9,8},{10,11... | collective-permute-start | bytes 3145736 | tf_op jit(solution)/shard_map/ppermute | solution.py:636
  9.4 44.3 %copy-start.43 = (s32[1024]{0:T(1024)}, s32[1024]{0:T(1024)S(1)}, u32[]{:S(2)}) copy-start(s32[1024]{0:T(1024)S(1)} %convert_reduce_fusion.2) | copy-start | bytes 12292
  30.8 21.5 %copy-start.14 = (bf16[512,512]{1,0:T(8,128)(2,1)S(1)}, bf16[512,512]{1,0:T(8,128)(2,1)}, u32[]{:S(2)}) copy-start(bf16[512,512]{1,0:T(8,128)(2,1)} %get-tuple-element.86) | copy-start | bytes 1572868
  30.8 15.4 %collective-permute-start.3 = (bf16[512,512]{1,0:T(8,128)(2,1)}, bf16[512,512]{1,0:T(8,128)(2,1)S(1)}, u32[]{:S(2)}, u32[]{:S(2)}) collective-permute-start(bf16[512,512]{1,0:T(8,128)(2,1)} %get-tuple-element.83.refs_11_), channel_id=1, source_target_pairs={{0,4},{2,6},{4,0},{6,2},{8,12},{10,14},{12,8},{14,10},{16,20},{18,... | collective-permute-start | bytes 1572872 | tf_op jit(solution)/shard_map/ppermute | solution.py:405
  37.2 15.1 %collective-permute-start.2 = (bf16[512,512]{1,0:T(8,128)(2,1)}, bf16[512,512]{1,0:T(8,128)(2,1)S(1)}, u32[]{:S(2)}, u32[]{:S(2)}) collective-permute-start(bf16[512,512]{1,0:T(8,128)(2,1)} %get-tuple-element.82.refs_10_), channel_id=1, source_target_pairs={{0,2},{2,0},{4,6},{6,4},{8,10},{10,8},{12,14},{14,12},{16,18},{18,... | collective-permute-start | bytes 1572872 | tf_op jit(solution)/shard_map/ppermute | solution.py:405
  47.4 9.3 %collective-permute-start.5 = (bf16[256,512]{1,0:T(8,128)(2,1)S(1)}, bf16[256,512]{1,0:T(8,128)(2,1)S(1)}, u32[]{:S(2)}, u32[]{:S(2)}) collective-permute-start(bf16[256,512]{1,0:T(8,128)(2,1)S(1)} %constant_dynamic-slice_fusion.6.refs_11_), channel_id=1, source_target_pairs={{0,2},{2,0},{4,6},{6,4},{8,10},{10,8},{12,14},{14,12},{16,18},{18,... | collective-permute-start | bytes 786440 | tf_op jit(solution)/shard_map/ppermute | solution.py:405
  52.4 22.1 %copy-start.38 = (bf16[256,512]{1,0:T(8,128)(2,1)}, bf16[256,512]{1,0:T(8,128)(2,1)S(1)}, u32[]{:S(2)}) copy-start(bf16[256,512]{1,0:T(8,128)(2,1)S(1)} %constant_dynamic-slice_fusion.7.refs_10_) | copy-start | bytes 786436
  52.5 6.4 %collective-permute-start.4 = (bf16[256,512]{1,0:T(8,128)(2,1)S(1)}, bf16[256,512]{1,0:T(8,128)(2,1)S(1)}, u32[]{:S(2)}, u32[]{:S(2)}) collective-permute-start(bf16[256,512]{1,0:T(8,128)(2,1)S(1)} %constant_dynamic-slice_fusion.7.refs_10_), channel_id=1, source_target_pairs={{0,4},{2,6},{4,0},{6,2},{8,12},{10,14},{12,8},{14,10},{16,20},{18,... | collective-permute-start | bytes 786440 | tf_op jit(solution)/shard_map/ppermute | solution.py:405
  59.0 15.6 %copy-start.26 = (bf16[2,256,512]{2,1,0:T(8,128)(2,1)}, bf16[2,256,512]{2,1,0:T(8,128)(2,1)S(1)}, u32[]{:S(2)}) copy-start(bf16[2,256,512]{2,1,0:T(8,128)(2,1)S(1)} %pad_maximum_fusion.refs_10_) | copy-start | bytes 1572868
  59.1 31.4 %collective-permute-start.6 = (bf16[2,256,512]{2,1,0:T(8,128)(2,1)S(1)}, bf16[2,256,512]{2,1,0:T(8,128)(2,1)S(1)}, u32[]{:S(2)}, u32[]{:S(2)}) collective-permute-start(bf16[2,256,512]{2,1,0:T(8,128)(2,1)S(1)} %pad_maximum_fusion.refs_10_), channel_id=1, source_target_pairs={{0,8},{2,10},{4,12},{6,14},{8,0},{10,2},{12,4},{14,6},{16,24},{18,... | collective-permute-start | bytes 1572872 | tf_op jit(solution)/shard_map/ppermute | solution.py:483
  90.6 16.8 %copy-start.22 = (bf16[2,256,512]{2,1,0:T(8,128)(2,1)}, bf16[2,256,512]{2,1,0:T(8,128)(2,1)S(1)}, u32[]{:S(2)}) copy-start(bf16[2,256,512]{2,1,0:T(8,128)(2,1)S(1)} %add_convert_fusion.13.refs_10_) | copy-start | bytes 1572868
  90.6 32.3 %collective-permute-start.7 = (bf16[2,256,512]{2,1,0:T(8,128)(2,1)S(1)}, bf16[2,256,512]{2,1,0:T(8,128)(2,1)S(1)}, u32[]{:S(2)}, u32[]{:S(2)}) collective-permute-start(bf16[2,256,512]{2,1,0:T(8,128)(2,1)S(1)} %add_convert_fusion.13.refs_10_), channel_id=1, source_target_pairs={{0,16},{2,18},{4,20},{6,22},{8,24},{10,26},{12,28},{14,30},{16,0},... | collective-permute-start | bytes 1572872 | tf_op jit(solution)/shard_map/ppermute | solution.py:483
  123.2 14.7 %collective-permute-start.9 = (bf16[256,512]{1,0:T(8,128)(2,1)S(1)}, bf16[256,512]{1,0:T(8,128)(2,1)S(1)}, u32[]{:S(2)}, u32[]{:S(2)}) collective-permute-start(bf16[256,512]{1,0:T(8,128)(2,1)S(1)} %get-tuple-element.186.refs_8_), channel_id=1, source_target_pairs={{0,2},{2,0},{4,6},{6,4},{8,10},{10,8},{12,14},{14,12},{16,18},{18,... | collective-permute-start | bytes 786440 | tf_op jit(solution)/shard_map/ppermute | solution.py:405
  124.8 13.2 %collective-permute-start.8 = (bf16[256,512]{1,0:T(8,128)(2,1)S(1)}, bf16[256,512]{1,0:T(8,128)(2,1)S(1)}, u32[]{:S(2)}, u32[]{:S(2)}) collective-permute-start(bf16[256,512]{1,0:T(8,128)(2,1)S(1)} %get-tuple-element.187.refs_7_), channel_id=1, source_target_pairs={{0,4},{2,6},{4,0},{6,2},{8,12},{10,14},{12,8},{14,10},{16,20},{18,... | collective-permute-start | bytes 786440 | tf_op jit(solution)/shard_map/ppermute | solution.py:405
  135.0 21.7 %collective-permute-start.12 = (bf16[512,512]{1,0:T(8,128)(2,1)}, bf16[512,512]{1,0:T(8,128)(2,1)S(1)}, u32[]{:S(2)}, u32[]{:S(2)}) collective-permute-start(bf16[512,512]{1,0:T(8,128)(2,1)} %get-tuple-element.97.refs_9_), channel_id=1, source_target_pairs={{0,2},{2,0},{4,6},{6,4},{8,10},{10,8},{12,14},{14,12},{16,18},{18,... | collective-permute-start | bytes 1572872 | tf_op jit(solution)/shard_map/ppermute | solution.py:405
  135.9 19.5 %collective-permute-start.13 = (bf16[512,512]{1,0:T(8,128)(2,1)}, bf16[512,512]{1,0:T(8,128)(2,1)S(1)}, u32[]{:S(2)}, u32[]{:S(2)}) collective-permute-start(bf16[512,512]{1,0:T(8,128)(2,1)} %get-tuple-element.98.refs_10_), channel_id=1, source_target_pairs={{0,4},{2,6},{4,0},{6,2},{8,12},{10,14},{12,8},{14,10},{16,20},{18,... | collective-permute-start | bytes 1572872 | tf_op jit(solution)/shard_map/ppermute | solution.py:405
  138.1 45.3 %collective-permute-start.10 = (bf16[512,512]{1,0:T(8,128)(2,1)S(1)}, bf16[512,512]{1,0:T(8,128)(2,1)S(1)}, u32[]{:S(2)}, u32[]{:S(2)}) collective-permute-start(bf16[512,512]{1,0:T(8,128)(2,1)S(1)} %pad_maximum_fusion.1.refs_7_.refs_0_), channel_id=1, source_target_pairs={{0,2},{2,0},{4,6},{6,4},{8,10},{10,8},{12,14},{14,12},{16,18},{18,... | collective-permute-start | bytes 1572872 | tf_op jit(solution)/shard_map/ppermute | solution.py:405
  139.2 46.2 %collective-permute-start.11 = (bf16[512,512]{1,0:T(8,128)(2,1)S(1)}, bf16[512,512]{1,0:T(8,128)(2,1)S(1)}, u32[]{:S(2)}, u32[]{:S(2)}) collective-permute-start(bf16[512,512]{1,0:T(8,128)(2,1)S(1)} %pad_maximum_fusion.2.refs_8_.refs_2_), channel_id=1, source_target_pairs={{0,4},{2,6},{4,0},{6,2},{8,12},{10,14},{12,8},{14,10},{16,20},{18,... | collective-permute-start | bytes 1572872 | tf_op jit(solution)/shard_map/ppermute | solution.py:405
  140.1 16.4 %copy-start.18 = (bf16[512,512]{1,0:T(8,128)(2,1)S(1)}, bf16[512,512]{1,0:T(8,128)(2,1)}, u32[]{:S(2)}) copy-start(bf16[512,512]{1,0:T(8,128)(2,1)} %get-tuple-element.103) | copy-start | bytes 1572868
  149.7 32.3 %collective-permute-start.17 = (bf16[512,512]{1,0:T(8,128)(2,1)}, bf16[512,512]{1,0:T(8,128)(2,1)S(1)}, u32[]{:S(2)}, u32[]{:S(2)}) collective-permute-start(bf16[512,512]{1,0:T(8,128)(2,1)} %get-tuple-element.105.refs_11_), channel_id=1, source_target_pairs={{0,4},{2,6},{4,0},{6,2},{8,12},{10,14},{12,8},{14,10},{16,20},{18,... | collective-permute-start | bytes 1572872 | tf_op jit(solution)/shard_map/ppermute | solution.py:405
  155.4 27.7 %collective-permute-start.16 = (bf16[512,512]{1,0:T(8,128)(2,1)}, bf16[512,512]{1,0:T(8,128)(2,1)S(1)}, u32[]{:S(2)}, u32[]{:S(2)}) collective-permute-start(bf16[512,512]{1,0:T(8,128)(2,1)} %get-tuple-element.104.refs_10_), channel_id=1, source_target_pairs={{0,2},{2,0},{4,6},{6,4},{8,10},{10,8},{12,14},{14,12},{16,18},{18,... | collective-permute-start | bytes 1572872 | tf_op jit(solution)/shard_map/ppermute | solution.py:405
  156.5 26.3 %copy-start.23 = (bf16[512,512]{1,0:T(8,128)(2,1)S(1)}, bf16[512,512]{1,0:T(8,128)(2,1)}, u32[]{:S(2)}) copy-start(bf16[512,512]{1,0:T(8,128)(2,1)} %get-tuple-element.109) | copy-start | bytes 1572868
  156.7 26.3 %copy-start.36 = (bf16[256,512]{1,0:T(8,128)(2,1)}, bf16[256,512]{1,0:T(8,128)(2,1)S(1)}, u32[]{:S(2)}) copy-start(bf16[256,512]{1,0:T(8,128)(2,1)S(1)} %constant_dynamic-slice_fusion.4.refs_9_) | copy-start | bytes 786436
  156.7 46.4 %collective-permute-start.15 = (bf16[256,512]{1,0:T(8,128)(2,1)S(1)}, bf16[256,512]{1,0:T(8,128)(2,1)S(1)}, u32[]{:S(2)}, u32[]{:S(2)}) collective-permute-start(bf16[256,512]{1,0:T(8,128)(2,1)S(1)} %constant_dynamic-slice_fusion.4.refs_9_), channel_id=1, source_target_pairs={{0,2},{2,0},{4,6},{6,4},{8,10},{10,8},{12,14},{14,12},{16,18},{18,... | collective-permute-start | bytes 786440 | tf_op jit(solution)/shard_map/ppermute | solution.py:405
  157.7 25.5 %copy-start.21 = (bf16[512,512]{1,0:T(8,128)(2,1)S(1)}, bf16[512,512]{1,0:T(8,128)(2,1)}, u32[]{:S(2)}) copy-start(bf16[512,512]{1,0:T(8,128)(2,1)} %get-tuple-element.108) | copy-start | bytes 1572868
  157.8 25.5 %copy-start.37 = (bf16[256,512]{1,0:T(8,128)(2,1)}, bf16[256,512]{1,0:T(8,128)(2,1)S(1)}, u32[]{:S(2)}) copy-start(bf16[256,512]{1,0:T(8,128)(2,1)S(1)} %constant_dynamic-slice_fusion.5.refs_8_) | copy-start | bytes 786436
  182.0 22.1 %collective-permute-start.14 = (bf16[256,512]{1,0:T(8,128)(2,1)S(1)}, bf16[256,512]{1,0:T(8,128)(2,1)S(1)}, u32[]{:S(2)}, u32[]{:S(2)}) collective-permute-start(bf16[256,512]{1,0:T(8,128)(2,1)S(1)} %constant_dynamic-slice_fusion.5.refs_8_), channel_id=1, source_target_pairs={{0,4},{2,6},{4,0},{6,2},{8,12},{10,14},{12,8},{14,10},{16,20},{18,... | collective-permute-start | bytes 786440 | tf_op jit(solution)/shard_map/ppermute | solution.py:405
  183.0 34.3 %collective-permute-start.21 = (bf16[256,512]{1,0:T(8,128)(2,1)S(1)}, bf16[256,512]{1,0:T(8,128)(2,1)S(1)}, u32[]{:S(2)}, u32[]{:S(2)}) collective-permute-start(bf16[256,512]{1,0:T(8,128)(2,1)S(1)} %constant_dynamic-slice_fusion.2.refs_14_), channel_id=1, source_target_pairs={{0,2},{2,0},{4,6},{6,4},{8,10},{10,8},{12,14},{14,12},{16,18},{18,... | collective-permute-start | bytes 786440 | tf_op jit(solution)/shard_map/ppermute | solution.py:405
  183.3 17.8 %copy-start.34 = (bf16[256,512]{1,0:T(8,128)(2,1)}, bf16[256,512]{1,0:T(8,128)(2,1)S(1)}, u32[]{:S(2)}) copy-start(bf16[256,512]{1,0:T(8,128)(2,1)S(1)} %constant_dynamic-slice_fusion.3.refs_13_) | copy-start | bytes 786436
  183.4 34.2 %collective-permute-start.20 = (bf16[256,512]{1,0:T(8,128)(2,1)S(1)}, bf16[256,512]{1,0:T(8,128)(2,1)S(1)}, u32[]{:S(2)}, u32[]{:S(2)}) collective-permute-start(bf16[256,512]{1,0:T(8,128)(2,1)S(1)} %constant_dynamic-slice_fusion.3.refs_13_), channel_id=1, source_target_pairs={{0,4},{2,6},{4,0},{6,2},{8,12},{10,14},{12,8},{14,10},{16,20},{18,... | collective-permute-start | bytes 786440 | tf_op jit(solution)/shard_map/ppermute | solution.py:405
  201.1 18.9 %collective-permute-start.22 = (bf16[512,512]{1,0:T(8,128)(2,1)}, bf16[512,512]{1,0:T(8,128)(2,1)S(1)}, u32[]{:S(2)}, u32[]{:S(2)}) collective-permute-start(bf16[512,512]{1,0:T(8,128)(2,1)} %get-tuple-element.110.refs_15_), channel_id=1, source_target_pairs={{0,2},{2,0},{4,6},{6,4},{8,10},{10,8},{12,14},{14,12},{16,18},{18,... | collective-permute-start | bytes 1572872 | tf_op jit(solution)/shard_map/ppermute | solution.py:405
  203.1 15.9 %collective-permute-start.23 = (bf16[512,512]{1,0:T(8,128)(2,1)}, bf16[512,512]{1,0:T(8,128)(2,1)S(1)}, u32[]{:S(2)}, u32[]{:S(2)}) collective-permute-start(bf16[512,512]{1,0:T(8,128)(2,1)} %get-tuple-element.111.refs_16_), channel_id=1, source_target_pairs={{0,4},{2,6},{4,0},{6,2},{8,12},{10,14},{12,8},{14,10},{16,20},{18,... | collective-permute-start | bytes 1572872 | tf_op jit(solution)/shard_map/ppermute | solution.py:405
  204.3 17.1 %collective-permute-start.19 = (bf16[2,256,512]{2,1,0:T(8,128)(2,1)S(1)}, bf16[2,256,512]{2,1,0:T(8,128)(2,1)S(1)}, u32[]{:S(2)}, u32[]{:S(2)}) collective-permute-start(bf16[2,256,512]{2,1,0:T(8,128)(2,1)S(1)} %pad_maximum_fusion.3.refs_12_), channel_id=1, source_target_pairs={{0,8},{2,10},{4,12},{6,14},{8,0},{10,2},{12,4},{14,6},{16,24},{18,... | collective-permute-start | bytes 1572872 | tf_op jit(solution)/shard_map/ppermute | solution.py:483
  217.3 87.3 %collective-permute-start.18 = (bf16[512,1024]{1,0:T(8,128)(2,1)}, bf16[512,1024]{1,0:T(8,128)(2,1)S(1)}, u32[]{:S(2)}, u32[]{:S(2)}) collective-permute-start(bf16[512,1024]{1,0:T(8,128)(2,1)} %get-tuple-element.112.refs_19_), channel_id=1, source_target_pairs={{0,1},{1,0},{2,3},{3,2},{4,5},{5,4},{6,7},{7,6},{8,9},{9,8},{10,11... | collective-permute-start | bytes 3145736 | tf_op jit(solution)/shard_map/ppermute | solution.py:703
  217.7 25.8 %collective-permute-start.38 = (bf16[2,256,512]{2,1,0:T(8,128)(2,1)S(1)}, bf16[2,256,512]{2,1,0:T(8,128)(2,1)S(1)}, u32[]{:S(2)}, u32[]{:S(2)}) collective-permute-start(bf16[2,256,512]{2,1,0:T(8,128)(2,1)S(1)} %pad_maximum_fusion.4.refs_16_), channel_id=1, source_target_pairs={{0,8},{2,10},{4,12},{6,14},{8,0},{10,2},{12,4},{14,6},{16,24},{18,... | collective-permute-start | bytes 1572872 | tf_op jit(solution)/shard_map/ppermute | solution.py:483
  219.2 19.9 %collective-permute-start.31 = (bf16[256,512]{1,0:T(8,128)(2,1)S(1)}, bf16[256,512]{1,0:T(8,128)(2,1)S(1)}, u32[]{:S(2)}, u32[]{:S(2)}) collective-permute-start(bf16[256,512]{1,0:T(8,128)(2,1)S(1)} %constant_dynamic-slice_fusion.refs_18_), channel_id=1, source_target_pairs={{0,2},{2,0},{4,6},{6,4},{8,10},{10,8},{12,14},{14,12},{16,18},{18,... | collective-permute-start | bytes 786440 | tf_op jit(solution)/shard_map/ppermute | solution.py:405
  220.3 19.0 %collective-permute-start.30 = (bf16[256,512]{1,0:T(8,128)(2,1)S(1)}, bf16[256,512]{1,0:T(8,128)(2,1)S(1)}, u32[]{:S(2)}, u32[]{:S(2)}) collective-permute-start(bf16[256,512]{1,0:T(8,128)(2,1)S(1)} %constant_dynamic-slice_fusion.1.refs_17_), channel_id=1, source_target_pairs={{0,4},{2,6},{4,0},{6,2},{8,12},{10,14},{12,8},{14,10},{16,20},{18,... | collective-permute-start | bytes 786440 | tf_op jit(solution)/shard_map/ppermute | solution.py:405
  221.6 31.4 %collective-permute-start.44 = (bf16[2,256,512]{2,1,0:T(8,128)(2,1)S(1)}, bf16[2,256,512]{2,1,0:T(8,128)(2,1)S(1)}, u32[]{:S(2)}, u32[]{:S(2)}) collective-permute-start(bf16[2,256,512]{2,1,0:T(8,128)(2,1)S(1)} %add_convert_fusion.7.refs_15_), channel_id=1, source_target_pairs={{0,16},{2,18},{4,20},{6,22},{8,24},{10,26},{12,28},{14,30},{16,0},... | collective-permute-start | bytes 1572872 | tf_op jit(solution)/shard_map/ppermute | solution.py:483
  239.1 62.7 %collective-permute-start.24 = (bf16[512,1024]{1,0:T(8,128)(2,1)}, bf16[512,1024]{1,0:T(8,128)(2,1)S(1)}, u32[]{:S(2)}, u32[]{:S(2)}) collective-permute-start(bf16[512,1024]{1,0:T(8,128)(2,1)} %get-tuple-element.124), channel_id=1, source_target_pairs={{0,1},{1,0},{2,3},{3,2},{4,5},{5,4},{6,7},{7,6},{8,9},{9,8},{10,11... | collective-permute-start | bytes 3145736 | tf_op jit(solution)/shard_map/ppermute | solution.py:704
  239.4 33.8 %collective-permute-start.32 = (bf16[2,256,512]{2,1,0:T(8,128)(2,1)S(1)}, bf16[2,256,512]{2,1,0:T(8,128)(2,1)S(1)}, u32[]{:S(2)}, u32[]{:S(2)}) collective-permute-start(bf16[2,256,512]{2,1,0:T(8,128)(2,1)S(1)} %pad_maximum_fusion.5), channel_id=1, source_target_pairs={{0,8},{2,10},{4,12},{6,14},{8,0},{10,2},{12,4},{14,6},{16,24},{18,... | collective-permute-start | bytes 1572872 | tf_op jit(solution)/shard_map/ppermute | solution.py:483
  243.6 37.9 %collective-permute-start.39 = (bf16[2,256,512]{2,1,0:T(8,128)(2,1)S(1)}, bf16[2,256,512]{2,1,0:T(8,128)(2,1)S(1)}, u32[]{:S(2)}, u32[]{:S(2)}) collective-permute-start(bf16[2,256,512]{2,1,0:T(8,128)(2,1)S(1)} %add_convert_fusion.2), channel_id=1, source_target_pairs={{0,16},{2,18},{4,20},{6,22},{8,24},{10,26},{12,28},{14,30},{16,0},... | collective-permute-start | bytes 1572872 | tf_op jit(solution)/shard_map/ppermute | solution.py:483
  253.3 29.3 %collective-permute-start.47 = (bf16[256,512]{1,0:T(8,128)(2,1)S(1)}, bf16[256,512]{1,0:T(8,128)(2,1)S(1)}, u32[]{:S(2)}, u32[]{:S(2)}) collective-permute-start(bf16[256,512]{1,0:T(8,128)(2,1)S(1)} %get-tuple-element.174), channel_id=1, source_target_pairs={{0,2},{2,0},{4,6},{6,4},{8,10},{10,8},{12,14},{14,12},{16,18},{18,... | collective-permute-start | bytes 786440 | tf_op jit(solution)/shard_map/ppermute | solution.py:405
  273.2 10.6 %collective-permute-start.45 = (bf16[256,512]{1,0:T(8,128)(2,1)S(1)}, bf16[256,512]{1,0:T(8,128)(2,1)S(1)}, u32[]{:S(2)}, u32[]{:S(2)}) collective-permute-start(bf16[256,512]{1,0:T(8,128)(2,1)S(1)} %get-tuple-element.175), channel_id=1, source_target_pairs={{0,4},{2,6},{4,0},{6,2},{8,12},{10,14},{12,8},{14,10},{16,20},{18,... | collective-permute-start | bytes 786440 | tf_op jit(solution)/shard_map/ppermute | solution.py:405
  281.5 49.9 %collective-permute-start.33 = (bf16[2,256,512]{2,1,0:T(8,128)(2,1)S(1)}, bf16[2,256,512]{2,1,0:T(8,128)(2,1)}, u32[]{:S(2)}, u32[]{:S(2)}) collective-permute-start(bf16[2,256,512]{2,1,0:T(8,128)(2,1)S(1)} %add_convert_fusion.4), channel_id=1, source_target_pairs={{0,16},{2,18},{4,20},{6,22},{8,24},{10,26},{12,28},{14,30},{16,0},... | collective-permute-start | bytes 1572872 | tf_op jit(solution)/shard_map/ppermute | solution.py:483
  282.6 25.4 %collective-permute-start.42 = (bf16[256,512]{1,0:T(8,128)(2,1)}, bf16[256,512]{1,0:T(8,128)(2,1)S(1)}, u32[]{:S(2)}, u32[]{:S(2)}) collective-permute-start(bf16[256,512]{1,0:T(8,128)(2,1)} %get-tuple-element.178), channel_id=1, source_target_pairs={{0,2},{2,0},{4,6},{6,4},{8,10},{10,8},{12,14},{14,12},{16,18},{18,... | collective-permute-start | bytes 786440 | tf_op jit(solution)/shard_map/ppermute | solution.py:405
  283.8 20.0 %copy-start = (bf16[512,1024]{1,0:T(8,128)(2,1)S(1)}, bf16[512,1024]{1,0:T(8,128)(2,1)}, u32[]{:S(2)}) copy-start(bf16[512,1024]{1,0:T(8,128)(2,1)} %refs_14_.1) | copy-start | bytes 3145732
  283.8 20.0 %copy-start.1 = (f32[512,1024]{1,0:T(8,128)S(1)}, f32[512,1024]{1,0:T(8,128)}, u32[]{:S(2)}) copy-start(f32[512,1024]{1,0:T(8,128)} %get-tuple-element.125) | copy-start | bytes 6291460
  283.8 25.3 %collective-permute-start.40 = (bf16[256,512]{1,0:T(8,128)(2,1)}, bf16[256,512]{1,0:T(8,128)(2,1)}, u32[]{:S(2)}, u32[]{:S(2)}) collective-permute-start(bf16[256,512]{1,0:T(8,128)(2,1)} %get-tuple-element.179), channel_id=1, source_target_pairs={{0,4},{2,6},{4,0},{6,2},{8,12},{10,14},{12,8},{14,10},{16,20},{18,... | collective-permute-start | bytes 786440 | tf_op jit(solution)/shard_map/ppermute | solution.py:405
  301.8 55.5 %collective-permute-start.46 = (bf16[512,512]{1,0:T(8,128)(2,1)S(1)}, bf16[512,512]{1,0:T(8,128)(2,1)}, u32[]{:S(2)}, u32[]{:S(2)}) collective-permute-start(bf16[512,512]{1,0:T(8,128)(2,1)S(1)} %pad_maximum_fusion.10.refs_0_), channel_id=1, source_target_pairs={{0,2},{2,0},{4,6},{6,4},{8,10},{10,8},{12,14},{14,12},{16,18},{18,... | collective-permute-start | bytes 1572872 | tf_op jit(solution)/shard_map/ppermute | solution.py:405
  304.7 54.6 %collective-permute-start.48 = (bf16[512,512]{1,0:T(8,128)(2,1)S(1)}, bf16[512,512]{1,0:T(8,128)(2,1)}, u32[]{:S(2)}, u32[]{:S(2)}) collective-permute-start(bf16[512,512]{1,0:T(8,128)(2,1)S(1)} %pad_maximum_fusion.11.refs_2_), channel_id=1, source_target_pairs={{0,4},{2,6},{4,0},{6,2},{8,12},{10,14},{12,8},{14,10},{16,20},{18,... | collective-permute-start | bytes 1572872 | tf_op jit(solution)/shard_map/ppermute | solution.py:405
  308.0 2.2 collective-permute-start.25
  310.3 29.3 %collective-permute-start.26 = (f32[8704]{0:T(1024)S(1)}, f32[8704]{0:T(1024)S(1)}, u32[]{:S(2)}, u32[]{:S(2)}) collective-permute-start(f32[8704]{0:T(1024)S(1)} %pad_maximum_fusion.12), channel_id=1, source_target_pairs={{0,2},{2,0},{4,6},{6,4},{8,10},{10,8},{12,14},{14,12},{16,18},{18,... | collective-permute-start | bytes 104456 | tf_op jit(solution)/shard_map/ppermute | solution.py:555
  332.7 17.6 %collective-permute-start.36 = (bf16[256,512]{1,0:T(8,128)(2,1)S(1)}, bf16[256,512]{1,0:T(8,128)(2,1)S(1)}, u32[]{:S(2)}, u32[]{:S(2)}) collective-permute-start(bf16[256,512]{1,0:T(8,128)(2,1)S(1)} %get-tuple-element.182), channel_id=1, source_target_pairs={{0,2},{2,0},{4,6},{6,4},{8,10},{10,8},{12,14},{14,12},{16,18},{18,... | collective-permute-start | bytes 786440 | tf_op jit(solution)/shard_map/ppermute | solution.py:405
  333.7 18.6 %collective-permute-start.34 = (bf16[256,512]{1,0:T(8,128)(2,1)S(1)}, bf16[256,512]{1,0:T(8,128)(2,1)S(1)}, u32[]{:S(2)}, u32[]{:S(2)}) collective-permute-start(bf16[256,512]{1,0:T(8,128)(2,1)S(1)} %get-tuple-element.183), channel_id=1, source_target_pairs={{0,4},{2,6},{4,0},{6,2},{8,12},{10,14},{12,8},{14,10},{16,20},{18,... | collective-permute-start | bytes 786440 | tf_op jit(solution)/shard_map/ppermute | solution.py:405
  339.6 4.7 %collective-permute-start.27 = (f32[8704]{0:T(1024)S(1)}, f32[8704]{0:T(1024)S(1)}, u32[]{:S(2)}, u32[]{:S(2)}) collective-permute-start(f32[8704]{0:T(1024)S(1)} %fusion.28), channel_id=1, source_target_pairs={{0,4},{2,6},{4,0},{6,2},{8,12},{10,14},{12,8},{14,10},{16,20},{18,... | collective-permute-start | bytes 104456 | tf_op jit(solution)/shard_map/ppermute | solution.py:555
  339.7 12.7 %copy-start.5 = (bf16[512,512]{1,0:T(8,128)(2,1)}, bf16[512,512]{1,0:T(8,128)(2,1)S(1)}, u32[]{:S(2)}) copy-start(bf16[512,512]{1,0:T(8,128)(2,1)S(1)} %pad_maximum_fusion.8.refs_0_) | copy-start | bytes 1572868
  344.3 4.0 %collective-permute-start.28 = (f32[8704]{0:T(1024)S(1)}, f32[8704]{0:T(1024)S(1)}, u32[]{:S(2)}, u32[]{:S(2)}) collective-permute-start(f32[8704]{0:T(1024)S(1)} %add.359), channel_id=1, source_target_pairs={{0,8},{2,10},{4,12},{6,14},{8,0},{10,2},{12,4},{14,6},{16,24},{18,... | collective-permute-start | bytes 104456 | tf_op jit(solution)/shard_map/ppermute | solution.py:555
  348.3 16.2 %collective-permute-start.41 = (bf16[512,512]{1,0:T(8,128)(2,1)S(1)}, bf16[512,512]{1,0:T(8,128)(2,1)}, u32[]{:S(2)}, u32[]{:S(2)}) collective-permute-start(bf16[512,512]{1,0:T(8,128)(2,1)S(1)} %pad_maximum_fusion.8.refs_0_), channel_id=1, source_target_pairs={{0,2},{2,0},{4,6},{6,4},{8,10},{10,8},{12,14},{14,12},{16,18},{18,... | collective-permute-start | bytes 1572872 | tf_op jit(solution)/shard_map/ppermute | solution.py:405
  350.3 14.6 %collective-permute-start.43 = (bf16[512,512]{1,0:T(8,128)(2,1)S(1)}, bf16[512,512]{1,0:T(8,128)(2,1)}, u32[]{:S(2)}, u32[]{:S(2)}) collective-permute-start(bf16[512,512]{1,0:T(8,128)(2,1)S(1)} %pad_maximum_fusion.9.refs_2_), channel_id=1, source_target_pairs={{0,4},{2,6},{4,0},{6,2},{8,12},{10,14},{12,8},{14,10},{16,20},{18,... | collective-permute-start | bytes 1572872 | tf_op jit(solution)/shard_map/ppermute | solution.py:405
  352.3 4.9 %collective-permute-start.29 = (f32[8704]{0:T(1024)S(1)}, f32[8704]{0:T(1024)S(1)}, u32[]{:S(2)}, u32[]{:S(2)}) collective-permute-start(f32[8704]{0:T(1024)S(1)} %add.360), channel_id=1, source_target_pairs={{0,16},{2,18},{4,20},{6,22},{8,24},{10,26},{12,28},{14,30},{16,0},... | collective-permute-start | bytes 104456 | tf_op jit(solution)/shard_map/ppermute | solution.py:555
  357.2 12.9 %collective-permute-start.35 = (bf16[512,512]{1,0:T(8,128)(2,1)S(1)}, bf16[512,512]{1,0:T(8,128)(2,1)}, u32[]{:S(2)}, u32[]{:S(2)}) collective-permute-start(bf16[512,512]{1,0:T(8,128)(2,1)S(1)} %pad_maximum_fusion.6.refs_0_), channel_id=1, source_target_pairs={{0,2},{2,0},{4,6},{6,4},{8,10},{10,8},{12,14},{14,12},{16,18},{18,... | collective-permute-start | bytes 1572872 | tf_op jit(solution)/shard_map/ppermute | solution.py:405
  357.4 13.0 %collective-permute-start.37 = (bf16[512,512]{1,0:T(8,128)(2,1)S(1)}, bf16[512,512]{1,0:T(8,128)(2,1)S(1)}, u32[]{:S(2)}, u32[]{:S(2)}) collective-permute-start(bf16[512,512]{1,0:T(8,128)(2,1)S(1)} %pad_maximum_fusion.7.refs_2_), channel_id=1, source_target_pairs={{0,4},{2,6},{4,0},{6,2},{8,12},{10,14},{12,8},{14,10},{16,20},{18,... | collective-permute-start | bytes 1572872 | tf_op jit(solution)/shard_map/ppermute | solution.py:405
  (36 other events, 153.8 us)
Sparse Core Ops, SparseCore 0:
  123.0 218.2 all-reduce.2

commit v4 on v3

--- a/solution.py
+++ b/solution.py
@@ -6,6 +6,7 @@
 from jax import lax
 from jax.experimental import pallas as pl
 from jax.experimental.pallas import tpu as pltpu
+from jax.sharding import Mesh
 from jax.sharding import PartitionSpec as P
 
 HD = 64
@@ -18,7 +19,7 @@
 F32 = jnp.float32
 BF16 = jnp.bfloat16
 PAIR = 2 * HD
-FIRST = 1
+CHUNK_PAIRS = 2
 QROWS = 256
 ROWS = 512
 HIDDEN = 256
@@ -120,7 +121,7 @@
     rows, width = second_in.shape
     cols = count * HIDDEN
     whole = pl.BlockSpec((rows, width), lambda j, at: (0, 0))
-    split = fast[1] == 2 and mid[1] == 2 and width == 2 * cols
+    split = fast[1] == 2 and mid[1] == 2
     out_specs = [
         pl.BlockSpec((rows, HIDDEN), lambda j, at: (0, j)),
         pl.BlockSpec((rows, HIDDEN), lambda j, at: (0, j)),
@@ -132,9 +133,10 @@
         jax.ShapeDtypeStruct((1, cols), F32),
     ]
     if split:
-        out_specs += [pl.BlockSpec((cols, HIDDEN), lambda j, at: (0, j))] * 2
-        out_specs += [pl.BlockSpec((HIDDEN, cols), lambda j, at: (j, 0))] * 2
-        out_shape += [jax.ShapeDtypeStruct((cols, cols), BF16)] * 4
+        out_specs += [pl.BlockSpec((width // 2, HIDDEN), lambda j, at: (0, j))] * 2
+        out_specs += [pl.BlockSpec((HIDDEN, width // 2), lambda j, at: (j, 0))] * 2
+        out_shape += [jax.ShapeDtypeStruct((width // 2, cols), BF16)] * 2
+        out_shape += [jax.ShapeDtypeStruct((cols, width // 2), BF16)] * 2
     else:
         out_specs += [
             pl.BlockSpec((width, HIDDEN), lambda j, at: (0, j)),
@@ -178,9 +180,10 @@
 
 
 def attention_kernel(
-    slots, first_ref, cot_ref, w_ref, wbias_ref, dense_ref, cos_ref, sin_ref, segq_ref, segk_ref,
-    context_ref, back_ref, grads_ref, dense_grads_ref, biasgrad_ref, mask_ref, dk_ref, dv_ref,
+    slots, split, at_ref, first_ref, cot_ref, w_ref, wbias_ref, dense_ref, cos_ref, sin_ref, segq_ref, segk_ref,
+    context_ref, back_ref, biasgrad_ref, *refs,
 ):
+    *out_refs, mask_ref, dk_ref, dv_ref = refs
     rows = first_ref.shape[0]
     blocks = rows // QROWS
     reach = -(-(MAXLEN - 1) // QROWS)
@@ -259,58 +262,80 @@
     back = back.astype(BF16)
     back_ref[...] = back
     weight_grad = dot(first, back, TN).astype(BF16)
-    for c in range(3):
-        grads_ref[c] = weight_grad[:, c * PAIR : (c + 1) * PAIR]
-    dense_grads_ref[...] = dot(context, cot, TN).astype(BF16)
-
-
-def attention_pair(first_in, cot, qkv, qkv_bias, dense_weight, cosine, sine, segment, slots, at, held=()):
+    dense_grad = dot(context, cot, TN).astype(BF16)
+    if split:
+        tiles = [dense_grad[:, c * PAIR : (c + 1) * PAIR] for c in range(dense_grad.shape[1] // PAIR)]
+        right = jnp.concatenate([weight_grad[:, 2 * PAIR :], jnp.concatenate(tiles, axis=0)], axis=1)
+        for side, grad in enumerate((weight_grad[:, : 2 * PAIR], right)):
+            half = grad.shape[0] // 2
+            first_half = at_ref[side] == 0
+            out_refs[2 * side][...] = jnp.where(first_half, grad[half:], grad[:half])
+            out_refs[2 * side + 1][...] = jnp.where(first_half, grad[:half], grad[half:])
+    else:
+        grads_ref, dense_grads_ref = out_refs
+        for c in range(3):
+            grads_ref[c] = weight_grad[:, c * PAIR : (c + 1) * PAIR]
+        dense_grads_ref[...] = dense_grad
+
+
+def attention_pair(
+    first_in, cot, qkv, qkv_bias, dense_weight, cosine, sine, segment, slots, pair, fast, mid, chunk, place, held
+):
     rows, width = first_in.shape
     reach = -(-(MAXLEN - 1) // QROWS)
     span = min(rows, (reach + 1) * QROWS)
-    whole = pl.BlockSpec((rows, width), lambda j: (0, 0))
-    table = pl.BlockSpec((rows, PAIR), lambda j: (0, 0))
+    split = fast[1] == 2 and mid[1] == 2
+    kept = list(chunk) if chunk else []
+
+    def fixed(*shape):
+        return pl.BlockSpec(shape, lambda j, at: (0,) * len(shape))
+
+    out_specs = [fixed(rows, PAIR), fixed(rows, 3 * PAIR), fixed(1, 3 * PAIR)]
+    out_shape = [
+        jax.ShapeDtypeStruct((rows, PAIR), BF16),
+        jax.ShapeDtypeStruct((rows, 3 * PAIR), BF16),
+        jax.ShapeDtypeStruct((1, 3 * PAIR), F32),
+    ]
+    if split:
+        out_specs += [pl.BlockSpec((width // 2, 2 * PAIR), lambda j, at: (0, place))] * 4
+        out_shape += [jax.ShapeDtypeStruct((width // 2, 2 * PAIR * CHUNK_PAIRS), BF16)] * 4
+    else:
+        out_specs += [fixed(3, width, PAIR), fixed(PAIR, width)]
+        out_shape += [jax.ShapeDtypeStruct((3, width, PAIR), BF16), jax.ShapeDtypeStruct((PAIR, width), BF16)]
     return pl.pallas_call(
-        after(functools.partial(attention_kernel, slots), 9, len(held)),
-        grid=(1,),
-        in_specs=[
-            whole,
-            whole,
-            pl.BlockSpec((3, width, PAIR), lambda j: (0, 0, at)),
-            pl.BlockSpec((3, 1, PAIR), lambda j: (0, 0, at)),
-            pl.BlockSpec((PAIR, width), lambda j: (at, 0)),
-            table,
-            table,
-            pl.BlockSpec((rows, 1), lambda j: (0, 0)),
-            pl.BlockSpec((1, rows), lambda j: (0, 0)),
-        ]
-        + [ANY] * len(held),
-        out_specs=[
-            pl.BlockSpec((rows, PAIR), lambda j: (0, 0)),
-            pl.BlockSpec((rows, 3 * PAIR), lambda j: (0, 0)),
-            pl.BlockSpec((3, width, PAIR), lambda j: (0, 0, 0)),
-            pl.BlockSpec((PAIR, width), lambda j: (0, 0)),
-            pl.BlockSpec((1, 3 * PAIR), lambda j: (0, 0)),
-        ],
-        out_shape=[
-            jax.ShapeDtypeStruct((rows, PAIR), BF16),
-            jax.ShapeDtypeStruct((rows, 3 * PAIR), BF16),
-            jax.ShapeDtypeStruct((3, width, PAIR), BF16),
-            jax.ShapeDtypeStruct((PAIR, width), BF16),
-            jax.ShapeDtypeStruct((1, 3 * PAIR), F32),
-        ],
-        scratch_shapes=[
-            pltpu.VMEM((rows, span), F32),
-            pltpu.VMEM((rows, PAIR), F32),
-            pltpu.VMEM((rows, PAIR), F32),
-        ],
+        after(functools.partial(attention_kernel, slots, split), 10, len(held) + len(kept)),
+        grid_spec=pltpu.PrefetchScalarGridSpec(
+            num_scalar_prefetch=1,
+            grid=(1,),
+            in_specs=[
+                fixed(rows, width),
+                fixed(rows, width),
+                pl.BlockSpec((3, width, PAIR), lambda j, at: (0, 0, pair)),
+                pl.BlockSpec((3, 1, PAIR), lambda j, at: (0, 0, pair)),
+                pl.BlockSpec((PAIR, width), lambda j, at: (pair, 0)),
+                fixed(rows, PAIR),
+                fixed(rows, PAIR),
+                fixed(rows, 1),
+                fixed(1, rows),
+            ]
+            + [ANY] * (len(held) + len(kept)),
+            out_specs=out_specs,
+            scratch_shapes=[
+                pltpu.VMEM((rows, span), F32),
+                pltpu.VMEM((rows, PAIR), F32),
+                pltpu.VMEM((rows, PAIR), F32),
+            ],
+        ),
+        out_shape=out_shape,
+        input_output_aliases={10 + k: 3 + k for k in range(len(kept))},
         compiler_params=PARAMS,
         cost_estimate=pl.CostEstimate(
-            flops=30 * rows * width * PAIR,
-            bytes_accessed=16 * width * PAIR,
-            transcendentals=2 * rows * span,
+            flops=30 * rows * width * PAIR, bytes_accessed=16 * width * PAIR, transcendentals=2 * rows * span
         ),
-    )(first_in, cot, qkv, qkv_bias, dense_weight, cosine, sine, segment.reshape(rows, 1), segment.reshape(1, rows), *held)
+    )(
+        jnp.stack([position(fast), position(mid)]), first_in, cot, qkv, qkv_bias, dense_weight, cosine, sine,
+        segment.reshape(rows, 1), segment.reshape(1, rows), *kept, *held,
+    )
 
 
 def branch_kernel(contexts, actives, slot_ref, *refs):
@@ -395,14 +420,17 @@
     return [(fast * mid, size // (fast * mid)), (fast, mid), (1, fast)]
 
 
+DP = ("slow", "mid", "fast")
+
+
 def position(ring):
-    return lax.axis_index("dp") // ring[0] % ring[1]
+    return lax.axis_index(DP) // ring[0] % ring[1]
 
 
 def hop(values, size, ring):
     stride, length = ring
     pairs = [(i, i + ((i // stride + 1) % length - i // stride % length) * stride) for i in range(size)]
-    return lax.ppermute(values, "dp", pairs)
+    return lax.ppermute(values, DP, pairs)
 
 
 def rows_of(values, index, length):
@@ -480,11 +508,83 @@
     step = 1
     while step < slow[1]:
         yield [both]
-        both = add(lax.ppermute(both, "dp", [(i, i ^ (step * slow[0])) for i in range(size)]), both)
+        both = add(lax.ppermute(both, DP, [(i, i ^ (step * slow[0])) for i in range(size)]), both)
         step *= 2
     left, right = yield from together(ring_pieces(both[0], size, mid), ring_pieces(both[1], size, fast))
     left, right = join(left, mid), join(right, fast)
     return (yield from together(ring_pieces(left, size, fast), ring_pieces(right, size, mid)))
+
+
+def halves_kernel(joins, cuts, at_ref, *refs):
+    for side in range(2):
+        came, own = refs[2 * side][...], refs[2 * side + 1][...]
+        lower = at_ref[side] == 0
+        if joins:
+            rows = own.shape[0]
+            out_ref = refs[4 + side]
+            out_ref[:rows] = jnp.where(lower, own, came)
+            out_ref[rows:] = jnp.where(lower, came, own)
+            continue
+        total = (came.astype(F32) + own.astype(F32)).astype(BF16)
+        if cuts:
+            half = total.shape[0] // 2
+            refs[4 + 2 * side][...] = jnp.where(lower, total[half:], total[:half])
+            refs[5 + 2 * side][...] = jnp.where(lower, total[:half], total[half:])
+        else:
+            refs[4 + side][...] = total
+
+
+def halves(kind, left, right, at, held=()):
+    joins, cuts = kind == "join", kind == "cut"
+    out_shape = []
+    for _, own in (left, right):
+        rows, cols = own.shape
+        if joins:
+            out_shape.append(jax.ShapeDtypeStruct((2 * rows, cols), BF16))
+        elif cuts:
+            out_shape += [jax.ShapeDtypeStruct((rows // 2, cols), BF16)] * 2
+        else:
+            out_shape.append(jax.ShapeDtypeStruct((rows, cols), BF16))
+    spec = pl.BlockSpec(memory_space=pltpu.VMEM)
+    size = left[0].size + right[0].size
+    return pl.pallas_call(
+        after(functools.partial(halves_kernel, joins, cuts), 5, len(held)),
+        in_specs=[pl.BlockSpec(memory_space=pltpu.SMEM)] + [spec] * 4 + [ANY] * len(held),
+        out_specs=[spec] * len(out_shape),
+        out_shape=out_shape,
+        compiler_params=PARAMS,
+        cost_estimate=pl.CostEstimate(flops=2 * size, bytes_accessed=8 * size, transcendentals=0),
+    )(jnp.stack(at), *left, *right, *held)
+
+
+def chunk_steps(left, right, rounds, size, calm, wait):
+    slow, mid, fast = rings(size)
+    at = [position(mid), position(fast)]
+    other = [(0, 1), (1, 0)]
+    yield [left[0], right[0]]
+    came = lax.ppermute(left[0], "fast", other), lax.ppermute(right[0], "mid", other)
+    left_away, left_own, right_away, right_own = halves("cut", (came[0], left[1]), (came[1], right[1]), at, rounds.block)
+    yield [left_away, right_away]
+    came = lax.ppermute(left_away, "mid", other), lax.ppermute(right_away, "fast", other)
+    left, right = halves("sum", (came[0], left_own), (came[1], right_own), at, rounds.block)
+    if calm:
+        yield [left, right]
+        left, right = lax.psum((left, right), "slow")
+        for _ in range(wait):
+            yield []
+    else:
+        step = 1
+        while step < slow[1]:
+            yield [left, right]
+            hops = [(i, i ^ step) for i in range(slow[1])]
+            came = lax.ppermute(left, "slow", hops), lax.ppermute(right, "slow", hops)
+            left, right = halves("sum", (came[0], left), (came[1], right), at, rounds.block)
+            step *= 2
+    yield [left, right]
+    came = lax.ppermute(left, "mid", other), lax.ppermute(right, "fast", other)
+    left, right = halves("join", (came[0], left), (came[1], right), at, rounds.block)
+    yield [left, right]
+    return [left, lax.ppermute(left, "fast", other)], [right, lax.ppermute(right, "mid", other)]
 
 
 def place_kernel(lefts, rights, kept, left_ref, right_ref, *refs):
@@ -648,43 +748,67 @@
     rows = cot.shape[0]
 
     _, mid, fast = rings(dp_size)
+    short = fast[1] == 2 and mid[1] == 2
+    pairs = head_width // PAIR
     totals = []
+    arrived = {}
 
     def finish(at, left, right):
+        if isinstance(at, tuple):
+            ends = [position(fast), position(mid)]
+            arrived[at] = halves("join", left[::-1], right[::-1], ends)
+            return arrived[at][0]
         inner, outer, token = place(totals, [(width, hidden), (hidden, width)], left, right, fast, mid, at)
         totals[:] = [inner, outer]
         return token
 
     rounds = Rounds(finish)
-    ffn = []
+    ffn = {}
     attn = []
     steps = hidden // HIDDEN
-    per = max(1, steps // 4)
-
-    def feed_forward():
+
+    def feed_forward(first, count, calm, wait):
         out = ffn_slice(
-            second_in, cot, inner_weight, inner_bias.reshape(1, -1), outer_weight, len(ffn) * per, per, fast, mid,
-            rounds.turn(),
+            second_in, cot, inner_weight, inner_bias.reshape(1, -1), outer_weight, first, count, fast, mid, rounds.turn()
         )
         rounds.block = [out[2]]
-        rounds.add(len(ffn), reduce_over_dp(out[3], out[4], dp_size))
-        ffn.append(out)
-
-    for _ in range(FIRST):
-        feed_forward()
+        if short:
+            rounds.add(first // count, chunk_steps(out[3], out[4], rounds, dp_size, calm, wait))
+        else:
+            rounds.add(first // count, reduce_over_dp(out[3], out[4], dp_size))
+        ffn[first] = out
+
+    if short and steps % 8 == 0:
+        quarter = steps // 4
+        feed_forward(2 * quarter, quarter, False, 0)
+        feed_forward(0, 2 * quarter, True, 3)
+        late = [(3 * quarter, quarter, False, 0)]
+    else:
+        feed_forward(0, 1, False, 0)
+        late = [(k, 1, False, 0) for k in range(1, steps)]
     segment, places = layout(seq_lengths[0], rows)
     cosine, sine = rotary_tables(places)
     qkv = jnp.transpose(qkv_weight, (1, 0, 2))
-    for pair in range(head_width // PAIR):
+    chunk = None
+    for pair in range(pairs):
         out = attention_pair(
-            first_in, cot, qkv, qkv_bias.reshape(3, 1, -1), dense_weight, cosine, sine, segment, slots, pair,
-            rounds.turn(),
+            first_in, cot, qkv, qkv_bias.reshape(3, 1, -1), dense_weight, cosine, sine, segment, slots, pair, fast, mid,
+            chunk, pair % CHUNK_PAIRS, rounds.turn(),
         )
-        rounds.block = [out[4]]
+        rounds.block = [out[2]]
         attn.append(out)
-    attn_sums = lax.psum(([a[2] for a in attn], [a[3] for a in attn]), "dp")
-    while len(ffn) * per < steps:
-        feed_forward()
+        chunk = out[3:] if short else None
+        if short and (pair % CHUNK_PAIRS == CHUNK_PAIRS - 1 or pair == pairs - 1):
+            rounds.add(
+                (pair // CHUNK_PAIRS,),
+                chunk_steps(tuple(out[3:5]), tuple(out[5:7]), rounds, dp_size, pair < pairs - 1, 2),
+            )
+            chunk = None
+    if not short:
+        attn_sums = lax.psum(([a[3] for a in attn], [a[4] for a in attn]), DP)
+    for slice_of in late:
+        feed_forward(*slice_of)
+    ffn = [ffn[first] for first in sorted(ffn)]
 
     order = here if tensor_size == 2 else jnp.int32(1)
     held = rounds.turn()
@@ -720,18 +844,28 @@
 
     over_all = jnp.concatenate([sums, jnp.sum(cotangent.astype(F32), axis=0, keepdims=True)], axis=0).reshape(-1)
     over_all = butterfly(over_all, "tensor", tensor_size)
-    qkvbias = jnp.concatenate([a[4].reshape(3, PAIR) for a in attn], axis=1).reshape(-1)
+    qkvbias = jnp.concatenate([a[2].reshape(3, PAIR) for a in attn], axis=1).reshape(-1)
     innerbias = jnp.concatenate([f[2] for f in ffn], axis=1).reshape(-1)
-    vectors = butterfly(jnp.concatenate([over_all, qkvbias, innerbias]), "dp", dp_size)
+    vectors = butterfly(jnp.concatenate([over_all, qkvbias, innerbias]), DP, dp_size)
     ends = [width * i for i in range(1, 6)] + [5 * width + 3 * head_width]
     gain1_grad, bias1_grad, gain2_grad, bias2_grad, outbias_grad, qkvbias_grad, innerbias_grad = jnp.split(vectors, ends)
 
+    rounds.block = []
     while rounds.live:
         rounds.turn()
     inner_grad, outer_grad = totals
-    qkv_sums, dense_sums = attn_sums
-    qkv_grad = jnp.concatenate([g.transpose(1, 0, 2) for g in qkv_sums], axis=2).astype(F32)
-    dense_grad = jnp.concatenate(dense_sums, axis=0).astype(F32)
+    if short:
+        lefts = [arrived[key][0].reshape(width, CHUNK_PAIRS, 2, PAIR) for key in sorted(arrived)]
+        rights = [arrived[key][1].reshape(width, CHUNK_PAIRS, 2, PAIR) for key in sorted(arrived)]
+        both = jnp.concatenate(lefts, axis=1)[:, :pairs].transpose(0, 2, 1, 3).reshape(width, 2, head_width)
+        rest = jnp.concatenate(rights, axis=1)[:, :pairs].transpose(0, 2, 1, 3).reshape(width, 2, head_width)
+        qkv_grad = jnp.concatenate([both, rest[:, :1]], axis=1).astype(F32)
+        dense_grad = rest[:, 1].reshape(width // PAIR, PAIR, head_width // PAIR, PAIR).transpose(2, 1, 0, 3)
+        dense_grad = dense_grad.reshape(head_width, width).astype(F32)
+    else:
+        qkv_sums, dense_sums = attn_sums
+        qkv_grad = jnp.concatenate([g.transpose(1, 0, 2) for g in qkv_sums], axis=2).astype(F32)
+        dense_grad = jnp.concatenate(dense_sums, axis=0).astype(F32)
     return (
         layer_out,
         residual_grad,
@@ -750,10 +884,12 @@
 
 
 def solution(mesh):
-    rows = P(("dp", "tensor"), None)
+    dp_size, tensor_size = mesh.shape["dp"], mesh.shape["tensor"]
+    digits = [length for _, length in rings(dp_size)]
+    rows = P(DP + ("tensor",), None)
     return jax.shard_map(
-        functools.partial(local, mesh.shape["dp"], mesh.shape["tensor"]),
-        mesh=mesh,
+        functools.partial(local, dp_size, tensor_size),
+        mesh=Mesh(mesh.devices.reshape(*digits, tensor_size), DP + ("tensor",)),
         in_specs=(
             rows,
             P(),
@@ -768,7 +904,7 @@
             P("tensor", None),
             P(),
             rows,
-            P("dp", None),
+            P(DP, None),
         ),
         out_specs=(
             rows,

time: 395 us -> 505 us (1.28)
  Pallas kernels: 152 us -> 202 us
  waiting for transfers between devices: 112 us -> 147 us
  local copies, waits for them, and re-layouts: 10.2 us -> 43.6 us
  starting transfers between devices: 69.4 us -> 59.3 us
    pallas_call x4 -> x27, Pallas kernels: 56.5 us -> 115 us  [the longest x4 59.4 us: attention_pair(): pl.pallas_call(after(functools.partial(attention_kernel, slots, split), 1...]
    ppermute x40 -> x52, waiting for transfers between devices: 99.1 us -> 118 us  [the longest x12 37.8 us: chunk_steps(): came = (lax.ppermute(left, 'slow', hops), lax.ppermute(right, 'slow', hops))]
    reshape x1 -> x7, local copies, waits for them, and re-layouts: 0.01 us -> 15.3 us  [the longest x2 4.41 us: local(): arrived[key][1].reshape(width, CHUNK_PAIRS, 2, PAIR)]
    ppermute x40 -> x52, starting transfers between devices: 66.5 us -> 55.2 us  [the longest x12 14.9 us: chunk_steps(): came = (lax.ppermute(left, 'slow', hops), lax.ppermute(right, 'slow', hops))]
    unnamed x100 -> x123, local copies, waits for them, and re-layouts: 5.47 us -> 16.6 us
    psum x1, waiting for transfers between devices: 0.01 us -> 10.3 us  [chunk_steps(): left, right = lax.psum((left, right), 'slow')]
    transpose x0 -> x2, other arithmetic: none -> 9.47 us  [the longest x1 5.23 us: local(): jnp.concatenate(lefts, axis=1)[:, :pairs].transpose(0, 2, 1, 3)]
    pallas_call x4 -> x3, Pallas kernels: 39 us -> 33.9 us  [ffn_slice(): pl.pallas_call(after(ffn_kernel, 6, len(held)), grid_spec=pltpu.PrefetchS...]
  transfers between devices with their start and end apart: 50 -> 62, of which waited for: 17 -> 18; matrix products, arithmetic and copies ran while one was open for 7% -> 12% of each run, Pallas kernels for 35% -> 31%
where the time goes in v4:
time: 505 us; the launch traced here: 497 us
  Pallas kernels  202 us (40%)
  waiting for transfers between devices  147 us (29%)
  starting transfers between devices  59.3 us (12%)
  local copies, waits for them, and re-layouts  43.6 us (9%)
  other arithmetic  30.7 us (6%)
  between operations  15.1 us (3%)
    pallas_call x4, Pallas kernels, attention_pair(): pl.pallas_call(after(functools.partial(attention_kernel, slots, split), 1...  59.4 us
    pallas_call x23, Pallas kernels, halves(): pl.pallas_call(after(functools.partial(halves_kernel, joins, cuts), 5, le...  55.4 us
    ppermute x12, waiting for transfers between devices, chunk_steps(): came = (lax.ppermute(left, 'slow', hops), lax.ppermute(right, 'slow', hops))  37.8 us
    ppermute x5, waiting for transfers between devices, chunk_steps(): lax.ppermute(left[0], 'fast', other)  37.2 us
    pallas_call x3, Pallas kernels, ffn_slice(): pl.pallas_call(after(ffn_kernel, 6, len(held)), grid_spec=pltpu.PrefetchS...  33.9 us
    pallas_call x2, Pallas kernels, rows_call(): pl.pallas_call(after(kernel, 1 + len(in_specs), len(held)), grid_spec=plt...  28.4 us
    pallas_call x3, Pallas kernels, place(): pl.pallas_call(functools.partial(place_kernel, len(left), len(right), len...  17.6 us
    ppermute x5, waiting for transfers between devices, butterfly(): lax.ppermute(values, axis, [(i, i ^ step) for i in range(size)])  16.8 us
  transfers between devices with their start and end apart: 62, of which 18 were waited for; matrix products, arithmetic and copies ran while one was open for 12% of the time, Pallas kernels for 31%

profile of v4, /device:TPU:0, one launch (start us, length us, event | category | flops | bytes accessed | tf_op | source)
XLA Modules:
  0.0 497.4 jit_solution(1441812419941003672)
XLA Ops:
  12.7 6.7 %shard_map.237 = (bf16[1024,1024]{1,0:T(8,128)(2,1)}, bf16[1024,1024]{1,0:T(8,128)(2,1)}, bf16[1024,1024]{1,0:T(8,128)(2,1)}) custom-call(s32[2]{0:T(128)} %pad_add_fusion.2.slot_ref, bf16[512,1024]{1,0:T(8,128)(2,1)} %refs_13_.1, bf16[512,1024]{1,0:T(8,128)(2,1)} %copy-done.4, bf16[512,1024]{1,0:T(8,128)(2,1)} %own_cot_ref.1, bf16[512,1024]{1,0:T(8,128)(2,1)} %copy-done.6, ...), custom_call_target="tpu_custom_call" | custom-call | flops 20971520 | bytes 10485760 | tf_op jit(solution)/shard_map/pallas_call | solution.py:69
  19.4 9.5 %shard_map.238 = (bf16[1024,512]{1,0:T(8,128)(2,1)}, bf16[1024,512]{1,0:T(8,128)(2,1)}, f32[1,512]{1,0:T(1,128)}, bf16[512,512]{1,0:T(8,128)(2,1)}, bf16[512,512...) custom-call(s32[2]{0:T(128)} %pad_add_fusion.1.refs_0_, ...), custom_call_target="tpu_custom_call" | custom-call | flops 4294967296 | bytes 10485760 | tf_op jit(solution)/shard_map/pallas_call | solution.py:149
  28.9 14.8 %shard_map.239 = (bf16[1024,1024]{1,0:T(8,128)(2,1)}, bf16[1024,1024]{1,0:T(8,128)(2,1)}, f32[1,1024]{1,0:T(1,128)}, bf16[512,1024]{1,0:T(8,128)(2,1)}, bf16[512...) custom-call(s32[2]{0:T(128)} %pad_add_fusion.1.refs_0_, ...), custom_call_target="tpu_custom_call" | custom-call | flops 8589934592 | bytes 20971520 | tf_op jit(solution)/shard_map/pallas_call | solution.py:149
  43.7 2.9 collective-permute-start.6
  51.0 3.2 fusion.12
  54.2 27.3 %collective-permute-done.2.refs_1_ = bf16[512,512]{1,0:T(8,128)(2,1)S(1)} collective-permute-done((bf16[512,512]{1,0:T(8,128)(2,1)}, bf16[512,512]{1,0:T(8,128)(2,1)S(1)}, u32[]{:S(2)}, u32[]{:S(2)}) %collective-permute-start.2) | collective-permute-done | bytes 524320 | tf_op jit(solution)/shard_map/ppermute | solution.py:565
  83.8 2.6 shard_map.240
  88.5 14.7 %shard_map.241 = (bf16[1024,128]{1,0:T(8,128)(2,1)}, bf16[1024,384]{1,0:T(8,128)(2,1)}, f32[1,384]{1,0:T(1,128)}, bf16[512,512]{1,0:T(8,128)(2,1)}, bf16[512,512...) custom-call(s32[2]{0:T(128)} %pad_add_fusion.1.refs_0_, ...), custom_call_target="tpu_custom_call" | custom-call | flops 4026531840 | bytes 2097152 | tf_op jit(solution)/shard_map/pallas_call | solution.py:305
  104.4 3.8 shard_map.243
  111.0 2.1 shard_map.242
  115.1 14.8 %shard_map.244 = (bf16[1024,128]{1,0:T(8,128)(2,1)}, bf16[1024,384]{1,0:T(8,128)(2,1)}, f32[1,384]{1,0:T(1,128)}, bf16[512,512]{1,0:T(8,128)(2,1)}, bf16[512,512...) custom-call(s32[2]{0:T(128)} %pad_add_fusion.1.refs_0_, ...), custom_call_target="tpu_custom_call", output_to_operand_aliasing={{3}: (10, {}), {4}: (11, {}), {5}: (12, {}), {6}: (13, {})} | custom-call | flops 4026531840 | bytes 2097152 | tf_op jit(solution)/shard_map/pallas_call | solution.py:305
  132.7 2.1 shard_map.245
  134.8 2.6 collective-permute-start.12
  138.5 2.6 shard_map.246
  141.1 15.1 %shard_map.247 = (bf16[1024,128]{1,0:T(8,128)(2,1)}, bf16[1024,384]{1,0:T(8,128)(2,1)}, f32[1,384]{1,0:T(1,128)}, bf16[512,512]{1,0:T(8,128)(2,1)}, bf16[512,512...) custom-call(s32[2]{0:T(128)} %pad_add_fusion.1.refs_0_, ...), custom_call_target="tpu_custom_call" | custom-call | flops 4026531840 | bytes 2097152 | tf_op jit(solution)/shard_map/pallas_call | solution.py:305
  158.6 2.1 shard_map.248
  163.5 2.7 shard_map.249
  168.5 14.8 %shard_map.250 = (bf16[1024,128]{1,0:T(8,128)(2,1)}, bf16[1024,384]{1,0:T(8,128)(2,1)}, f32[1,384]{1,0:T(1,128)}, bf16[512,512]{1,0:T(8,128)(2,1)}, bf16[512,512...) custom-call(s32[2]{0:T(128)} %pad_add_fusion.1.refs_0_, ...), custom_call_target="tpu_custom_call", output_to_operand_aliasing={{3}: (10, {}), {4}: (11, {}), {5}: (12, {}), {6}: (13, {})} | custom-call | flops 4026531840 | bytes 2097152 | tf_op jit(solution)/shard_map/pallas_call | solution.py:305
  184.1 2.2 shard_map.251
  187.1 2.0 shard_map.252
  189.2 9.6 %shard_map.253 = (bf16[1024,512]{1,0:T(8,128)(2,1)}, bf16[1024,512]{1,0:T(8,128)(2,1)}, f32[1,512]{1,0:T(1,128)}, bf16[512,512]{1,0:T(8,128)(2,1)}, bf16[512,512...) custom-call(s32[2]{0:T(128)} %pad_add_fusion.1.refs_0_, ...), custom_call_target="tpu_custom_call" | custom-call | flops 4294967296 | bytes 10485760 | tf_op jit(solution)/shard_map/pallas_call | solution.py:149
  201.4 9.9 %collective-permute-done.22.refs_1_ = bf16[512,512]{1,0:T(8,128)(2,1)S(1)} collective-permute-done((bf16[512,512]{1,0:T(8,128)(2,1)S(1)}, bf16[512,512]{1,0:T(8,128)(2,1)S(1)}, u32[]{:S(2)}, u32[]{:S(2)}) %collective-permute-start.22) | collective-permute-done | bytes 524320 | tf_op jit(solution)/shard_map/ppermute | solution.py:565
  213.0 2.6 shard_map.255
  220.2 4.9 collective-permute-done.25.refs_1_
  227.1 16.4 %collective-permute-done.26.refs_3_ = bf16[256,512]{1,0:T(8,128)(2,1)} collective-permute-done((bf16[256,512]{1,0:T(8,128)(2,1)}, bf16[256,512]{1,0:T(8,128)(2,1)}, u32[]{:S(2)}, u32[]{:S(2)}) %collective-permute-start.26) | collective-permute-done | bytes 262176 | tf_op jit(solution)/shard_map/ppermute | solution.py:568
  243.5 2.1 shard_map.257
  245.6 2.9 collective-permute-start.39
  249.5 2.7 shard_map.258
  255.3 5.4 %shard_map.254 = (f32[1024,2048]{1,0:T(8,128)}, f32[2048,1024]{1,0:T(8,128)}, f32[8,128]{1,0:T(8,128)}) custom-call(s32[2]{0:T(128)} %get-tuple-element.273.left_ref, s32[2]{0:T(128)} %get-tuple-element.274.right_ref, bf16[512,512]{1,0:T(8,128)(2,1)} %get-tuple-element.186.refs_7_.refs_0_, bf16[512,512]{1,0:T(8,128)(2,1)} %copy-done.21, ...), custom_call_target="tpu_custom_call" | custom-call | bytes 6291456 | tf_op jit(solution)/shard_map/pallas_call | solution.py:629
  260.7 11.7 %shard_map.256 = (bf16[512,1024]{1,0:T(8,128)(2,1)}, bf16[512,1024]{1,0:T(8,128)(2,1)}) custom-call(s32[2]{0:T(128)} %pad_add_fusion.refs_0_, bf16[1024,128]{1,0:T(8,128)(2,1)} %get-tuple-element.146.refs_1_, bf16[1024,128]{1,0:T(8,128)(2,1)} %get-tuple-element.160.refs_2_, bf16[1024,128]{1,0:T(8,128)(2,1)} %get-tuple-element.170.refs_3_, ...), custom_call_target="tpu_custom_call" | custom-call | flops 5368709120 | bytes 16777216 | tf_op jit(solution)/shard_map/pallas_call | solution.py:406
  272.4 10.3 %all-reduce.3.cloned.1.call-done = (bf16[256,1024]{1,0:T(8,128)(2,1)}, bf16[512,512]{1,0:T(8,128)(2,1)}, bf16[256,512]{1,0:T(8,128)(2,1)}, bf16[256,512]{1,0:T(8,128)(2,1)}) async-done(((bf16[256,1024]{1,0:T(8,128)(2,1)}, bf16[512,512]{1,0:T(8,128)(2,1)}, bf16[256,512]{1,0:T(8,128)(2,1)}, bf16[256,512]{1,0:T(8,128)(2,1)}), (bf16[256,1024]{1,0:T(8,128)(2,1)}, bf16[512,512]{1,0:T(8,128)(2,1)}, ...) | async-done | bytes 1572880 | tf_op jit(solution)/shard_map/psum | solution.py:572
  282.7 16.7 %shard_map.259 = (bf16[512,1024]{1,0:T(8,128)(2,1)}, f32[512,1024]{1,0:T(8,128)}, f32[4,1024]{1,0:T(4,128)}) custom-call(s32[2]{0:T(128)} %pad_add_fusion.refs_0_, bf16[1024,384]{1,0:T(8,128)(2,1)} %get-tuple-element.205.refs_1_, bf16[1024,384]{1,0:T(8,128)(2,1)} %get-tuple-element.206.refs_2_, bf16[1024,384]{1,0:T(8,128)(2,1)} %get-tuple-element.207.refs_3_, ...), custom_call_target="tpu_custom_call" | custom-call | flops 7516192768 | bytes 16777216 | tf_op jit(solution)/shard_map/pallas_call | solution.py:406
  299.5 2.1 shard_map.262
  301.6 2.4 collective-permute-start.41
  305.3 2.1 shard_map.266
  309.7 13.4 %collective-permute-done.41.refs_1_ = bf16[256,512]{1,0:T(8,128)(2,1)S(1)} collective-permute-done((bf16[256,512]{1,0:T(8,128)(2,1)}, bf16[256,512]{1,0:T(8,128)(2,1)S(1)}, u32[]{:S(2)}, u32[]{:S(2)}) %collective-permute-start.41) | collective-permute-done | bytes 262176 | tf_op jit(solution)/shard_map/ppermute | solution.py:580
  323.1 5.1 %collective-permute-done.42.refs_3_ = bf16[256,512]{1,0:T(8,128)(2,1)S(1)} collective-permute-done((bf16[256,512]{1,0:T(8,128)(2,1)}, bf16[256,512]{1,0:T(8,128)(2,1)S(1)}, u32[]{:S(2)}, u32[]{:S(2)}) %collective-permute-start.42) | collective-permute-done | bytes 262176 | tf_op jit(solution)/shard_map/ppermute | solution.py:580
  335.4 2.1 shard_map.267
  341.6 15.2 %collective-permute-done.51.refs_1_ = bf16[256,512]{1,0:T(8,128)(2,1)S(1)} collective-permute-done((bf16[256,512]{1,0:T(8,128)(2,1)}, bf16[256,512]{1,0:T(8,128)(2,1)S(1)}, u32[]{:S(2)}, u32[]{:S(2)}) %collective-permute-start.51) | collective-permute-done | bytes 262176 | tf_op jit(solution)/shard_map/ppermute | solution.py:580
  357.9 2.2 shard_map.264
  360.1 2.3 collective-permute-done.52.refs_3_
  362.7 2.1 shard_map.268
  367.0 2.2 shard_map.260
  370.7 2.1 fusion.11
  373.5 11.9 %collective-permute-done.53.refs_1_ = bf16[256,512]{1,0:T(8,128)(2,1)S(1)} collective-permute-done((bf16[256,512]{1,0:T(8,128)(2,1)}, bf16[256,512]{1,0:T(8,128)(2,1)S(1)}, u32[]{:S(2)}, u32[]{:S(2)}) %collective-permute-start.53) | collective-permute-done | bytes 262176 | tf_op jit(solution)/shard_map/ppermute | solution.py:584
  388.1 3.6 convert_reduce_fusion.1
  392.0 2.3 shard_map.269
  394.3 2.9 shard_map.265
  397.2 2.3 reshape.205
  403.2 2.9 shard_map.270
  406.1 5.8 %collective-permute-done.37.refs_1_ = bf16[512,512]{1,0:T(8,128)(2,1)} collective-permute-done((bf16[512,512]{1,0:T(8,128)(2,1)}, bf16[512,512]{1,0:T(8,128)(2,1)}, u32[]{:S(2)}, u32[]{:S(2)}) %collective-permute-start.37) | collective-permute-done | bytes 524320 | tf_op jit(solution)/shard_map/ppermute | solution.py:587
  414.1 2.9 shard_map.261
  417.1 2.2 reshape.204
  419.7 4.2 maximum_bitcast_fusion.1
  423.9 2.1 reshape.201
  426.0 16.8 %collective-permute-done.31 = f32[8704]{0:T(1024)S(1)} collective-permute-done((f32[8704]{0:T(1024)S(1)}, f32[8704]{0:T(1024)S(1)}, u32[]{:S(2)}, u32[]{:S(2)}) %collective-permute-start.31) | collective-permute-done | bytes 34848 | tf_op jit(solution)/shard_map/ppermute | solution.py:655
  443.5 5.2 %maximum_bitcast_fusion = bf16[1024,2,4,128]{3,1,2,0:T(2,128)(2,1)} fusion(bf16[1024,2,2,128]{3,2,1,0:T(2,128)(2,1)S(1)} %reshape.202, bf16[1024,2,2,128]{3,2,1,0:T(2,128)(2,1)} %reshape.201), kind=kLoop, calls=%fused_computation.18 | loop fusion | flops 1048576 | bytes 4194304 | tf_op jit(solution)/shard_map/transpose | solution.py:860
  450.6 4.1 reshape.206
  458.8 4.1 reshape.203
  462.9 2.1 collective-permute-start.34
  465.0 4.7 maximum_convert_fusion
  471.4 2.8 copy.55
  477.8 7.0 %shard_map.271 = (f32[1024,2048]{1,0:T(8,128)}, f32[2048,1024]{1,0:T(8,128)}, f32[8,128]{1,0:T(8,128)}) custom-call(s32[2]{0:T(128)} %get-tuple-element.273.left_ref, s32[2]{0:T(128)} %get-tuple-element.274.right_ref, bf16[512,1024]{1,0:T(8,128)(2,1)} %get-tuple-element.245.refs_0_, ...), custom_call_target="tpu_custom_call", output_to_operand_aliasing={{0}: (6, {}), {1}: (7, {})} | custom-call | bytes 12582912 | tf_op jit(solution)/shard_map/pallas_call | solution.py:629
  484.9 5.2 %shard_map.272 = (f32[1024,2048]{1,0:T(8,128)}, f32[2048,1024]{1,0:T(8,128)}, f32[8,128]{1,0:T(8,128)}) custom-call(s32[2]{0:T(128)} %get-tuple-element.273.left_ref, s32[2]{0:T(128)} %get-tuple-element.274.right_ref, bf16[512,512]{1,0:T(8,128)(2,1)} %get-tuple-element.243.refs_0_, ...), custom_call_target="tpu_custom_call", output_to_operand_aliasing={{0}: (6, {}), {1}: (7, {})} | custom-call | bytes 6291456 | tf_op jit(solution)/shard_map/pallas_call | solution.py:629
  (275 shorter events, 90.1 us)
Async XLA Ops:
  7.2 3.5 collective-permute-start
  7.7 4.0 collective-permute-start.1
  43.7 59.4 %collective-permute-start.6 = (bf16[512,1024]{1,0:T(8,128)(2,1)}, bf16[512,1024]{1,0:T(8,128)(2,1)S(1)}, u32[]{:S(2)}, u32[]{:S(2)}) collective-permute-start(bf16[512,1024]{1,0:T(8,128)(2,1)} %get-tuple-element.144.refs_13_), channel_id=1, source_target_pairs={{0,2},{2,0},{1,3},{3,1},{4,6},{6,4},{5,7},{7,5},{8,10},{10,8},{9,1... | collective-permute-start | bytes 3145736 | tf_op jit(solution)/shard_map/ppermute | solution.py:565
  46.6 56.5 %collective-permute-start.7 = (bf16[1024,512]{1,0:T(8,128)(2,1)}, bf16[1024,512]{1,0:T(8,128)(2,1)S(1)}, u32[]{:S(2)}, u32[]{:S(2)}) collective-permute-start(bf16[1024,512]{1,0:T(8,128)(2,1)} %get-tuple-element.145.refs_14_), channel_id=1, source_target_pairs={{0,4},{4,0},{1,5},{5,1},{2,6},{6,2},{3,7},{7,3},{8,12},{12,8},{9,1... | collective-permute-start | bytes 3145736 | tf_op jit(solution)/shard_map/ppermute | solution.py:565
  48.1 33.4 %collective-permute-start.2 = (bf16[512,512]{1,0:T(8,128)(2,1)}, bf16[512,512]{1,0:T(8,128)(2,1)S(1)}, u32[]{:S(2)}, u32[]{:S(2)}) collective-permute-start(bf16[512,512]{1,0:T(8,128)(2,1)} %get-tuple-element.137.refs_7_), channel_id=1, source_target_pairs={{0,2},{2,0},{1,3},{3,1},{4,6},{6,4},{5,7},{7,5},{8,10},{10,8},{9,1... | collective-permute-start | bytes 1572872 | tf_op jit(solution)/shard_map/ppermute | solution.py:565
  48.7 34.2 %collective-permute-start.3 = (bf16[512,512]{1,0:T(8,128)(2,1)}, bf16[512,512]{1,0:T(8,128)(2,1)S(1)}, u32[]{:S(2)}, u32[]{:S(2)}) collective-permute-start(bf16[512,512]{1,0:T(8,128)(2,1)} %get-tuple-element.138.refs_8_), channel_id=1, source_target_pairs={{0,4},{4,0},{1,5},{5,1},{2,6},{6,2},{3,7},{7,3},{8,12},{12,8},{9,1... | collective-permute-start | bytes 1572872 | tf_op jit(solution)/shard_map/ppermute | solution.py:565
  86.4 23.8 %collective-permute-start.4 = (bf16[256,512]{1,0:T(8,128)(2,1)}, bf16[256,512]{1,0:T(8,128)(2,1)S(1)}, u32[]{:S(2)}, u32[]{:S(2)}) collective-permute-start(bf16[256,512]{1,0:T(8,128)(2,1)} %get-tuple-element.142.refs_11_), channel_id=1, source_target_pairs={{0,4},{4,0},{1,5},{5,1},{2,6},{6,2},{3,7},{7,3},{8,12},{12,8},{9,1... | collective-permute-start | bytes 786440 | tf_op jit(solution)/shard_map/ppermute | solution.py:568
  87.9 22.3 %collective-permute-start.5 = (bf16[256,512]{1,0:T(8,128)(2,1)}, bf16[256,512]{1,0:T(8,128)(2,1)S(1)}, u32[]{:S(2)}, u32[]{:S(2)}) collective-permute-start(bf16[256,512]{1,0:T(8,128)(2,1)} %get-tuple-element.143.refs_12_), channel_id=1, source_target_pairs={{0,2},{2,0},{1,3},{3,1},{4,6},{6,4},{5,7},{7,5},{8,10},{10,8},{9,1... | collective-permute-start | bytes 786440 | tf_op jit(solution)/shard_map/ppermute | solution.py:568
  108.2 29.2 %collective-permute-start.10 = (bf16[256,1024]{1,0:T(8,128)(2,1)}, bf16[256,1024]{1,0:T(8,128)(2,1)S(1)}, u32[]{:S(2)}, u32[]{:S(2)}) collective-permute-start(bf16[256,1024]{1,0:T(8,128)(2,1)} %get-tuple-element.158.refs_17_), channel_id=1, source_target_pairs={{0,4},{4,0},{1,5},{5,1},{2,6},{6,2},{3,7},{7,3},{8,12},{12,8},{9,1... | collective-permute-start | bytes 1572872 | tf_op jit(solution)/shard_map/ppermute | solution.py:568
  108.6 29.1 %collective-permute-start.11 = (bf16[512,512]{1,0:T(8,128)(2,1)}, bf16[512,512]{1,0:T(8,128)(2,1)S(1)}, u32[]{:S(2)}, u32[]{:S(2)}) collective-permute-start(bf16[512,512]{1,0:T(8,128)(2,1)} %get-tuple-element.159.refs_18_), channel_id=1, source_target_pairs={{0,2},{2,0},{1,3},{3,1},{4,6},{6,4},{5,7},{7,5},{8,10},{10,8},{9,1... | collective-permute-start | bytes 1572872 | tf_op jit(solution)/shard_map/ppermute | solution.py:568
  113.1 17.3 %collective-permute-start.8 = (bf16[256,512]{1,0:T(8,128)(2,1)}, bf16[256,512]{1,0:T(8,128)(2,1)S(1)}, u32[]{:S(2)}, u32[]{:S(2)}) collective-permute-start(bf16[256,512]{1,0:T(8,128)(2,1)} %get-tuple-element.154.refs_15_.refs_2_), channel_id=1, source_target_pairs={{0,8},{8,0},{16,24},{24,16},{1,9},{9,1},{17,25},{25,17},{2,10},{10... | collective-permute-start | bytes 786440 | tf_op jit(solution)/shard_map/ppermute | solution.py:580
  114.6 17.4 %collective-permute-start.9 = (bf16[256,512]{1,0:T(8,128)(2,1)}, bf16[256,512]{1,0:T(8,128)(2,1)S(1)}, u32[]{:S(2)}, u32[]{:S(2)}) collective-permute-start(bf16[256,512]{1,0:T(8,128)(2,1)} %get-tuple-element.155.refs_16_.refs_4_), channel_id=1, source_target_pairs={{0,8},{8,0},{16,24},{24,16},{1,9},{9,1},{17,25},{25,17},{2,10},{10... | collective-permute-start | bytes 786440 | tf_op jit(solution)/shard_map/ppermute | solution.py:580
  129.9 32.6 %collective-permute-start.14 = (bf16[512,512]{1,0:T(8,128)(2,1)}, bf16[512,512]{1,0:T(8,128)(2,1)S(1)}, u32[]{:S(2)}, u32[]{:S(2)}) collective-permute-start(bf16[512,512]{1,0:T(8,128)(2,1)} %get-tuple-element.168.refs_15_), channel_id=1, source_target_pairs={{0,2},{2,0},{1,3},{3,1},{4,6},{6,4},{5,7},{7,5},{8,10},{10,8},{9,1... | collective-permute-start | bytes 1572872 | tf_op jit(solution)/shard_map/ppermute | solution.py:565
  130.4 32.1 %collective-permute-start.15 = (bf16[512,512]{1,0:T(8,128)(2,1)}, bf16[512,512]{1,0:T(8,128)(2,1)S(1)}, u32[]{:S(2)}, u32[]{:S(2)}) collective-permute-start(bf16[512,512]{1,0:T(8,128)(2,1)} %get-tuple-element.169.refs_16_), channel_id=1, source_target_pairs={{0,4},{4,0},{1,5},{5,1},{2,6},{6,2},{3,7},{7,3},{8,12},{12,8},{9,1... | collective-permute-start | bytes 1572872 | tf_op jit(solution)/shard_map/ppermute | solution.py:565
  134.8 21.4 %collective-permute-start.12 = (bf16[256,512]{1,0:T(8,128)(2,1)}, bf16[256,512]{1,0:T(8,128)(2,1)S(1)}, u32[]{:S(2)}, u32[]{:S(2)}) collective-permute-start(bf16[256,512]{1,0:T(8,128)(2,1)} %get-tuple-element.162.refs_11_.refs_2_), channel_id=1, source_target_pairs={{0,16},{8,24},{16,0},{24,8},{1,17},{9,25},{17,1},{25,9},{2,18},{10... | collective-permute-start | bytes 786440 | tf_op jit(solution)/shard_map/ppermute | solution.py:580
  137.4 20.6 %collective-permute-start.13 = (bf16[256,512]{1,0:T(8,128)(2,1)}, bf16[256,512]{1,0:T(8,128)(2,1)S(1)}, u32[]{:S(2)}, u32[]{:S(2)}) collective-permute-start(bf16[256,512]{1,0:T(8,128)(2,1)} %get-tuple-element.163.refs_12_.refs_4_), channel_id=1, source_target_pairs={{0,16},{8,24},{16,0},{24,8},{1,17},{9,25},{17,1},{25,9},{2,18},{10... | collective-permute-start | bytes 786440 | tf_op jit(solution)/shard_map/ppermute | solution.py:580
  160.7 22.5 %collective-permute-start.16 = (bf16[256,512]{1,0:T(8,128)(2,1)}, bf16[256,512]{1,0:T(8,128)(2,1)S(1)}, u32[]{:S(2)}, u32[]{:S(2)}) collective-permute-start(bf16[256,512]{1,0:T(8,128)(2,1)} %get-tuple-element.176.refs_15_.refs_2_), channel_id=1, source_target_pairs={{0,4},{4,0},{1,5},{5,1},{2,6},{6,2},{3,7},{7,3},{8,12},{12,8},{9,1... | collective-permute-start | bytes 786440 | tf_op jit(solution)/shard_map/ppermute | solution.py:584
  161.2 22.1 %collective-permute-start.17 = (bf16[256,512]{1,0:T(8,128)(2,1)}, bf16[256,512]{1,0:T(8,128)(2,1)S(1)}, u32[]{:S(2)}, u32[]{:S(2)}) collective-permute-start(bf16[256,512]{1,0:T(8,128)(2,1)} %get-tuple-element.177.refs_16_.refs_4_), channel_id=1, source_target_pairs={{0,2},{2,0},{1,3},{3,1},{4,6},{6,4},{5,7},{7,5},{8,10},{10,8},{9,1... | collective-permute-start | bytes 786440 | tf_op jit(solution)/shard_map/ppermute | solution.py:584
  166.2 20.2 %collective-permute-start.18 = (bf16[256,512]{1,0:T(8,128)(2,1)}, bf16[256,512]{1,0:T(8,128)(2,1)S(1)}, u32[]{:S(2)}, u32[]{:S(2)}) collective-permute-start(bf16[256,512]{1,0:T(8,128)(2,1)} %get-tuple-element.180.refs_17_), channel_id=1, source_target_pairs={{0,4},{4,0},{1,5},{5,1},{2,6},{6,2},{3,7},{7,3},{8,12},{12,8},{9,1... | collective-permute-start | bytes 786440 | tf_op jit(solution)/shard_map/ppermute | solution.py:568
  167.7 18.6 %collective-permute-start.19 = (bf16[256,512]{1,0:T(8,128)(2,1)}, bf16[256,512]{1,0:T(8,128)(2,1)S(1)}, u32[]{:S(2)}, u32[]{:S(2)}) collective-permute-start(bf16[256,512]{1,0:T(8,128)(2,1)} %get-tuple-element.181.refs_18_), channel_id=1, source_target_pairs={{0,2},{2,0},{1,3},{3,1},{4,6},{6,4},{5,7},{7,5},{8,10},{10,8},{9,1... | collective-permute-start | bytes 786440 | tf_op jit(solution)/shard_map/ppermute | solution.py:568
  198.8 83.9 %all-reduce.3.cloned.1.call-start = ((), (), s32[]{:S(2)}) async-start(), calls=%async_computation | async-start | bytes 3145728 | tf_op jit(solution)/shard_map/psum | solution.py:572
  199.6 11.7 %collective-permute-start.22 = (bf16[512,512]{1,0:T(8,128)(2,1)S(1)}, bf16[512,512]{1,0:T(8,128)(2,1)S(1)}, u32[]{:S(2)}, u32[]{:S(2)}) collective-permute-start(bf16[512,512]{1,0:T(8,128)(2,1)S(1)} %copy-done.59), channel_id=1, source_target_pairs={{0,2},{2,0},{1,3},{3,1},{4,6},{6,4},{5,7},{7,5},{8,10},{10,8},{9,1... | collective-permute-start | bytes 1572872 | tf_op jit(solution)/shard_map/ppermute | solution.py:565
  200.9 11.4 %collective-permute-start.23 = (bf16[512,512]{1,0:T(8,128)(2,1)S(1)}, bf16[512,512]{1,0:T(8,128)(2,1)S(1)}, u32[]{:S(2)}, u32[]{:S(2)}) collective-permute-start(bf16[512,512]{1,0:T(8,128)(2,1)S(1)} %copy-done.60), channel_id=1, source_target_pairs={{0,4},{4,0},{1,5},{5,1},{2,6},{6,2},{3,7},{7,3},{8,12},{12,8},{9,1... | collective-permute-start | bytes 1572872 | tf_op jit(solution)/shard_map/ppermute | solution.py:565
  215.6 9.5 %collective-permute-start.25 = (bf16[256,512]{1,0:T(8,128)(2,1)}, bf16[256,512]{1,0:T(8,128)(2,1)S(1)}, u32[]{:S(2)}, u32[]{:S(2)}) collective-permute-start(bf16[256,512]{1,0:T(8,128)(2,1)} %get-tuple-element.199.refs_12_), channel_id=1, source_target_pairs={{0,4},{4,0},{1,5},{5,1},{2,6},{6,2},{3,7},{7,3},{8,12},{12,8},{9,1... | collective-permute-start | bytes 786440 | tf_op jit(solution)/shard_map/ppermute | solution.py:568
  216.2 32.3 %collective-permute-start.27 = (bf16[512,512]{1,0:T(8,128)(2,1)}, bf16[512,512]{1,0:T(8,128)(2,1)S(1)}, u32[]{:S(2)}, u32[]{:S(2)}) collective-permute-start(bf16[512,512]{1,0:T(8,128)(2,1)} %get-tuple-element.201.refs_14_), channel_id=1, source_target_pairs={{0,2},{2,0},{1,3},{3,1},{4,6},{6,4},{5,7},{7,5},{8,10},{10,8},{9,1... | collective-permute-start | bytes 1572872 | tf_op jit(solution)/shard_map/ppermute | solution.py:565
  216.9 31.7 %collective-permute-start.28 = (bf16[512,512]{1,0:T(8,128)(2,1)}, bf16[512,512]{1,0:T(8,128)(2,1)S(1)}, u32[]{:S(2)}, u32[]{:S(2)}) collective-permute-start(bf16[512,512]{1,0:T(8,128)(2,1)} %get-tuple-element.202.refs_15_), channel_id=1, source_target_pairs={{0,4},{4,0},{1,5},{5,1},{2,6},{6,2},{3,7},{7,3},{8,12},{12,8},{9,1... | collective-permute-start | bytes 1572872 | tf_op jit(solution)/shard_map/ppermute | solution.py:565
  218.4 35.3 %collective-permute-start.20 = (bf16[512,512]{1,0:T(8,128)(2,1)S(1)}, bf16[512,512]{1,0:T(8,128)(2,1)S(1)}, u32[]{:S(2)}, u32[]{:S(2)}) collective-permute-start(bf16[512,512]{1,0:T(8,128)(2,1)S(1)} %copy-done.19), channel_id=1, source_target_pairs={{0,2},{2,0},{1,3},{3,1},{4,6},{6,4},{5,7},{7,5},{8,10},{10,8},{9,1... | collective-permute-start | bytes 1572872 | tf_op jit(solution)/shard_map/ppermute | solution.py:587
  219.7 34.8 %collective-permute-start.21 = (bf16[512,512]{1,0:T(8,128)(2,1)S(1)}, bf16[512,512]{1,0:T(8,128)(2,1)S(1)}, u32[]{:S(2)}, u32[]{:S(2)}) collective-permute-start(bf16[512,512]{1,0:T(8,128)(2,1)S(1)} %copy-done.20), channel_id=1, source_target_pairs={{0,4},{4,0},{1,5},{5,1},{2,6},{6,2},{3,7},{7,3},{8,12},{12,8},{9,1... | collective-permute-start | bytes 1572872 | tf_op jit(solution)/shard_map/ppermute | solution.py:587
  225.1 18.4 %collective-permute-start.26 = (bf16[256,512]{1,0:T(8,128)(2,1)}, bf16[256,512]{1,0:T(8,128)(2,1)}, u32[]{:S(2)}, u32[]{:S(2)}) collective-permute-start(bf16[256,512]{1,0:T(8,128)(2,1)} %get-tuple-element.200.refs_13_), channel_id=1, source_target_pairs={{0,2},{2,0},{1,3},{3,1},{4,6},{6,4},{5,7},{7,5},{8,10},{10,8},{9,1... | collective-permute-start | bytes 786440 | tf_op jit(solution)/shard_map/ppermute | solution.py:568
  245.6 53.8 %collective-permute-start.39 = (bf16[256,512]{1,0:T(8,128)(2,1)}, bf16[256,512]{1,0:T(8,128)(2,1)}, u32[]{:S(2)}, u32[]{:S(2)}) collective-permute-start(bf16[256,512]{1,0:T(8,128)(2,1)} %get-tuple-element.214.refs_16_.refs_2_), channel_id=1, source_target_pairs={{0,8},{8,0},{16,24},{24,16},{1,9},{9,1},{17,25},{25,17},{2,10},{10... | collective-permute-start | bytes 786440 | tf_op jit(solution)/shard_map/ppermute | solution.py:580
  248.5 50.9 %collective-permute-start.40 = (bf16[256,512]{1,0:T(8,128)(2,1)}, bf16[256,512]{1,0:T(8,128)(2,1)}, u32[]{:S(2)}, u32[]{:S(2)}) collective-permute-start(bf16[256,512]{1,0:T(8,128)(2,1)} %get-tuple-element.215.refs_17_.refs_4_), channel_id=1, source_target_pairs={{0,8},{8,0},{16,24},{24,16},{1,9},{9,1},{17,25},{25,17},{2,10},{10... | collective-permute-start | bytes 786440 | tf_op jit(solution)/shard_map/ppermute | solution.py:580
  252.1 52.4 %collective-permute-start.47 = (bf16[256,512]{1,0:T(8,128)(2,1)}, bf16[256,512]{1,0:T(8,128)(2,1)S(1)}, u32[]{:S(2)}, u32[]{:S(2)}) collective-permute-start(bf16[256,512]{1,0:T(8,128)(2,1)} %get-tuple-element.218.refs_18_), channel_id=1, source_target_pairs={{0,4},{4,0},{1,5},{5,1},{2,6},{6,2},{3,7},{7,3},{8,12},{12,8},{9,1... | collective-permute-start | bytes 786440 | tf_op jit(solution)/shard_map/ppermute | solution.py:568
  253.7 50.8 %collective-permute-start.48 = (bf16[256,512]{1,0:T(8,128)(2,1)}, bf16[256,512]{1,0:T(8,128)(2,1)S(1)}, u32[]{:S(2)}, u32[]{:S(2)}) collective-permute-start(bf16[256,512]{1,0:T(8,128)(2,1)} %get-tuple-element.219.refs_19_), channel_id=1, source_target_pairs={{0,2},{2,0},{1,3},{3,1},{4,6},{6,4},{5,7},{7,5},{8,10},{10,8},{9,1... | collective-permute-start | bytes 786440 | tf_op jit(solution)/shard_map/ppermute | solution.py:568
  299.4 69.8 %collective-permute-start.29 = (bf16[512,1024]{1,0:T(8,128)(2,1)}, bf16[512,1024]{1,0:T(8,128)(2,1)}, u32[]{:S(2)}, u32[]{:S(2)}) collective-permute-start(bf16[512,1024]{1,0:T(8,128)(2,1)} %get-tuple-element.220), channel_id=1, source_target_pairs={{0,1},{1,0},{2,3},{3,2},{4,5},{5,4},{6,7},{7,6},{8,9},{9,8},{10,11... | collective-permute-start | bytes 3145736 | tf_op jit(solution)/shard_map/ppermute | solution.py:828
  301.6 21.6 %collective-permute-start.41 = (bf16[256,512]{1,0:T(8,128)(2,1)}, bf16[256,512]{1,0:T(8,128)(2,1)S(1)}, u32[]{:S(2)}, u32[]{:S(2)}) collective-permute-start(bf16[256,512]{1,0:T(8,128)(2,1)} %get-tuple-element.226.refs_2_), channel_id=1, source_target_pairs={{0,16},{8,24},{16,0},{24,8},{1,17},{9,25},{17,1},{25,9},{2,18},{10... | collective-permute-start | bytes 786440 | tf_op jit(solution)/shard_map/ppermute | solution.py:580
  304.0 24.3 %collective-permute-start.42 = (bf16[256,512]{1,0:T(8,128)(2,1)}, bf16[256,512]{1,0:T(8,128)(2,1)S(1)}, u32[]{:S(2)}, u32[]{:S(2)}) collective-permute-start(bf16[256,512]{1,0:T(8,128)(2,1)} %get-tuple-element.227.refs_4_), channel_id=1, source_target_pairs={{0,16},{8,24},{16,0},{24,8},{1,17},{9,25},{17,1},{25,9},{2,18},{10... | collective-permute-start | bytes 786440 | tf_op jit(solution)/shard_map/ppermute | solution.py:580
  307.4 26.6 %collective-permute-start.49 = (bf16[256,512]{1,0:T(8,128)(2,1)}, bf16[256,512]{1,0:T(8,128)(2,1)S(1)}, u32[]{:S(2)}, u32[]{:S(2)}) collective-permute-start(bf16[256,512]{1,0:T(8,128)(2,1)} %get-tuple-element.237.refs_2_), channel_id=1, source_target_pairs={{0,8},{8,0},{16,24},{24,16},{1,9},{9,1},{17,25},{25,17},{2,10},{10... | collective-permute-start | bytes 786440 | tf_op jit(solution)/shard_map/ppermute | solution.py:580
  308.9 48.9 %copy-start.54 = (f32[1,384]{1,0:T(1,128)S(1)}, f32[1,384]{1,0:T(1,128)}, u32[]{:S(2)}) copy-start(f32[1,384]{1,0:T(1,128)} %get-tuple-element.185.refs_5_.refs_6_) | copy-start | bytes 4612
  308.9 49.0 %copy-start.53 = (f32[1,384]{1,0:T(1,128)S(1)}, f32[1,384]{1,0:T(1,128)}, u32[]{:S(2)}) copy-start(f32[1,384]{1,0:T(1,128)} %get-tuple-element.175.refs_5_.refs_14_) | copy-start | bytes 4612
  308.9 25.1 %collective-permute-start.50 = (bf16[256,512]{1,0:T(8,128)(2,1)}, bf16[256,512]{1,0:T(8,128)(2,1)S(1)}, u32[]{:S(2)}, u32[]{:S(2)}) collective-permute-start(bf16[256,512]{1,0:T(8,128)(2,1)} %get-tuple-element.238.refs_4_), channel_id=1, source_target_pairs={{0,8},{8,0},{16,24},{24,16},{1,9},{9,1},{17,25},{25,17},{2,10},{10... | collective-permute-start | bytes 786440 | tf_op jit(solution)/shard_map/ppermute | solution.py:580
  331.0 8.0 %collective-permute-start.43 = (bf16[256,512]{1,0:T(8,128)(2,1)}, bf16[256,512]{1,0:T(8,128)(2,1)S(1)}, u32[]{:S(2)}, u32[]{:S(2)}) collective-permute-start(bf16[256,512]{1,0:T(8,128)(2,1)} %get-tuple-element.228.refs_2_), channel_id=1, source_target_pairs={{0,4},{4,0},{1,5},{5,1},{2,6},{6,2},{3,7},{7,3},{8,12},{12,8},{9,1... | collective-permute-start | bytes 786440 | tf_op jit(solution)/shard_map/ppermute | solution.py:584
  332.5 8.5 %collective-permute-start.44 = (bf16[256,512]{1,0:T(8,128)(2,1)}, bf16[256,512]{1,0:T(8,128)(2,1)S(1)}, u32[]{:S(2)}, u32[]{:S(2)}) collective-permute-start(bf16[256,512]{1,0:T(8,128)(2,1)} %get-tuple-element.229.refs_4_), channel_id=1, source_target_pairs={{0,2},{2,0},{1,3},{3,1},{4,6},{6,4},{5,7},{7,5},{8,10},{10,8},{9,1... | collective-permute-start | bytes 786440 | tf_op jit(solution)/shard_map/ppermute | solution.py:584
  337.5 19.3 %collective-permute-start.51 = (bf16[256,512]{1,0:T(8,128)(2,1)}, bf16[256,512]{1,0:T(8,128)(2,1)S(1)}, u32[]{:S(2)}, u32[]{:S(2)}) collective-permute-start(bf16[256,512]{1,0:T(8,128)(2,1)} %get-tuple-element.239.refs_2_), channel_id=1, source_target_pairs={{0,16},{8,24},{16,0},{24,8},{1,17},{9,25},{17,1},{25,9},{2,18},{10... | collective-permute-start | bytes 786440 | tf_op jit(solution)/shard_map/ppermute | solution.py:580
  337.9 35.0 %collective-permute-start.24 = (bf16[512,1024]{1,0:T(8,128)(2,1)}, bf16[512,1024]{1,0:T(8,128)(2,1)}, u32[]{:S(2)}, u32[]{:S(2)}) collective-permute-start(bf16[512,1024]{1,0:T(8,128)(2,1)} %get-tuple-element.203.refs_20_), channel_id=1, source_target_pairs={{0,1},{1,0},{2,3},{3,2},{4,5},{5,4},{6,7},{7,6},{8,9},{9,8},{10,11... | collective-permute-start | bytes 3145736 | tf_op jit(solution)/shard_map/ppermute | solution.py:827
  339.0 23.4 %collective-permute-start.52 = (bf16[256,512]{1,0:T(8,128)(2,1)}, bf16[256,512]{1,0:T(8,128)(2,1)}, u32[]{:S(2)}, u32[]{:S(2)}) collective-permute-start(bf16[256,512]{1,0:T(8,128)(2,1)} %get-tuple-element.240.refs_4_), channel_id=1, source_target_pairs={{0,16},{8,24},{16,0},{24,8},{1,17},{9,25},{17,1},{25,9},{2,18},{10... | collective-permute-start | bytes 786440 | tf_op jit(solution)/shard_map/ppermute | solution.py:580
  341.0 23.8 %collective-permute-start.35 = (bf16[256,512]{1,0:T(8,128)(2,1)S(1)}, bf16[256,512]{1,0:T(8,128)(2,1)}, u32[]{:S(2)}, u32[]{:S(2)}) collective-permute-start(bf16[256,512]{1,0:T(8,128)(2,1)S(1)} %copy-done.25), channel_id=1, source_target_pairs={{0,4},{4,0},{1,5},{5,1},{2,6},{6,2},{3,7},{7,3},{8,12},{12,8},{9,1... | collective-permute-start | bytes 786440 | tf_op jit(solution)/shard_map/ppermute | solution.py:584
  357.5 9.0 %collective-permute-start.36 = (bf16[256,512]{1,0:T(8,128)(2,1)}, bf16[256,512]{1,0:T(8,128)(2,1)}, u32[]{:S(2)}, u32[]{:S(2)}) collective-permute-start(bf16[256,512]{1,0:T(8,128)(2,1)} %get-tuple-element.258.refs_4_), channel_id=1, source_target_pairs={{0,2},{2,0},{1,3},{3,1},{4,6},{6,4},{5,7},{7,5},{8,10},{10,8},{9,1... | collective-permute-start | bytes 786440 | tf_op jit(solution)/shard_map/ppermute | solution.py:584
  362.4 25.1 %collective-permute-start.45 = (bf16[512,512]{1,0:T(8,128)(2,1)}, bf16[512,512]{1,0:T(8,128)(2,1)S(1)}, u32[]{:S(2)}, u32[]{:S(2)}) collective-permute-start(bf16[512,512]{1,0:T(8,128)(2,1)} %get-tuple-element.230.refs_2_), channel_id=1, source_target_pairs={{0,2},{2,0},{1,3},{3,1},{4,6},{6,4},{5,7},{7,5},{8,10},{10,8},{9,1... | collective-permute-start | bytes 1572872 | tf_op jit(solution)/shard_map/ppermute | solution.py:587
  364.8 27.1 %collective-permute-start.46 = (bf16[512,512]{1,0:T(8,128)(2,1)}, bf16[512,512]{1,0:T(8,128)(2,1)}, u32[]{:S(2)}, u32[]{:S(2)}) collective-permute-start(bf16[512,512]{1,0:T(8,128)(2,1)} %get-tuple-element.231.refs_4_), channel_id=1, source_target_pairs={{0,4},{4,0},{1,5},{5,1},{2,6},{6,2},{3,7},{7,3},{8,12},{12,8},{9,1... | collective-permute-start | bytes 1572872 | tf_op jit(solution)/shard_map/ppermute | solution.py:587
  366.4 19.0 %collective-permute-start.53 = (bf16[256,512]{1,0:T(8,128)(2,1)}, bf16[256,512]{1,0:T(8,128)(2,1)S(1)}, u32[]{:S(2)}, u32[]{:S(2)}) collective-permute-start(bf16[256,512]{1,0:T(8,128)(2,1)} %get-tuple-element.241.refs_2_), channel_id=1, source_target_pairs={{0,4},{4,0},{1,5},{5,1},{2,6},{6,2},{3,7},{7,3},{8,12},{12,8},{9,1... | collective-permute-start | bytes 786440 | tf_op jit(solution)/shard_map/ppermute | solution.py:584
  369.2 18.0 %collective-permute-start.54 = (bf16[256,512]{1,0:T(8,128)(2,1)}, bf16[256,512]{1,0:T(8,128)(2,1)S(1)}, u32[]{:S(2)}, u32[]{:S(2)}) collective-permute-start(bf16[256,512]{1,0:T(8,128)(2,1)} %get-tuple-element.242.refs_4_), channel_id=1, source_target_pairs={{0,2},{2,0},{1,3},{3,1},{4,6},{6,4},{5,7},{7,5},{8,10},{10,8},{9,1... | collective-permute-start | bytes 786440 | tf_op jit(solution)/shard_map/ppermute | solution.py:584
  372.9 27.1 %collective-permute-start.57 = (bf16[256,1024]{1,0:T(8,128)(2,1)}, bf16[256,1024]{1,0:T(8,128)(2,1)}, u32[]{:S(2)}, u32[]{:S(2)}) collective-permute-start(bf16[256,1024]{1,0:T(8,128)(2,1)} %get-tuple-element.255.refs_14_.refs_2_), channel_id=1, source_target_pairs={{0,4},{4,0},{1,5},{5,1},{2,6},{6,2},{3,7},{7,3},{8,12},{12,8},{9,1... | collective-permute-start | bytes 1572872 | tf_op jit(solution)/shard_map/ppermute | solution.py:584
  385.4 16.3 %collective-permute-start.58 = (bf16[512,512]{1,0:T(8,128)(2,1)}, bf16[512,512]{1,0:T(8,128)(2,1)}, u32[]{:S(2)}, u32[]{:S(2)}) collective-permute-start(bf16[512,512]{1,0:T(8,128)(2,1)} %get-tuple-element.256.refs_15_.refs_4_), channel_id=1, source_target_pairs={{0,2},{2,0},{1,3},{3,1},{4,6},{6,4},{5,7},{7,5},{8,10},{10,8},{9,1... | collective-permute-start | bytes 1572872 | tf_op jit(solution)/shard_map/ppermute | solution.py:584
  387.2 24.7 %collective-permute-start.37 = (bf16[512,512]{1,0:T(8,128)(2,1)}, bf16[512,512]{1,0:T(8,128)(2,1)}, u32[]{:S(2)}, u32[]{:S(2)}) collective-permute-start(bf16[512,512]{1,0:T(8,128)(2,1)} %get-tuple-element.223.refs_2_), channel_id=1, source_target_pairs={{0,2},{2,0},{1,3},{3,1},{4,6},{6,4},{5,7},{7,5},{8,10},{10,8},{9,1... | collective-permute-start | bytes 1572872 | tf_op jit(solution)/shard_map/ppermute | solution.py:587
  387.5 26.1 %collective-permute-start.38 = (bf16[512,512]{1,0:T(8,128)(2,1)}, bf16[512,512]{1,0:T(8,128)(2,1)}, u32[]{:S(2)}, u32[]{:S(2)}) collective-permute-start(bf16[512,512]{1,0:T(8,128)(2,1)} %get-tuple-element.224.refs_4_), channel_id=1, source_target_pairs={{0,4},{4,0},{1,5},{5,1},{2,6},{6,2},{3,7},{7,3},{8,12},{12,8},{9,1... | collective-permute-start | bytes 1572872 | tf_op jit(solution)/shard_map/ppermute | solution.py:587
  391.8 27.4 %collective-permute-start.30 = (f32[5120]{0:T(1024)S(1)}, f32[5120]{0:T(1024)S(1)}, u32[]{:S(2)}, u32[]{:S(2)}) collective-permute-start(f32[5120]{0:T(1024)S(1)} %reshape.194), channel_id=1, source_target_pairs={{0,1},{1,0},{2,3},{3,2},{4,5},{5,4},{6,7},{7,6},{8,9},{9,8},{10,11... | collective-permute-start | bytes 61448 | tf_op jit(solution)/shard_map/ppermute | solution.py:655
  400.0 84.9 %collective-permute-start.55 = (bf16[512,512]{1,0:T(8,128)(2,1)}, bf16[512,512]{1,0:T(8,128)(2,1)}, u32[]{:S(2)}, u32[]{:S(2)}) collective-permute-start(bf16[512,512]{1,0:T(8,128)(2,1)} %get-tuple-element.243.refs_0_), channel_id=1, source_target_pairs={{0,2},{2,0},{1,3},{3,1},{4,6},{6,4},{5,7},{7,5},{8,10},{10,8},{9,1... | collective-permute-start | bytes 1572872 | tf_op jit(solution)/shard_map/ppermute | solution.py:587
  401.7 83.2 %collective-permute-start.56 = (bf16[512,512]{1,0:T(8,128)(2,1)}, bf16[512,512]{1,0:T(8,128)(2,1)}, u32[]{:S(2)}, u32[]{:S(2)}) collective-permute-start(bf16[512,512]{1,0:T(8,128)(2,1)} %get-tuple-element.244.refs_2_), channel_id=1, source_target_pairs={{0,4},{4,0},{1,5},{5,1},{2,6},{6,2},{3,7},{7,3},{8,12},{12,8},{9,1... | collective-permute-start | bytes 1572872 | tf_op jit(solution)/shard_map/ppermute | solution.py:587
  411.8 66.0 %collective-permute-start.59 = (bf16[512,1024]{1,0:T(8,128)(2,1)}, bf16[512,1024]{1,0:T(8,128)(2,1)}, u32[]{:S(2)}, u32[]{:S(2)}) collective-permute-start(bf16[512,1024]{1,0:T(8,128)(2,1)} %get-tuple-element.245.refs_0_), channel_id=1, source_target_pairs={{0,2},{2,0},{1,3},{3,1},{4,6},{6,4},{5,7},{7,5},{8,10},{10,8},{9,1... | collective-permute-start | bytes 3145736 | tf_op jit(solution)/shard_map/ppermute | solution.py:587
  413.6 64.3 %collective-permute-start.60 = (bf16[1024,512]{1,0:T(8,128)(2,1)}, bf16[1024,512]{1,0:T(8,128)(2,1)}, u32[]{:S(2)}, u32[]{:S(2)}) collective-permute-start(bf16[1024,512]{1,0:T(8,128)(2,1)} %get-tuple-element.246.refs_2_), channel_id=1, source_target_pairs={{0,4},{4,0},{1,5},{5,1},{2,6},{6,2},{3,7},{7,3},{8,12},{12,8},{9,1... | collective-permute-start | bytes 3145736 | tf_op jit(solution)/shard_map/ppermute | solution.py:587
  419.2 23.5 %collective-permute-start.31 = (f32[8704]{0:T(1024)S(1)}, f32[8704]{0:T(1024)S(1)}, u32[]{:S(2)}, u32[]{:S(2)}) collective-permute-start(f32[8704]{0:T(1024)S(1)} %pad_maximum_fusion), channel_id=1, source_target_pairs={{0,2},{2,0},{4,6},{6,4},{8,10},{10,8},{12,14},{14,12},{16,18},{18,... | collective-permute-start | bytes 104456 | tf_op jit(solution)/shard_map/ppermute | solution.py:655
  442.8 11.9 %collective-permute-start.32 = (f32[8704]{0:T(1024)S(1)}, f32[8704]{0:T(1024)S(1)}, u32[]{:S(2)}, u32[]{:S(2)}) collective-permute-start(f32[8704]{0:T(1024)S(1)} %fusion.20), channel_id=1, source_target_pairs={{0,4},{2,6},{4,0},{6,2},{8,12},{10,14},{12,8},{14,10},{16,20},{18,... | collective-permute-start | bytes 104456 | tf_op jit(solution)/shard_map/ppermute | solution.py:655
  454.7 8.2 %collective-permute-start.33 = (f32[8704]{0:T(1024)S(1)}, f32[8704]{0:T(1024)S(1)}, u32[]{:S(2)}, u32[]{:S(2)}) collective-permute-start(f32[8704]{0:T(1024)S(1)} %add.254), channel_id=1, source_target_pairs={{0,8},{2,10},{4,12},{6,14},{8,0},{10,2},{12,4},{14,6},{16,24},{18,... | collective-permute-start | bytes 104456 | tf_op jit(solution)/shard_map/ppermute | solution.py:655
  462.9 13.1 %collective-permute-start.34 = (f32[8704]{0:T(1024)S(1)}, f32[8704]{0:T(1024)S(1)}, u32[]{:S(2)}, u32[]{:S(2)}) collective-permute-start(f32[8704]{0:T(1024)S(1)} %add.255), channel_id=1, source_target_pairs={{0,16},{2,18},{4,20},{6,22},{8,24},{10,26},{12,28},{14,30},{16,0},... | collective-permute-start | bytes 104456 | tf_op jit(solution)/shard_map/ppermute | solution.py:655
  (59 other events, 453.8 us)
Sparse Core Ops, SparseCore 0:
  202.3 80.3 all-reduce.2
